TPU v7x, 32 devices: a whole 2x2x4 slice. The times are simulated.
32 devices in a mesh: ctx: 8 (over y, x, core), head: 4 (over z).
Axes of the slice: x: 2, y: 2, z: 4, core: 2. Of those that a mesh axis runs over, the one named last changes fastest.
Arguments:
- queries: bfloat16 [2048, 4096], P(('ctx', 'head')), may hold values from -4.6 to 4.6
- fresh_keys: bfloat16 [2048, 1024], P(('ctx', 'head')), may hold values from -4.6 to 4.6
- fresh_values: bfloat16 [2048, 1024], P(('ctx', 'head')), may hold values from -6 to 6
- cache_keys: bfloat16 [2048, 1024], P('ctx', 'head'), may hold values from -6 to 6
- cache_values: bfloat16 [2048, 1024], P('ctx', 'head'), may hold values from -6 to 6
- page_request: int32 [128], P('ctx'), may hold values from 0 to 2
- prompt_lengths: int32 [2], replicated, may hold values from 1 to 1792, 2048 in all
- output_weight: bfloat16 [4096, 4096], P('head'), may hold values from -0.375 to 0.375
Outputs:
- mixed: bfloat16 [2048, 4096], P(('ctx', 'head'))
Inputs may be any that keep to these rules, and one draw needn't show every extreme that they name: `page_request`: value 2 marks a free page that no prompt reads.
All inputs are finite; a program needn't handle non-finite values.
Results may differ from a plain program's by a relative error of at most 0.015.
Values may be sent and summed in bfloat16 or wider, within the bound.
No kernel may reach another device: no remote copies, remote signals or barrier semaphores. Data moves between devices by JAX's collectives and lax.ppermute only.
A program may use at most 64 MiB of HBM per device.

v0:
```python
import math

import jax
import jax.numpy as jnp
from jax import lax
from jax.sharding import PartitionSpec as P

HD = 128
PAGE = 16


def attend_piece(carried, key_piece, query_group, row_req, row_pos, head_dim):
    key_part, value_part, key_req, key_pos = key_piece
    key_count = key_part.shape[0]
    block_rows = math.gcd(key_count, 1024)
    kv_groups = query_group.shape[0]
    key_three = key_part.reshape(key_count, kv_groups, head_dim)
    value_three = value_part.reshape(key_count, kv_groups, head_dim)
    score_scale = 1.0 / math.sqrt(head_dim)

    def one_block(block_id, running_state):
        running, totals, accumulated = running_state
        offset = block_id * block_rows
        key_block = lax.dynamic_slice_in_dim(key_three, offset, block_rows, 0)
        value_block = lax.dynamic_slice_in_dim(value_three, offset, block_rows, 0)
        req_block = lax.dynamic_slice_in_dim(key_req, offset, block_rows, 0)
        pos_block = lax.dynamic_slice_in_dim(key_pos, offset, block_rows, 0)
        scores = (
            jnp.einsum("gqd,kgd->gqk", query_group, key_block, preferred_element_type=jnp.float32)
            * score_scale
        )
        visible = (row_req[:, None] == req_block[None, :]) & (
            pos_block[None, :] <= row_pos[:, None]
        )
        masked = jnp.where(visible[None], scores, -1e30)
        newmax = jnp.maximum(running, jnp.max(masked, axis=-1))
        weights = jnp.where(visible[None], jnp.exp(masked - newmax[..., None]), 0.0)
        factor = jnp.exp(running - newmax)
        totals = totals * factor + jnp.sum(weights, axis=-1)
        summed = jnp.einsum(
            "gqk,kgd->gqd",
            weights.astype(jnp.bfloat16),
            value_block,
            preferred_element_type=jnp.float32,
        )
        accumulated = accumulated * factor[..., None] + summed
        return (newmax, totals, accumulated)

    return lax.fori_loop(0, key_count // block_rows, one_block, carried)


def shards(
    queries,
    fresh_keys,
    fresh_values,
    cache_keys,
    cache_values,
    page_request,
    prompt_lengths,
    output_weight,
):
    ctx_count = lax.axis_size("ctx")
    local_query, local_key, local_value = (
        lax.all_to_all(queries, "head", split_axis=1, concat_axis=0, tiled=True),
        lax.all_to_all(fresh_keys, "head", split_axis=1, concat_axis=0, tiled=True),
        lax.all_to_all(fresh_values, "head", split_axis=1, concat_axis=0, tiled=True),
    )
    block_len = local_query.shape[0]
    half_len = block_len // 2
    rank_id = lax.axis_index("ctx")
    offsets = jnp.arange(block_len, dtype=jnp.int32)
    pieces = jnp.where(offsets < half_len, rank_id, 2 * ctx_count - 1 - rank_id)
    position = pieces * half_len + offsets % half_len
    ends = jnp.cumsum(prompt_lengths)
    request = jnp.sum((position[:, None] >= ends[None, :]).astype(jnp.int32), axis=1)
    head_dim = HD
    kv_groups = local_key.shape[1] // head_dim
    repeat_heads = local_query.shape[1] // local_key.shape[1]
    rows_all = block_len * repeat_heads
    query_group = local_query.reshape(block_len, kv_groups, repeat_heads, head_dim)
    query_group = jnp.transpose(query_group, (1, 0, 2, 3)).reshape(kv_groups, rows_all, head_dim)
    row_req = jnp.repeat(request, repeat_heads)
    row_pos = jnp.repeat(position, repeat_heads)
    cache_req = jnp.repeat(page_request, PAGE)
    start_state = (
        jnp.full((kv_groups, rows_all), -1e30, jnp.float32),
        jnp.zeros((kv_groups, rows_all), jnp.float32),
        jnp.zeros((kv_groups, rows_all, head_dim), jnp.float32),
    )
    state_now = attend_piece(
        start_state,
        (
            lax.all_gather(local_key, "ctx", axis=0, tiled=True),
            lax.all_gather(local_value, "ctx", axis=0, tiled=True),
            lax.all_gather(request, "ctx", axis=0, tiled=True),
            lax.all_gather(position, "ctx", axis=0, tiled=True),
        ),
        query_group,
        row_req,
        row_pos,
        head_dim,
    )
    key_part = lax.all_gather(cache_keys, "ctx", axis=0, tiled=True)
    value_part = lax.all_gather(cache_values, "ctx", axis=0, tiled=True)
    key_req = lax.all_gather(cache_req, "ctx", axis=0, tiled=True)
    key_pos = jnp.full((key_part.shape[0],), -1, jnp.int32)
    state_now = attend_piece(
        state_now, (key_part, value_part, key_req, key_pos), query_group, row_req, row_pos, head_dim
    )
    running, totals, accumulated = state_now
    attended = (accumulated / totals[..., None]).reshape(
        kv_groups, block_len, repeat_heads, head_dim
    )
    attended = (
        jnp.transpose(attended, (1, 0, 2, 3))
        .reshape(block_len, kv_groups * repeat_heads * head_dim)
        .astype(jnp.bfloat16)
    )
    return lax.psum_scatter(
        jnp.dot(attended, output_weight, preferred_element_type=jnp.float32).astype(jnp.bfloat16),
        "head",
        scatter_dimension=0,
        tiled=True,
    )


def solution(mesh):
    placed = (
        P(("ctx", "head"), None),
        P(("ctx", "head"), None),
        P(("ctx", "head"), None),
        P("ctx", "head"),
        P("ctx", "head"),
        P("ctx"),
        P(),
        P("head", None),
    )
    return jax.shard_map(
        shards, mesh=mesh, in_specs=placed, out_specs=P(("ctx", "head"), None), check_vma=False
    )
```

profile of v0, /device:TPU:0, one launch (start us, length us, event | category | flops | bytes accessed | tf_op | source)
XLA Modules:
  0.0 198.2 jit_solution(17167322485427617610)
XLA Ops:
  6.5 0.9 copy.80
  7.5 12.3 %all_to_all.54 = bf16[64,4,256]{2,0,1:T(8,128)(2,1)} all-to-all(bf16[64,4,256]{2,0,1:T(8,128)(2,1)S(1)} %bitcast.92), channel_id=1, replica_groups=mesh['ctx'=8,'head'=4] {'head'}, dimensions={1} | all-to-all | bytes 262144 | tf_op jit(solution)/shard_map/all_to_all | solution.py:66
  19.8 0.0 all-gather.8.cloned.1.call-start
  19.8 0.9 copy.81
  20.7 9.0 %all_to_all.55 = bf16[64,4,256]{2,0,1:T(8,128)(2,1)} all-to-all(bf16[64,4,256]{2,0,1:T(8,128)(2,1)S(1)} %bitcast.93), channel_id=1, replica_groups=mesh['ctx'=8,'head'=4] {'head'}, dimensions={1} | all-to-all | bytes 262144 | tf_op jit(solution)/shard_map/all_to_all | solution.py:65
  29.7 0.0 all-gather.12.cloned.1.call-start
  29.8 1.7 copy.62
  31.5 1.9 copy.79
  33.4 3.5 %all-to-all-start.1 = ((bf16[64,4,1024]{2,0,1:T(8,128)(2,1)}), bf16[64,4,1024]{2,0,1:T(8,128)(2,1)S(1)}, u32[]{:S(2)}, u32[]{:S(2)}) async-start(bf16[64,4,1024]{2,0,1:T(8,128)(2,1)} %bitcast.63), calls=%async_computation.1 | async-start | bytes 1048576 | tf_op jit(solution)/shard_map/all_to_all | solution.py:64
  36.9 0.0 all-gather.14.cloned.1.call-start
  36.9 1.7 copy.63
  38.6 0.0 reduce-scatter.2.cloned.1.call-start
  38.7 0.8 reduce-window.8
  39.5 0.7 broadcast_in_dim.133
  40.2 0.1 reshape.201
  40.3 0.1 fusion.44
  40.4 8.9 %all-gather = s32[8,1,256]{2,1,0:T(1,128)S(1)} all-gather(s32[1,1,256]{2,1,0:T(1,128)S(1)} %bitcast.94), channel_id=1, replica_groups=mesh['ctx'=8,'head'=4] {'ctx'}, dimensions={0}, use_global_device_ids=true | all-gather | bytes 9216 | tf_op jit(solution)/shard_map/all_gather | solution.py:95
  49.3 8.8 %all-gather.1 = s32[8,1,256]{2,1,0:T(1,128)S(1)} all-gather(s32[1,1,256]{2,1,0:T(1,128)S(1)} %bitcast.100), channel_id=1, replica_groups=mesh['ctx'=8,'head'=4] {'ctx'}, dimensions={0}, use_global_device_ids=true | all-gather | bytes 9216 | tf_op jit(solution)/shard_map/all_gather | solution.py:96
  58.1 7.9 %all-gather.2 = s32[8,1,256]{2,1,0:T(1,128)S(1)} all-gather(s32[1,1,256]{2,1,0:T(1,128)S(1)} %reshape.201), channel_id=1, replica_groups=mesh['ctx'=8,'head'=4] {'ctx'}, dimensions={0}, use_global_device_ids=true | all-gather | bytes 9216 | tf_op jit(solution)/shard_map/all_gather | solution.py:105
  66.0 0.4 reshape.191
  66.4 1.0 copy.57
  67.4 1.5 copy.59
  68.9 2.3 %copy.55 = bf16[2048,256]{0,1:T(8,128)(2,1)} copy(bf16[2048,256]{1,0:T(8,128)(2,1)} %all-gather.8.cloned.1.call-done) | data formatting | bytes 2097152 | tf_op jit(solution)/shard_map/all_gather | solution.py:93
  71.2 35.0 %while.37 = (s32[]{:T(128)}, f32[2,1024]{1,0:T(2,128)S(1)}, f32[2,1024]{1,0:T(2,128)S(1)}, f32[2,1024,128]{2,1,0:T(8,128)S(1)}, s32[2048]{0:T(1024)S(1)}, /*inde...) while((s32[]{:T(128)}, f32[2,1024]{1,0:T(2,128)S(1)}, ...), condition=%wide.region_5.6_spmd.clone, body=%wide.region_2.5_spmd.clone.sunk | while | flops 1104947200 | bytes 66775280 | solution.py:49
  71.2 0.1 broadcast_in_dim.233
  71.3 0.1 eq.101
  71.4 0.1 broadcast_in_dim.232
  71.5 0.1 le.85
  71.6 1.2 compare_and_fusion.5
  72.8 6.3 %fusion.74 = (f32[2,1024]{1,0:T(2,128)S(1)}, f32[2,1024,1024]{2,1,0:T(8,128)}) fusion(pred[1024,1024]{0,1:T(8,128)(4,1)S(1)} %compare_and_fusion.5, bf16[2,1024,128]{2,1,0:T(8,128)(2,1)} %get-tuple-element.748, bf16[2048,2,128]{0,2,1:T(8,128)(2,1)} %get-tuple-element.747, s32[]{:T(128)S(6)} %select_n.146), kind=kOutput, calls=%fused_computation.26.clone.1 | convolution fusion | flops 543160320 | bytes 10493956 | tf_op jit(solution)/shard_map/while/body/eval_jaxpr/gqd,kgd->gqk/dot_general | solution.py:29
  79.1 4.7 %fusion.76 = f32[2,1024]{1,0:T(2,128)S(1)} fusion(f32[2,1024,1024]{2,1,0:T(8,128)} %get-tuple-element.708, f32[2,1024]{1,0:T(2,128)S(1)} %fusion.75, pred[1024,1024]{0,1:T(8,128)(4,1)S(1)} %compare_and_fusion.5), kind=kLoop, calls=%fused_computation.28.clone.1 | loop fusion | flops 10483712 | bytes 9453568 | tf_op jit(solution)/shard_map/while/body/eval_jaxpr/reduce_sum | solution.py:39
  83.9 1.1 copy-done
  84.9 3.7 %fusion.78 = f32[2,1024,128]{2,1,0:T(8,128)S(1)} fusion(f32[2,1024,1024]{2,1,0:T(8,128)S(1)} %copy-done, f32[2,1024]{1,0:T(2,128)S(1)} %fusion.75, pred[1024,1024]{0,1:T(8,128)(4,1)S(1)} %compare_and_fusion.5, f32[2,1024,128]{2,1,0:T(8,128)S(1)} %get-tuple-element.729, bf16[2048,2,128]{0,2,1:T(8,128)(2,1)S(1)} %get-tuple-element.749, ...), kind=kOutput, calls=%fused_computation.32.clone.1 | convolution fusion | flops 548143104 | bytes 12075013 | tf_op jit(solution)/shard_map/while/body/eval_jaxpr/gqk,kgd->gqd/dot_general | solution.py:40
  88.7 0.1 broadcast_in_dim.233
  88.8 0.1 eq.101
  88.9 0.1 broadcast_in_dim.232
  89.0 0.1 le.85
  89.1 1.2 compare_and_fusion.5
  90.3 6.3 %fusion.74 = (f32[2,1024]{1,0:T(2,128)S(1)}, f32[2,1024,1024]{2,1,0:T(8,128)}) fusion(pred[1024,1024]{0,1:T(8,128)(4,1)S(1)} %compare_and_fusion.5, bf16[2,1024,128]{2,1,0:T(8,128)(2,1)} %get-tuple-element.748, bf16[2048,2,128]{0,2,1:T(8,128)(2,1)} %get-tuple-element.747, s32[]{:T(128)S(6)} %select_n.146), kind=kOutput, calls=%fused_computation.26.clone.1 | convolution fusion | flops 543160320 | bytes 10493956 | tf_op jit(solution)/shard_map/while/body/eval_jaxpr/gqd,kgd->gqk/dot_general | solution.py:29
  96.6 4.7 %fusion.76 = f32[2,1024]{1,0:T(2,128)S(1)} fusion(f32[2,1024,1024]{2,1,0:T(8,128)} %get-tuple-element.708, f32[2,1024]{1,0:T(2,128)S(1)} %fusion.75, pred[1024,1024]{0,1:T(8,128)(4,1)S(1)} %compare_and_fusion.5), kind=kLoop, calls=%fused_computation.28.clone.1 | loop fusion | flops 10483712 | bytes 9453568 | tf_op jit(solution)/shard_map/while/body/eval_jaxpr/reduce_sum | solution.py:39
  101.4 1.1 copy-done
  102.5 3.7 %fusion.78 = f32[2,1024,128]{2,1,0:T(8,128)S(1)} fusion(f32[2,1024,1024]{2,1,0:T(8,128)S(1)} %copy-done, f32[2,1024]{1,0:T(2,128)S(1)} %fusion.75, pred[1024,1024]{0,1:T(8,128)(4,1)S(1)} %compare_and_fusion.5, f32[2,1024,128]{2,1,0:T(8,128)S(1)} %get-tuple-element.729, bf16[2048,2,128]{0,2,1:T(8,128)(2,1)S(1)} %get-tuple-element.749, ...), kind=kOutput, calls=%fused_computation.32.clone.1 | convolution fusion | flops 548143104 | bytes 12075013 | tf_op jit(solution)/shard_map/while/body/eval_jaxpr/gqk,kgd->gqd/dot_general | solution.py:40
  106.3 12.5 %all-gather.14.cloned.1.call-done = bf16[2048,256]{0,1:T(8,128)(2,1)} async-done(((bf16[256,256]{0,1:T(8,128)(2,1)}), bf16[2048,256]{0,1:T(8,128)(2,1)}) %all-gather.14.cloned.1.call-update) | async-done | bytes 1048592 | tf_op jit(solution)/shard_map/all_gather | solution.py:104
  118.8 21.1 %while.36 = (s32[]{:T(128)}, f32[2,1024]{1,0:T(2,128)S(1)}, f32[2,1024]{1,0:T(2,128)S(1)}, f32[2,1024,128]{2,1,0:T(8,128)S(1)}, s32[2048]{0:T(1024)S(1)}, /*inde...) while((s32[]{:T(128)}, f32[2,1024]{1,0:T(2,128)S(1)}, ...), condition=%wide.region_9.10_spmd.clone, body=%wide.region_6.9_spmd.clone.sunk | while | flops 1103630592 | bytes 37391064 | solution.py:49
  118.8 0.1 broadcast_in_dim.223
  118.9 0.1 eq.97
  119.0 0.1 broadcast.215
  119.1 0.1 le.81
  119.3 0.7 compare_and_fusion.4
  120.0 3.2 %fusion.68 = (f32[2,1024]{1,0:T(2,128)S(1)}, f32[2,1024,1024]{2,1,0:T(8,128)S(1)}) fusion(pred[1024,1024]{0,1:T(8,128)(4,1)S(1)} %compare_and_fusion.4, bf16[2,1024,128]{2,1,0:T(8,128)(2,1)} %get-tuple-element.790, bf16[2048,2,128]{0,2,1:T(8,128)(2,1)} %get-tuple-element.789, s32[]{:T(128)S(6)} %select_n.140), kind=kOutput, calls=%fused_computation.6.clone.1 | convolution fusion | flops 543160320 | bytes 10493956 | tf_op jit(solution)/shard_map/while/body/eval_jaxpr/gqd,kgd->gqk/dot_general | solution.py:29
  123.3 2.3 %fusion.69 = f32[2,1024]{1,0:T(2,128)S(1)} fusion(f32[2,1024,1024]{2,1,0:T(8,128)S(1)} %get-tuple-element.693, f32[2,1024]{1,0:T(2,128)S(1)} %max.19, pred[1024,1024]{0,1:T(8,128)(4,1)S(1)} %compare_and_fusion.4), kind=kLoop, calls=%fused_computation.8.clone.1 | loop fusion | flops 10483712 | bytes 9453568 | tf_op jit(solution)/shard_map/while/body/eval_jaxpr/reduce_sum | solution.py:39
  125.6 3.7 %fusion.70 = f32[2,1024,128]{2,1,0:T(8,128)S(1)} fusion(f32[2,1024,1024]{2,1,0:T(8,128)S(1)} %get-tuple-element.693, f32[2,1024]{1,0:T(2,128)S(1)} %max.19, pred[1024,1024]{0,1:T(8,128)(4,1)S(1)} %compare_and_fusion.4, f32[2,1024,128]{2,1,0:T(8,128)S(1)} %get-tuple-element.773, bf16[2048,2,128]{0,2,1:T(8,128)(2,1)S(1)} %copy-done.1, ...), kind=kOutput, calls=%fused_computation.12.clone.1 | convolution fusion | flops 547880960 | bytes 12075012 | tf_op jit(solution)/shard_map/while/body/eval_jaxpr/gqk,kgd->gqd/dot_general | solution.py:40
  129.4 0.1 broadcast_in_dim.223
  129.5 0.1 eq.97
  129.6 0.1 broadcast.215
  129.7 0.1 le.81
  129.8 0.7 compare_and_fusion.4
  130.6 3.2 %fusion.68 = (f32[2,1024]{1,0:T(2,128)S(1)}, f32[2,1024,1024]{2,1,0:T(8,128)S(1)}) fusion(pred[1024,1024]{0,1:T(8,128)(4,1)S(1)} %compare_and_fusion.4, bf16[2,1024,128]{2,1,0:T(8,128)(2,1)} %get-tuple-element.790, bf16[2048,2,128]{0,2,1:T(8,128)(2,1)} %get-tuple-element.789, s32[]{:T(128)S(6)} %select_n.140), kind=kOutput, calls=%fused_computation.6.clone.1 | convolution fusion | flops 543160320 | bytes 10493956 | tf_op jit(solution)/shard_map/while/body/eval_jaxpr/gqd,kgd->gqk/dot_general | solution.py:29
  133.9 2.3 %fusion.69 = f32[2,1024]{1,0:T(2,128)S(1)} fusion(f32[2,1024,1024]{2,1,0:T(8,128)S(1)} %get-tuple-element.693, f32[2,1024]{1,0:T(2,128)S(1)} %max.19, pred[1024,1024]{0,1:T(8,128)(4,1)S(1)} %compare_and_fusion.4), kind=kLoop, calls=%fused_computation.8.clone.1 | loop fusion | flops 10483712 | bytes 9453568 | tf_op jit(solution)/shard_map/while/body/eval_jaxpr/reduce_sum | solution.py:39
  136.2 3.7 %fusion.70 = f32[2,1024,128]{2,1,0:T(8,128)S(1)} fusion(f32[2,1024,1024]{2,1,0:T(8,128)S(1)} %get-tuple-element.693, f32[2,1024]{1,0:T(2,128)S(1)} %max.19, pred[1024,1024]{0,1:T(8,128)(4,1)S(1)} %compare_and_fusion.4, f32[2,1024,128]{2,1,0:T(8,128)S(1)} %get-tuple-element.773, bf16[2048,2,128]{0,2,1:T(8,128)(2,1)S(1)} %copy-done.1, ...), kind=kOutput, calls=%fused_computation.12.clone.1 | convolution fusion | flops 547880960 | bytes 12075012 | tf_op jit(solution)/shard_map/while/body/eval_jaxpr/gqk,kgd->gqd/dot_general | solution.py:40
  139.9 0.3 divide_convert_fusion
  140.3 0.3 copy.66
  140.5 7.1 %convolution_convert_fusion = bf16[256,4096]{1,0:T(8,128)(2,1)} fusion(bf16[256,1024]{0,1:T(8,128)(2,1)S(1)} %bitcast.82, bf16[1024,4096]{1,0:T(8,128)(2,1)} %param.19), kind=kOutput, calls=%fused_computation.47 | convolution fusion | flops 2148532224 | bytes 11010048 | tf_op jit(solution)/shard_map/dot_general | solution.py:120
  147.7 44.0 %reduce-scatter.2.cloned.1.call-done = bf16[64,4096]{1,0:T(8,128)(2,1)} async-done(((bf16[256,4096]{1,0:T(8,128)(2,1)}), bf16[64,4096]{1,0:T(8,128)(2,1)}) %reduce-scatter.2.cloned.1.call-update) | async-done | bytes 524304 | tf_op jit(solution)/shard_map/reduce_scatter | solution.py:119
  (40 shorter events, 0.3 us)
Async XLA Ops:
  6.5 60.8 %all-gather.10.cloned.1.call-start = ((), (), s32[]{:S(2)}) async-start(), calls=%async_computation.5 | async-start | bytes 1179648 | tf_op jit(solution)/shard_map/all_gather | solution.py:94
  19.8 49.1 %all-gather.8.cloned.1.call-start = ((), (), s32[]{:S(2)}) async-start(), calls=%async_computation.4 | async-start | bytes 1179648 | tf_op jit(solution)/shard_map/all_gather | solution.py:93
  29.7 76.5 %all-gather.12.cloned.1.call-start = ((), (), s32[]{:S(2)}) async-start(), calls=%async_computation.6 | async-start | bytes 1179648 | tf_op jit(solution)/shard_map/all_gather | solution.py:103
  33.4 32.7 %all-to-all-start.1 = ((bf16[64,4,1024]{2,0,1:T(8,128)(2,1)}), bf16[64,4,1024]{2,0,1:T(8,128)(2,1)S(1)}, u32[]{:S(2)}, u32[]{:S(2)}) async-start(bf16[64,4,1024]{2,0,1:T(8,128)(2,1)} %bitcast.63), calls=%async_computation.1 | async-start | bytes 1048576 | tf_op jit(solution)/shard_map/all_to_all | solution.py:64
  36.9 81.9 %all-gather.14.cloned.1.call-start = ((), (), s32[]{:S(2)}) async-start(), calls=%async_computation.7 | async-start | bytes 1179648 | tf_op jit(solution)/shard_map/all_gather | solution.py:104
  38.6 153.1 %reduce-scatter.2.cloned.1.call-start = ((), (), s32[]{:S(2)}) async-start(), calls=%async_computation.8 | async-start | bytes 2621440 | tf_op jit(solution)/shard_map/reduce_scatter | solution.py:119
  79.1 5.8 %copy-start = (f32[2,1024,1024]{2,1,0:T(8,128)S(1)}, f32[2,1024,1024]{2,1,0:T(8,128)}, u32[]{:S(2)}) copy-start(f32[2,1024,1024]{2,1,0:T(8,128)} %get-tuple-element.708) | copy-start | bytes 25165828 | tf_op jit(solution)/shard_map/while
  96.6 5.9 %copy-start = (f32[2,1024,1024]{2,1,0:T(8,128)S(1)}, f32[2,1024,1024]{2,1,0:T(8,128)}, u32[]{:S(2)}) copy-start(f32[2,1024,1024]{2,1,0:T(8,128)} %get-tuple-element.708) | copy-start | bytes 25165828 | tf_op jit(solution)/shard_map/while
  120.0 5.6 %copy-start.1 = (bf16[2048,2,128]{0,2,1:T(8,128)(2,1)S(1)}, bf16[2048,2,128]{0,2,1:T(8,128)(2,1)}, u32[]{:S(2)}) copy-start(bf16[2048,2,128]{0,2,1:T(8,128)(2,1)} %get-tuple-element.791) | copy-start | bytes 3145732 | tf_op jit(solution)/shard_map/while
  130.6 5.6 %copy-start.1 = (bf16[2048,2,128]{0,2,1:T(8,128)(2,1)S(1)}, bf16[2048,2,128]{0,2,1:T(8,128)(2,1)}, u32[]{:S(2)}) copy-start(bf16[2048,2,128]{0,2,1:T(8,128)(2,1)} %get-tuple-element.791) | copy-start | bytes 3145732 | tf_op jit(solution)/shard_map/while
Sparse Core Ops, SparseCore 0:
  19.9 22.5 all-gather.9
  44.4 23.5 all-gather.7
  69.8 23.5 all-gather.11
  95.2 23.5 all-gather.13
  147.8 43.8 reduce-scatter.1
where the time goes:
time: 199 us; the launch traced here: 198 us
  waiting for transfers between devices  56.7 us (28%)
  blocking collectives  46.9 us (24%)
  matrix products  41 us (21%)
  other arithmetic  19.3 us (10%)
  local copies, waits for them, and re-layouts  17.1 us (9%)
  between operations  13.3 us (7%)
  starting transfers between devices  3.66 us (2%)
    reduce_scatter x1, waiting for transfers between devices, shards(): lax.psum_scatter(jnp.dot(attended, output_weight, preferred_element_type=...  44 us
    dot_general x4, matrix products, one_block(): jnp.einsum('gqd,kgd->gqk', query_group, key_block, preferred_element_type...  19 us
    dot_general x4, matrix products, one_block(): jnp.einsum('gqk,kgd->gqd', weights.astype(jnp.bfloat16), value_block, pre...  14.8 us
    reduce_sum x4, other arithmetic, one_block(): totals = totals * factor + jnp.sum(weights, axis=-1)  14 us
    all_gather x1, waiting for transfers between devices, shards(): value_part = lax.all_gather(cache_values, 'ctx', axis=0, tiled=True)  12.5 us
    all_to_all x1, blocking collectives, shards(): lax.all_to_all(fresh_values, 'head', split_axis=1, concat_axis=0, tiled=T...  12.3 us
    all_to_all x1, blocking collectives, shards(): lax.all_to_all(fresh_keys, 'head', split_axis=1, concat_axis=0, tiled=True)  8.97 us
    all_gather x1, blocking collectives, shards(): lax.all_gather(request, 'ctx', axis=0, tiled=True)  8.87 us
  transfers between devices with their start and end apart: 6, of which 2 were waited for; matrix products, arithmetic and copies ran while one was open for 23% of the time, Pallas kernels for 0%

commit v1 on v0

v1 whole, which is shorter than its diff:
```python
import functools
import math

import jax
import jax.numpy as jnp
from jax import lax
from jax.experimental import pallas as pl
from jax.experimental.pallas import tpu as pltpu
from jax.sharding import PartitionSpec as P

HD = 128
PAGE = 16
LANES = 128
HIDDEN = -1e30
BF16 = jnp.bfloat16
F32 = jnp.float32


def iota(shape, dim):
    return lax.broadcasted_iota(jnp.int32, shape, dim)


def pack_fresh_kernel(info, k_ref, v_ref, *outs):
    width = k_ref.shape[1] // len(outs)
    for x, out in enumerate(outs):
        columns = pl.ds(pl.multiple_of((info[1] ^ x) * width, width), width)
        out[:, :width] = k_ref[:, columns]
        out[:, width:] = v_ref[:, columns]


def pack_query_kernel(info, q_ref, *outs):
    width = q_ref.shape[1] // len(outs)
    for x, out in enumerate(outs):
        out[...] = q_ref[:, pl.ds(pl.multiple_of((info[1] ^ x) * width, width), width)]


def pack_cache_kernel(pages, k_ref, v_ref, out):
    tokens, width = k_ref.shape
    count = tokens // PAGE
    out[:tokens, :width] = k_ref[...]
    out[:tokens, width:] = v_ref[...]
    page = iota((count, 2 * width), 0)
    owner = jnp.zeros((count, 2 * width), jnp.int32)
    for p in range(count):
        owner = jnp.where(page == p, pages[p], owner)
    out[tokens:, :] = owner.astype(F32).astype(BF16)


def whole(shape):
    return pl.BlockSpec(shape, memory_space=pltpu.VMEM)


def smem():
    return pl.BlockSpec(memory_space=pltpu.SMEM)


def anywhere():
    return pl.BlockSpec(memory_space=pl.ANY)


def request_of(position, ends, requests):
    request = jnp.zeros(position.shape, jnp.int32)
    for r in range(requests):
        request += (position >= ends(r)).astype(jnp.int32)
    return request


def chunk_kernel(x_chunk, n_ctx, n_head, requests, info, q_hbm, *refs):
    cache_hbm, fresh_hbm = refs[:n_ctx], refs[n_ctx:2 * n_ctx]
    w_hbm, out, q_vm, cache, fresh, w_vm, scores, mixed, sems = refs[2 * n_ctx:]
    rows, q_width = q_vm.shape
    tokens, kv_width = fresh.shape[1:]
    groups = kv_width // (2 * HD)
    repeat = q_width // (groups * HD)
    pages = tokens // PAGE
    half = n_head * rows // 2
    c, h = info[0], info[1]
    ends = lambda r: info[2 + r]

    copies = [pltpu.make_async_copy(q_hbm, q_vm, sems.at[0])]
    for b in range(n_ctx):
        copies.append(pltpu.make_async_copy(cache_hbm[b], cache.at[b], sems.at[1 + b]))
    for b in range(n_ctx):
        copies.append(pltpu.make_async_copy(fresh_hbm[b], fresh.at[b], sems.at[1 + n_ctx + b]))
    copies.append(pltpu.make_async_copy(w_hbm, w_vm, sems.at[1 + 2 * n_ctx]))
    for copy in copies:
        copy.start()

    def start_of(rank, head):
        first = head * rows < half
        return jnp.where(first, rank, 2 * n_ctx - 1 - rank) * half + lax.rem(head * rows, half)

    p0 = start_of(c, h ^ x_chunk)
    lane = iota((rows, LANES), 1)
    row = iota((rows, LANES), 0)
    row_lane = lane - (LANES - rows)
    q_mask = (lane == request_of(p0 + row, ends, requests)) | (row_lane == row)
    q_mask = jnp.where(q_mask, 1.0, 0.0).astype(BF16)
    q_mask = jnp.concatenate([q_mask] * repeat, axis=0)

    def fresh_mask(b):
        parts = []
        for x in range(n_head):
            position = start_of(c ^ b, h ^ x) + row
            other = (lane < requests) & (request_of(position, ends, requests) != lane)
            later = (row_lane >= 0) & (position > p0 + row_lane)
            parts.append(jnp.where(other | later, HIDDEN, 0.0))
        return jnp.concatenate(parts, axis=0).astype(BF16)

    def cache_mask(b):
        owner = cache[b, tokens:, :LANES].astype(F32)
        page_lane = iota((pages, LANES), 1)
        other = (page_lane < requests) & (owner != page_lane.astype(F32))
        bias = jnp.where(other, HIDDEN, 0.0)
        bias = jnp.broadcast_to(bias[:, None, :], (pages, PAGE, LANES))
        return bias.reshape(tokens, LANES).astype(BF16)

    copies[0].wait()
    q_rows = []
    for g in range(groups):
        heads = [q_vm[:, (g * repeat + j) * HD:(g * repeat + j + 1) * HD] for j in range(repeat)]
        q_rows.append(jnp.concatenate([jnp.concatenate(heads, axis=0), q_mask], axis=1))

    scale = math.log2(math.e) / math.sqrt(HD)
    blocks = 2 * n_ctx
    largest = [None] * groups
    for b in range(blocks):
        copies[1 + b].wait()
        source = cache.at[b] if b < n_ctx else fresh.at[b - n_ctx]
        mask = cache_mask(b) if b < n_ctx else fresh_mask(b - n_ctx)
        for g in range(groups):
            keys = jnp.concatenate([source[:tokens, g * HD:(g + 1) * HD], mask], axis=1)
            s = lax.dot_general(q_rows[g], keys, (((1,), (1,)), ((), ())), preferred_element_type=F32)
            scores[g, :, b * tokens:(b + 1) * tokens] = s
            top = s[:, :LANES]
            for t in range(1, tokens // LANES):
                top = jnp.maximum(top, s[:, t * LANES:(t + 1) * LANES])
            largest[g] = top if b == 0 else jnp.maximum(largest[g], top)

    ones = jnp.ones((tokens, HD), BF16)
    for g in range(groups):
        top = jnp.max(largest[g], axis=1, keepdims=True) * scale
        summed = jnp.zeros((repeat * rows, 2 * HD), F32)
        for b in range(blocks):
            source = cache.at[b] if b < n_ctx else fresh.at[b - n_ctx]
            s = scores[g, :, b * tokens:(b + 1) * tokens]
            weights = jnp.exp2(s * scale - top).astype(BF16)
            values = jnp.concatenate([source[:tokens, (groups + g) * HD:(groups + g + 1) * HD], ones], axis=1)
            summed += jnp.dot(weights, values, preferred_element_type=F32)
        attended = (summed[:, :HD] / summed[:, HD:]).astype(BF16)
        for j in range(repeat):
            mixed[:, (g * repeat + j) * HD:(g * repeat + j + 1) * HD] = attended[j * rows:(j + 1) * rows]

    copies[-1].wait()
    step = min(1024, out.shape[1])
    for n in range(out.shape[1] // step):
        out[:, n * step:(n + 1) * step] = jnp.dot(
            mixed[...], w_vm[:, n * step:(n + 1) * step], preferred_element_type=F32
        ).astype(BF16)


def chunk(x, info, q, cache, fresh, weight, n_head, requests):
    n_ctx = len(cache)
    rows, q_width = q.shape
    tokens, kv_width = fresh[0].shape
    groups = kv_width // (2 * HD)
    repeat = q_width // (groups * HD)
    keys = 2 * n_ctx * tokens
    columns = weight.shape[1]
    return pl.pallas_call(
        functools.partial(chunk_kernel, x, n_ctx, n_head, requests),
        out_shape=jax.ShapeDtypeStruct((rows, columns), BF16),
        in_specs=[smem()] + [anywhere()] * (2 + 2 * n_ctx),
        out_specs=pl.BlockSpec(memory_space=pltpu.VMEM),
        scratch_shapes=[
            pltpu.VMEM((rows, q_width), BF16),
            pltpu.VMEM((n_ctx, cache[0].shape[0], kv_width), BF16),
            pltpu.VMEM((n_ctx, tokens, kv_width), BF16),
            pltpu.VMEM(weight.shape, BF16),
            pltpu.VMEM((groups, repeat * rows, keys), F32),
            pltpu.VMEM((rows, q_width), BF16),
            pltpu.SemaphoreType.DMA((2 + 2 * n_ctx,)),
        ],
        compiler_params=pltpu.CompilerParams(vmem_limit_bytes=40 * 1024 * 1024),
        cost_estimate=pl.CostEstimate(
            flops=8 * rows * q_width * keys + 2 * rows * q_width * columns,
            bytes_accessed=2 * (weight.size + keys * kv_width),
            transcendentals=rows * (q_width // HD) * keys,
        ),
    )(info, q, *cache, *fresh, weight)


def swap(value, axis, mask):
    return lax.ppermute(value, axis, [(i, i ^ mask) for i in range(lax.axis_size(axis))])


def gather_ctx(block):
    n_ctx = lax.axis_size("ctx")
    blocks = [None] * n_ctx
    for m in range(0, n_ctx, 2):
        blocks[m] = swap(block, "ctx", m) if m else block
    for m in range(0, n_ctx, 2):
        blocks[m + 1] = swap(blocks[m], "ctx", 1)
    return blocks


def shards(queries, fresh_keys, fresh_values, cache_keys, cache_values, page_request, prompt_lengths, output_weight):
    n_ctx, n_head = lax.axis_size("ctx"), lax.axis_size("head")
    requests = prompt_lengths.shape[0]
    rows = queries.shape[0]
    info = jnp.concatenate([
        jnp.stack([lax.axis_index("ctx"), lax.axis_index("head")]).astype(jnp.int32),
        jnp.stack([sum(prompt_lengths[i] for i in range(r + 1)) for r in range(requests)]),
    ])

    kv_width = 2 * fresh_keys.shape[1] // n_head
    fresh = pl.pallas_call(
        pack_fresh_kernel,
        out_shape=[jax.ShapeDtypeStruct((rows, kv_width), BF16)] * n_head,
        in_specs=[smem(), whole(fresh_keys.shape), whole(fresh_values.shape)],
        out_specs=[whole((rows, kv_width))] * n_head,
    )(info, fresh_keys, fresh_values)
    tokens = cache_keys.shape[0]
    cache = pl.pallas_call(
        pack_cache_kernel,
        out_shape=jax.ShapeDtypeStruct((tokens + tokens // PAGE, kv_width), BF16),
        in_specs=[smem(), whole(cache_keys.shape), whole(cache_values.shape)],
        out_specs=whole((tokens + tokens // PAGE, kv_width)),
    )(page_request, cache_keys, cache_values)
    q_width = queries.shape[1] // n_head
    query = pl.pallas_call(
        pack_query_kernel,
        out_shape=[jax.ShapeDtypeStruct((rows, q_width), BF16)] * n_head,
        in_specs=[smem(), whole(queries.shape)],
        out_specs=[whole((rows, q_width))] * n_head,
    )(info, queries)

    fresh = [swap(fresh[x], "head", x) if x else fresh[x] for x in range(n_head)]
    cache = gather_ctx(cache)
    fresh = gather_ctx(jnp.concatenate(fresh, axis=0))
    query = [swap(query[x], "head", x) if x else query[x] for x in range(n_head)]

    part = lambda x: chunk(x, info, query[x], cache, fresh, output_weight, n_head, requests)
    total = None
    for x in [*range(n_head - 1, 0, -1), 0]:
        partial = part(x)
        got = (swap(partial, "head", x) if x else partial).astype(F32)
        total = got if total is None else total + got
    return total.astype(BF16)


def solution(mesh):
    placed = (
        P(("ctx", "head"), None),
        P(("ctx", "head"), None),
        P(("ctx", "head"), None),
        P("ctx", "head"),
        P("ctx", "head"),
        P("ctx"),
        P(),
        P("head", None),
    )
    return jax.shard_map(
        shards, mesh=mesh, in_specs=placed, out_specs=P(("ctx", "head"), None), check_vma=False
    )
```

time: 199 us -> 112 us (0.56)
  blocking collectives: 46.9 us -> 0 us
  Pallas kernels: 0 us -> 42.9 us
  matrix products: 41 us -> 0 us
  waiting for transfers between devices: 56.7 us -> 34.2 us
  starting transfers between devices: 3.66 us -> 23.8 us
  other arithmetic: 19.3 us -> 2.32 us
  between operations: 13.3 us -> 1.49 us
  local copies, waits for them, and re-layouts: 17.1 us -> 7.2 us
    reduce_scatter x1 -> x0, waiting for transfers between devices: 44 us -> none  [shards(): lax.psum_scatter(jnp.dot(attended, output_weight, preferred_element_type=...]
    pallas_call x0 -> x7, Pallas kernels: none -> 42.9 us  [the longest x4 37.6 us: chunk(): pl.pallas_call(functools.partial(chunk_kernel, x, n_ctx, n_head, requests...]
    dot_general x9 -> x0, matrix products: 41 us -> none  [the longest x4 19 us: one_block(): jnp.einsum('gqd,kgd->gqk', query_group, key_block, preferred_element_type...]
    ppermute x0 -> x23, waiting for transfers between devices: none -> 34.2 us  [swap(): lax.ppermute(value, axis, [(i, i ^ mask) for i in range(lax.axis_size(axi...]
    all_gather x3 -> x0, blocking collectives: 25.6 us -> none  [the longest x1 8.87 us: shards(): lax.all_gather(request, 'ctx', axis=0, tiled=True)]
    ppermute x0 -> x23, starting transfers between devices: none -> 23.8 us  [swap(): lax.ppermute(value, axis, [(i, i ^ mask) for i in range(lax.axis_size(axi...]
    all_to_all x2 -> x0, blocking collectives: 21.3 us -> none  [the longest x1 12.3 us: shards(): lax.all_to_all(fresh_values, 'head', split_axis=1, concat_axis=0, tiled=T...]
    reduce_sum x5 -> x0, other arithmetic: 14.1 us -> none  [the longest x4 14 us: one_block(): totals = totals * factor + jnp.sum(weights, axis=-1)]
  transfers between devices with their start and end apart: 6 -> 23, of which waited for: 2 -> 8; matrix products, arithmetic and copies ran while one was open for 23% -> 3% of each run, Pallas kernels for 0% -> 37%
where the time goes in v1:
time: 112 us
  Pallas kernels  42.9 us (38%)
  waiting for transfers between devices  34.2 us (31%)
  starting transfers between devices  23.8 us (21%)
  local copies, waits for them, and re-layouts  7.2 us (6%)
  other arithmetic  2.32 us (2%)
  between operations  1.49 us (1%)
    pallas_call x4, Pallas kernels, chunk(): pl.pallas_call(functools.partial(chunk_kernel, x, n_ctx, n_head, requests...  37.6 us
    ppermute x23, waiting for transfers between devices, swap(): lax.ppermute(value, axis, [(i, i ^ mask) for i in range(lax.axis_size(axi...  34.2 us
    ppermute x23, starting transfers between devices, swap(): lax.ppermute(value, axis, [(i, i ^ mask) for i in range(lax.axis_size(axi...  23.8 us
    unnamed x17, local copies, waits for them, and re-layouts  5.81 us
  transfers between devices with their start and end apart: 23, of which 8 were waited for; matrix products, arithmetic and copies ran while one was open for 3% of the time, Pallas kernels for 37%

profile of v1, /device:TPU:0, one launch (start us, length us, event | category | flops | bytes accessed | tf_op | source)
XLA Modules:
  0.0 111.9 jit_solution(8734527527385954664)
XLA Ops:
  0.0 1.7 %shard_map.83.refs_0_ = bf16[272,512]{1,0:T(8,128)(2,1)} custom-call(s32[16]{0:T(128)} %pages.1, bf16[256,256]{1,0:T(8,128)(2,1)} %k_ref.2, bf16[256,256]{1,0:T(8,128)(2,1)} %v_ref.2), custom_call_target="tpu_custom_call" | custom-call | tf_op jit(solution)/shard_map/pallas_call | solution.py:224
  1.7 3.9 %collective-permute-start.6 = (bf16[272,512]{1,0:T(8,128)(2,1)}, bf16[272,512]{1,0:T(8,128)(2,1)S(1)}, u32[]{:S(2)}, u32[]{:S(2)}) collective-permute-start(bf16[272,512]{1,0:T(8,128)(2,1)} %shard_map.83.refs_0_), channel_id=1, source_target_pairs={{0,24},{4,28},{8,16},{12,20},{16,8},{20,12},{24,0},{28,4},{1,25},{... | collective-permute-start | bytes 835592 | tf_op jit(solution)/shard_map/ppermute | solution.py:194
  5.6 0.5 collective-permute-start.4
  6.1 0.1 collective-permute-start.2
  6.2 1.4 %fusion = (s32[1]{0:T(128)}, s32[1]{0:T(128)}) fusion(s32[2]{0:T(128)} %param.14), kind=kLoop, calls=%fused_computation.6 | loop fusion | bytes 16 | tf_op jit(solution)/shard_map/slice | solution.py:213
  8.9 1.3 %pad_add_fusion.info = s32[4]{0:T(128)} fusion(s32[1]{0:T(128)S(6)} %add.13, s32[1]{0:T(128)} %get-tuple-element.22, s32[1]{0:T(128)} %bitcast.1, s32[1]{0:T(128)} %bitcast), kind=kLoop, calls=%fused_computation.5 | loop fusion | flops 12 | bytes 32 | tf_op jit(solution)/shard_map/concatenate | solution.py:211
  10.2 1.7 %shard_map.84 = (bf16[64,512]{1,0:T(8,128)(2,1)}, bf16[64,512]{1,0:T(8,128)(2,1)}, bf16[64,512]{1,0:T(8,128)(2,1)}, bf16[64,512]{1,0:T(8,128)(2,1)}) custom-call(s32[4]{0:T(128)} %pad_add_fusion.info, bf16[64,1024]{1,0:T(8,128)(2,1)} %k_ref.3, bf16[64,1024]{1,0:T(8,128)(2,1)} %v_ref.3), custom_call_target="tpu_custom_call" | custom-call | tf_op jit(solution)/shard_map/pallas_call | solution.py:217
  11.9 2.1 %collective-permute-start.8 = (bf16[64,512]{1,0:T(8,128)(2,1)}, bf16[64,512]{1,0:T(8,128)(2,1)S(1)}, u32[]{:S(2)}, u32[]{:S(2)}) collective-permute-start(bf16[64,512]{1,0:T(8,128)(2,1)} %get-tuple-element.15), channel_id=1, source_target_pairs={{0,1},{1,0},{2,3},{3,2},{4,5},{5,4},{6,7},{7,6},{8,9},{9,8},{10,11... | collective-permute-start | bytes 196616 | tf_op jit(solution)/shard_map/ppermute | solution.py:194
  13.9 2.6 %collective-permute-start.9 = (bf16[64,512]{1,0:T(8,128)(2,1)}, bf16[64,512]{1,0:T(8,128)(2,1)S(1)}, u32[]{:S(2)}, u32[]{:S(2)}) collective-permute-start(bf16[64,512]{1,0:T(8,128)(2,1)} %get-tuple-element.16), channel_id=1, source_target_pairs={{0,2},{1,3},{2,0},{3,1},{4,6},{5,7},{6,4},{7,5},{8,10},{9,11},{10,... | collective-permute-start | bytes 196616 | tf_op jit(solution)/shard_map/ppermute | solution.py:194
  16.5 1.9 %shard_map.82 = (bf16[64,1024]{1,0:T(8,128)(2,1)}, bf16[64,1024]{1,0:T(8,128)(2,1)}, bf16[64,1024]{1,0:T(8,128)(2,1)}, bf16[64,1024]{1,0:T(8,128)(2,1)}) custom-call(s32[4]{0:T(128)} %pad_add_fusion.info, bf16[64,4096]{1,0:T(8,128)(2,1)} %q_ref.1), custom_call_target="tpu_custom_call" | custom-call | tf_op jit(solution)/shard_map/pallas_call | solution.py:231
  18.4 0.8 constant_dynamic-update-slice_fusion.3
  19.3 0.0 collective-permute-done.8
  19.3 0.0 collective-permute-start.1
  19.3 0.7 collective-permute-done.9
  20.0 1.8 %collective-permute-start.10 = (bf16[64,512]{1,0:T(8,128)(2,1)}, bf16[64,512]{1,0:T(8,128)(2,1)S(1)}, u32[]{:S(2)}, u32[]{:S(2)}) collective-permute-start(bf16[64,512]{1,0:T(8,128)(2,1)} %get-tuple-element.17), channel_id=1, source_target_pairs={{0,3},{1,2},{2,1},{3,0},{4,7},{5,6},{6,5},{7,4},{8,11},{9,10},{10,... | collective-permute-start | bytes 196616 | tf_op jit(solution)/shard_map/ppermute | solution.py:194
  21.8 4.5 %collective-permute-done.10 = bf16[64,512]{1,0:T(8,128)(2,1)S(1)} collective-permute-done((bf16[64,512]{1,0:T(8,128)(2,1)}, bf16[64,512]{1,0:T(8,128)(2,1)S(1)}, u32[]{:S(2)}, u32[]{:S(2)}) %collective-permute-start.10) | collective-permute-done | bytes 65568 | tf_op jit(solution)/shard_map/ppermute | solution.py:194
  26.4 1.8 %collective-permute-start = (bf16[64,1024]{1,0:T(8,128)(2,1)}, bf16[64,1024]{1,0:T(8,128)(2,1)S(1)}, u32[]{:S(2)}, u32[]{:S(2)}) collective-permute-start(bf16[64,1024]{1,0:T(8,128)(2,1)} %get-tuple-element.13), channel_id=1, source_target_pairs={{0,3},{1,2},{2,1},{3,0},{4,7},{5,6},{6,5},{7,4},{8,11},{9,10},{10,... | collective-permute-start | bytes 393224 | tf_op jit(solution)/shard_map/ppermute | solution.py:194
  28.2 5.1 %collective-permute-done.q_hbm = bf16[64,1024]{1,0:T(8,128)(2,1)S(1)} collective-permute-done((bf16[64,1024]{1,0:T(8,128)(2,1)}, bf16[64,1024]{1,0:T(8,128)(2,1)S(1)}, u32[]{:S(2)}, u32[]{:S(2)}) %collective-permute-start) | collective-permute-done | bytes 131104 | tf_op jit(solution)/shard_map/ppermute | solution.py:194
  33.3 2.4 %collective-permute-start.16 = (bf16[256,512]{1,0:T(8,128)(2,1)S(1)}, bf16[256,512]{1,0:T(8,128)(2,1)S(1)}, u32[]{:S(2)}, u32[]{:S(2)}) collective-permute-start(bf16[256,512]{1,0:T(8,128)(2,1)S(1)} %constant_dynamic-update-slice_fusion.refs_8_), channel_id=1, source_target_pairs={{0,24},{4,28},{8,16},{12,20},{16,8},{20,12},{24,0},{28,4},{1,25},{... | collective-permute-start | bytes 786440 | tf_op jit(solution)/shard_map/ppermute | solution.py:194
  35.8 0.0 collective-permute-done.6.refs_6_
  35.8 0.5 collective-permute-start.14
  36.3 0.0 collective-permute-done.4.refs_4_
  36.3 0.0 collective-permute-start.7
  36.3 0.0 collective-permute-done.2.refs_2_
  36.3 0.6 collective-permute-start.12
  36.9 0.0 collective-permute-done.1.refs_1_
  36.9 0.2 collective-permute-start.11
  37.1 4.9 %collective-permute-done.16.refs_14_ = bf16[256,512]{1,0:T(8,128)(2,1)S(1)} collective-permute-done((bf16[256,512]{1,0:T(8,128)(2,1)S(1)}, bf16[256,512]{1,0:T(8,128)(2,1)S(1)}, u32[]{:S(2)}, u32[]{:S(2)}) %collective-permute-start.16) | collective-permute-done | bytes 262176 | tf_op jit(solution)/shard_map/ppermute | solution.py:194
  41.9 0.0 collective-permute-start.5
  41.9 3.6 %collective-permute-done.14.refs_12_ = bf16[256,512]{1,0:T(8,128)(2,1)S(1)} collective-permute-done((bf16[256,512]{1,0:T(8,128)(2,1)S(1)}, bf16[256,512]{1,0:T(8,128)(2,1)S(1)}, u32[]{:S(2)}, u32[]{:S(2)}) %collective-permute-start.14) | collective-permute-done | bytes 262176 | tf_op jit(solution)/shard_map/ppermute | solution.py:194
  45.6 0.0 collective-permute-start.3
  45.6 0.7 collective-permute-done.12.refs_10_
  46.3 0.0 collective-permute-start.17
  46.3 0.0 collective-permute-done.11.refs_9_
  46.3 0.5 collective-permute-start.15
  46.8 0.0 collective-permute-done.7.refs_7_
  46.8 0.1 collective-permute-start.13
  46.9 0.0 collective-permute-done.5.refs_5_
  46.9 0.0 collective-permute-start.19
  46.9 0.2 collective-permute-done.3.refs_3_
  47.1 2.2 %collective-permute-start.21 = (bf16[64,1024]{1,0:T(8,128)(2,1)}, bf16[64,1024]{1,0:T(8,128)(2,1)S(1)}, u32[]{:S(2)}, u32[]{:S(2)}) collective-permute-start(bf16[64,1024]{1,0:T(8,128)(2,1)} %get-tuple-element.19), channel_id=1, source_target_pairs={{0,1},{1,0},{2,3},{3,2},{4,5},{5,4},{6,7},{7,6},{8,9},{9,8},{10,11... | collective-permute-start | bytes 393224 | tf_op jit(solution)/shard_map/ppermute | solution.py:194
  49.3 0.0 collective-permute-done.17.refs_15_
  49.3 0.0 collective-permute-done.15.refs_13_
  49.3 0.0 collective-permute-done.13.refs_11_
  49.3 0.0 copy-start
  49.3 3.4 %copy-done = bf16[1024,4096]{1,0:T(8,128)(2,1)S(1)} copy-done((bf16[1024,4096]{1,0:T(8,128)(2,1)S(1)}, bf16[1024,4096]{1,0:T(8,128)(2,1)}, u32[]{:S(2)}) %copy-start) | copy-done | bytes 8388632
  52.7 1.0 copy-done.1
  53.7 0.6 copy-done.4
  54.3 9.4 %shard_map.85 = bf16[64,4096]{1,0:T(8,128)(2,1)S(1)} custom-call(s32[4]{0:T(128)S(1)} %copy-done.4, bf16[64,1024]{1,0:T(8,128)(2,1)S(1)} %collective-permute-done.q_hbm, bf16[272,512]{1,0:T(8,128)(2,1)S(1)} %copy-done.1, bf16[272,512]{1,0:T(8,128)(2,1)S(1)} %collective-permute-done.1.refs_1_, bf16[272,512]{1,0:T(8,128)(2,1)S(1)} %collective-permute-done.2.refs_2_, ...), custom_call_target="tpu_custom_call" | custom-call | flops 2684354560 | bytes 12582912 | tf_op jit(solution)/shard_map/pallas_call | solution.py:170
  63.6 2.0 %collective-permute-start.18 = (bf16[64,4096]{1,0:T(8,128)(2,1)S(1)}, bf16[64,4096]{1,0:T(8,128)(2,1)S(1)}, u32[]{:S(2)}, u32[]{:S(2)}) collective-permute-start(bf16[64,4096]{1,0:T(8,128)(2,1)S(1)} %shard_map.85), channel_id=1, source_target_pairs={{0,3},{1,2},{2,1},{3,0},{4,7},{5,6},{6,5},{7,4},{8,11},{9,10},{10,... | collective-permute-start | bytes 1572872 | tf_op jit(solution)/shard_map/ppermute | solution.py:194
  65.7 0.0 collective-permute-done.19.q_hbm
  65.7 0.0 copy-done.2
  65.7 9.4 %shard_map.86 = bf16[64,4096]{1,0:T(8,128)(2,1)S(1)} custom-call(s32[4]{0:T(128)S(1)} %copy-done.4, bf16[64,1024]{1,0:T(8,128)(2,1)S(1)} %collective-permute-done.19.q_hbm, bf16[272,512]{1,0:T(8,128)(2,1)S(1)} %copy-done.2, bf16[272,512]{1,0:T(8,128)(2,1)S(1)} %collective-permute-done.1.refs_1_, bf16[272,512]{1,0:T(8,128)(2,1)S(1)} %collective-permute-done.2.refs_2_, ...), custom_call_target="tpu_custom_call" | custom-call | flops 2684354560 | bytes 12582912 | tf_op jit(solution)/shard_map/pallas_call | solution.py:170
  75.0 0.0 slice-start.1
  75.1 0.1 collective-permute-start.20
  75.1 0.0 collective-permute-done.21.q_hbm
  75.2 9.6 %shard_map.87 = bf16[64,4096]{1,0:T(8,128)(2,1)S(1)} custom-call(s32[4]{0:T(128)S(1)} %copy-done.4, bf16[64,1024]{1,0:T(8,128)(2,1)S(1)} %collective-permute-done.21.q_hbm, bf16[272,512]{1,0:T(8,128)(2,1)S(1)} %copy-done.2, bf16[272,512]{1,0:T(8,128)(2,1)S(1)} %collective-permute-done.1.refs_1_, bf16[272,512]{1,0:T(8,128)(2,1)S(1)} %collective-permute-done.2.refs_2_, ...), custom_call_target="tpu_custom_call" | custom-call | flops 2684354560 | bytes 12582912 | tf_op jit(solution)/shard_map/pallas_call | solution.py:170
  84.7 2.5 %collective-permute-start.22 = (bf16[64,4096]{1,0:T(8,128)(2,1)S(1)}, bf16[64,4096]{1,0:T(8,128)(2,1)S(1)}, u32[]{:S(2)}, u32[]{:S(2)}) collective-permute-start(bf16[64,4096]{1,0:T(8,128)(2,1)S(1)} %shard_map.87), channel_id=1, source_target_pairs={{0,1},{1,0},{2,3},{3,2},{4,5},{5,4},{6,7},{7,6},{8,9},{9,8},{10,11... | collective-permute-start | bytes 1572872 | tf_op jit(solution)/shard_map/ppermute | solution.py:194
  87.2 0.0 copy-done.3
  87.2 9.4 %shard_map.88 = bf16[64,4096]{1,0:T(8,128)(2,1)S(1)} custom-call(s32[4]{0:T(128)S(1)} %copy-done.4, bf16[64,1024]{1,0:T(8,128)(2,1)S(1)} %copy-done.3, bf16[272,512]{1,0:T(8,128)(2,1)S(1)} %copy-done.2, bf16[272,512]{1,0:T(8,128)(2,1)S(1)} %collective-permute-done.1.refs_1_, bf16[272,512]{1,0:T(8,128)(2,1)S(1)} %collective-permute-done.2.refs_2_, ...), custom_call_target="tpu_custom_call" | custom-call | flops 2684354560 | bytes 12582912 | tf_op jit(solution)/shard_map/pallas_call | solution.py:170
  96.6 0.0 collective-permute-done.18
  96.6 14.3 %collective-permute-done.20 = bf16[64,4096]{1,0:T(8,128)(2,1)S(1)} collective-permute-done((bf16[64,4096]{1,0:T(8,128)(2,1)S(1)}, bf16[64,4096]{1,0:T(8,128)(2,1)S(1)}, u32[]{:S(2)}, u32[]{:S(2)}) %collective-permute-start.20) | collective-permute-done | bytes 524320 | tf_op jit(solution)/shard_map/ppermute | solution.py:194
  110.9 0.0 collective-permute-done.22
  110.9 1.1 add_convert_fusion
  (11 shorter events, 0.0 us)
Async XLA Ops:
  1.7 64.0 %copy-start.2 = (bf16[272,512]{1,0:T(8,128)(2,1)S(1)}, bf16[272,512]{1,0:T(8,128)(2,1)}, u32[]{:S(2)}) copy-start(bf16[272,512]{1,0:T(8,128)(2,1)} %shard_map.83.refs_0_) | copy-start | bytes 835588
  1.7 34.1 %collective-permute-start.6 = (bf16[272,512]{1,0:T(8,128)(2,1)}, bf16[272,512]{1,0:T(8,128)(2,1)S(1)}, u32[]{:S(2)}, u32[]{:S(2)}) collective-permute-start(bf16[272,512]{1,0:T(8,128)(2,1)} %shard_map.83.refs_0_), channel_id=1, source_target_pairs={{0,24},{4,28},{8,16},{12,20},{16,8},{20,12},{24,0},{28,4},{1,25},{... | collective-permute-start | bytes 835592 | tf_op jit(solution)/shard_map/ppermute | solution.py:194
  5.6 30.7 %collective-permute-start.4 = (bf16[272,512]{1,0:T(8,128)(2,1)}, bf16[272,512]{1,0:T(8,128)(2,1)S(1)}, u32[]{:S(2)}, u32[]{:S(2)}) collective-permute-start(bf16[272,512]{1,0:T(8,128)(2,1)} %shard_map.83.refs_0_), channel_id=1, source_target_pairs={{0,16},{4,20},{8,24},{12,28},{16,0},{20,4},{24,8},{28,12},{1,17},{... | collective-permute-start | bytes 835592 | tf_op jit(solution)/shard_map/ppermute | solution.py:194
  6.1 30.2 %collective-permute-start.2 = (bf16[272,512]{1,0:T(8,128)(2,1)}, bf16[272,512]{1,0:T(8,128)(2,1)S(1)}, u32[]{:S(2)}, u32[]{:S(2)}) collective-permute-start(bf16[272,512]{1,0:T(8,128)(2,1)} %shard_map.83.refs_0_), channel_id=1, source_target_pairs={{0,8},{4,12},{8,0},{12,4},{16,24},{20,28},{24,16},{28,20},{1,9},{5... | collective-permute-start | bytes 835592 | tf_op jit(solution)/shard_map/ppermute | solution.py:194
  11.9 7.4 %collective-permute-start.8 = (bf16[64,512]{1,0:T(8,128)(2,1)}, bf16[64,512]{1,0:T(8,128)(2,1)S(1)}, u32[]{:S(2)}, u32[]{:S(2)}) collective-permute-start(bf16[64,512]{1,0:T(8,128)(2,1)} %get-tuple-element.15), channel_id=1, source_target_pairs={{0,1},{1,0},{2,3},{3,2},{4,5},{5,4},{6,7},{7,6},{8,9},{9,8},{10,11... | collective-permute-start | bytes 196616 | tf_op jit(solution)/shard_map/ppermute | solution.py:194
  13.9 6.1 %collective-permute-start.9 = (bf16[64,512]{1,0:T(8,128)(2,1)}, bf16[64,512]{1,0:T(8,128)(2,1)S(1)}, u32[]{:S(2)}, u32[]{:S(2)}) collective-permute-start(bf16[64,512]{1,0:T(8,128)(2,1)} %get-tuple-element.16), channel_id=1, source_target_pairs={{0,2},{1,3},{2,0},{3,1},{4,6},{5,7},{6,4},{7,5},{8,10},{9,11},{10,... | collective-permute-start | bytes 196616 | tf_op jit(solution)/shard_map/ppermute | solution.py:194
  19.3 17.6 %collective-permute-start.1 = (bf16[272,512]{1,0:T(8,128)(2,1)}, bf16[272,512]{1,0:T(8,128)(2,1)S(1)}, u32[]{:S(2)}, u32[]{:S(2)}) collective-permute-start(bf16[272,512]{1,0:T(8,128)(2,1)} %shard_map.83.refs_0_), channel_id=1, source_target_pairs={{0,4},{4,0},{8,12},{12,8},{16,20},{20,16},{24,28},{28,24},{1,5},{5... | collective-permute-start | bytes 835592 | tf_op jit(solution)/shard_map/ppermute | solution.py:194
  20.0 6.3 %collective-permute-start.10 = (bf16[64,512]{1,0:T(8,128)(2,1)}, bf16[64,512]{1,0:T(8,128)(2,1)S(1)}, u32[]{:S(2)}, u32[]{:S(2)}) collective-permute-start(bf16[64,512]{1,0:T(8,128)(2,1)} %get-tuple-element.17), channel_id=1, source_target_pairs={{0,3},{1,2},{2,1},{3,0},{4,7},{5,6},{6,5},{7,4},{8,11},{9,10},{10,... | collective-permute-start | bytes 196616 | tf_op jit(solution)/shard_map/ppermute | solution.py:194
  26.4 7.0 %collective-permute-start = (bf16[64,1024]{1,0:T(8,128)(2,1)}, bf16[64,1024]{1,0:T(8,128)(2,1)S(1)}, u32[]{:S(2)}, u32[]{:S(2)}) collective-permute-start(bf16[64,1024]{1,0:T(8,128)(2,1)} %get-tuple-element.13), channel_id=1, source_target_pairs={{0,3},{1,2},{2,1},{3,0},{4,7},{5,6},{6,5},{7,4},{8,11},{9,10},{10,... | collective-permute-start | bytes 393224 | tf_op jit(solution)/shard_map/ppermute | solution.py:194
  33.3 8.6 %collective-permute-start.16 = (bf16[256,512]{1,0:T(8,128)(2,1)S(1)}, bf16[256,512]{1,0:T(8,128)(2,1)S(1)}, u32[]{:S(2)}, u32[]{:S(2)}) collective-permute-start(bf16[256,512]{1,0:T(8,128)(2,1)S(1)} %constant_dynamic-update-slice_fusion.refs_8_), channel_id=1, source_target_pairs={{0,24},{4,28},{8,16},{12,20},{16,8},{20,12},{24,0},{28,4},{1,25},{... | collective-permute-start | bytes 786440 | tf_op jit(solution)/shard_map/ppermute | solution.py:194
  35.8 9.8 %collective-permute-start.14 = (bf16[256,512]{1,0:T(8,128)(2,1)S(1)}, bf16[256,512]{1,0:T(8,128)(2,1)S(1)}, u32[]{:S(2)}, u32[]{:S(2)}) collective-permute-start(bf16[256,512]{1,0:T(8,128)(2,1)S(1)} %constant_dynamic-update-slice_fusion.refs_8_), channel_id=1, source_target_pairs={{0,16},{4,20},{8,24},{12,28},{16,0},{20,4},{24,8},{28,12},{1,17},{... | collective-permute-start | bytes 786440 | tf_op jit(solution)/shard_map/ppermute | solution.py:194
  36.3 10.5 %collective-permute-start.7 = (bf16[272,512]{1,0:T(8,128)(2,1)S(1)}, bf16[272,512]{1,0:T(8,128)(2,1)S(1)}, u32[]{:S(2)}, u32[]{:S(2)}) collective-permute-start(bf16[272,512]{1,0:T(8,128)(2,1)S(1)} %collective-permute-done.6.refs_6_), channel_id=1, source_target_pairs={{0,4},{4,0},{8,12},{12,8},{16,20},{20,16},{24,28},{28,24},{1,5},{5... | collective-permute-start | bytes 835592 | tf_op jit(solution)/shard_map/ppermute | solution.py:194
  36.3 10.0 %collective-permute-start.12 = (bf16[256,512]{1,0:T(8,128)(2,1)S(1)}, bf16[256,512]{1,0:T(8,128)(2,1)S(1)}, u32[]{:S(2)}, u32[]{:S(2)}) collective-permute-start(bf16[256,512]{1,0:T(8,128)(2,1)S(1)} %constant_dynamic-update-slice_fusion.refs_8_), channel_id=1, source_target_pairs={{0,8},{4,12},{8,0},{12,4},{16,24},{20,28},{24,16},{28,20},{1,9},{5... | collective-permute-start | bytes 786440 | tf_op jit(solution)/shard_map/ppermute | solution.py:194
  36.9 9.4 %collective-permute-start.11 = (bf16[256,512]{1,0:T(8,128)(2,1)S(1)}, bf16[256,512]{1,0:T(8,128)(2,1)S(1)}, u32[]{:S(2)}, u32[]{:S(2)}) collective-permute-start(bf16[256,512]{1,0:T(8,128)(2,1)S(1)} %constant_dynamic-update-slice_fusion.refs_8_), channel_id=1, source_target_pairs={{0,4},{4,0},{8,12},{12,8},{16,20},{20,16},{24,28},{28,24},{1,5},{5... | collective-permute-start | bytes 786440 | tf_op jit(solution)/shard_map/ppermute | solution.py:194
  41.9 5.0 %collective-permute-start.5 = (bf16[272,512]{1,0:T(8,128)(2,1)S(1)}, bf16[272,512]{1,0:T(8,128)(2,1)S(1)}, u32[]{:S(2)}, u32[]{:S(2)}) collective-permute-start(bf16[272,512]{1,0:T(8,128)(2,1)S(1)} %collective-permute-done.4.refs_4_), channel_id=1, source_target_pairs={{0,4},{4,0},{8,12},{12,8},{16,20},{20,16},{24,28},{28,24},{1,5},{5... | collective-permute-start | bytes 835592 | tf_op jit(solution)/shard_map/ppermute | solution.py:194
  45.6 1.6 %collective-permute-start.3 = (bf16[272,512]{1,0:T(8,128)(2,1)S(1)}, bf16[272,512]{1,0:T(8,128)(2,1)S(1)}, u32[]{:S(2)}, u32[]{:S(2)}) collective-permute-start(bf16[272,512]{1,0:T(8,128)(2,1)S(1)} %collective-permute-done.2.refs_2_), channel_id=1, source_target_pairs={{0,4},{4,0},{8,12},{12,8},{16,20},{20,16},{24,28},{28,24},{1,5},{5... | collective-permute-start | bytes 835592 | tf_op jit(solution)/shard_map/ppermute | solution.py:194
  46.3 3.0 %collective-permute-start.17 = (bf16[256,512]{1,0:T(8,128)(2,1)S(1)}, bf16[256,512]{1,0:T(8,128)(2,1)S(1)}, u32[]{:S(2)}, u32[]{:S(2)}) collective-permute-start(bf16[256,512]{1,0:T(8,128)(2,1)S(1)} %collective-permute-done.16.refs_14_), channel_id=1, source_target_pairs={{0,4},{4,0},{8,12},{12,8},{16,20},{20,16},{24,28},{28,24},{1,5},{5... | collective-permute-start | bytes 786440 | tf_op jit(solution)/shard_map/ppermute | solution.py:194
  46.3 3.0 %collective-permute-start.15 = (bf16[256,512]{1,0:T(8,128)(2,1)S(1)}, bf16[256,512]{1,0:T(8,128)(2,1)S(1)}, u32[]{:S(2)}, u32[]{:S(2)}) collective-permute-start(bf16[256,512]{1,0:T(8,128)(2,1)S(1)} %collective-permute-done.14.refs_12_), channel_id=1, source_target_pairs={{0,4},{4,0},{8,12},{12,8},{16,20},{20,16},{24,28},{28,24},{1,5},{5... | collective-permute-start | bytes 786440 | tf_op jit(solution)/shard_map/ppermute | solution.py:194
  46.8 2.5 %collective-permute-start.13 = (bf16[256,512]{1,0:T(8,128)(2,1)S(1)}, bf16[256,512]{1,0:T(8,128)(2,1)S(1)}, u32[]{:S(2)}, u32[]{:S(2)}) collective-permute-start(bf16[256,512]{1,0:T(8,128)(2,1)S(1)} %collective-permute-done.12.refs_10_), channel_id=1, source_target_pairs={{0,4},{4,0},{8,12},{12,8},{16,20},{20,16},{24,28},{28,24},{1,5},{5... | collective-permute-start | bytes 786440 | tf_op jit(solution)/shard_map/ppermute | solution.py:194
  46.9 18.8 %collective-permute-start.19 = (bf16[64,1024]{1,0:T(8,128)(2,1)}, bf16[64,1024]{1,0:T(8,128)(2,1)S(1)}, u32[]{:S(2)}, u32[]{:S(2)}) collective-permute-start(bf16[64,1024]{1,0:T(8,128)(2,1)} %get-tuple-element.18), channel_id=1, source_target_pairs={{0,2},{1,3},{2,0},{3,1},{4,6},{5,7},{6,4},{7,5},{8,10},{9,11},{10,... | collective-permute-start | bytes 393224 | tf_op jit(solution)/shard_map/ppermute | solution.py:194
  47.1 28.0 %collective-permute-start.21 = (bf16[64,1024]{1,0:T(8,128)(2,1)}, bf16[64,1024]{1,0:T(8,128)(2,1)S(1)}, u32[]{:S(2)}, u32[]{:S(2)}) collective-permute-start(bf16[64,1024]{1,0:T(8,128)(2,1)} %get-tuple-element.19), channel_id=1, source_target_pairs={{0,1},{1,0},{2,3},{3,2},{4,5},{5,4},{6,7},{7,6},{8,9},{9,8},{10,11... | collective-permute-start | bytes 393224 | tf_op jit(solution)/shard_map/ppermute | solution.py:194
  49.3 3.4 %copy-start = (bf16[1024,4096]{1,0:T(8,128)(2,1)S(1)}, bf16[1024,4096]{1,0:T(8,128)(2,1)}, u32[]{:S(2)}) copy-start(bf16[1024,4096]{1,0:T(8,128)(2,1)} %refs_16_.7) | copy-start | bytes 25165828
  52.7 1.0 copy-start.1
  53.7 0.6 copy-start.4
  63.6 33.0 %collective-permute-start.18 = (bf16[64,4096]{1,0:T(8,128)(2,1)S(1)}, bf16[64,4096]{1,0:T(8,128)(2,1)S(1)}, u32[]{:S(2)}, u32[]{:S(2)}) collective-permute-start(bf16[64,4096]{1,0:T(8,128)(2,1)S(1)} %shard_map.85), channel_id=1, source_target_pairs={{0,3},{1,2},{2,1},{3,0},{4,7},{5,6},{6,5},{7,4},{8,11},{9,10},{10,... | collective-permute-start | bytes 1572872 | tf_op jit(solution)/shard_map/ppermute | solution.py:194
  65.7 21.5 %slice-start = ((s8[8388608]{0:T(1024)(128)(4,1)}), s8[4194304]{0:T(1024)(128)(4,1)S(1)}, s32[]{:S(2)}) async-start(s8[8388608]{0:T(1024)(128)(4,1)} %bitcast.2), calls=%async_computation | async-start | bytes 8388608
  75.0 12.1 %slice-start.1 = ((s8[8388608]{0:T(1024)(128)(4,1)}), s8[4194304]{0:T(1024)(128)(4,1)S(1)}, s32[]{:S(2)}) async-start(s8[8388608]{0:T(1024)(128)(4,1)} %bitcast.2), calls=%async_computation.1 | async-start | bytes 8388608
  75.1 12.1 %copy-start.3 = (bf16[64,1024]{1,0:T(8,128)(2,1)S(1)}, bf16[64,1024]{1,0:T(8,128)(2,1)}, u32[]{:S(2)}) copy-start(bf16[64,1024]{1,0:T(8,128)(2,1)} %get-tuple-element.20.q_hbm) | copy-start | bytes 393220
  75.1 35.8 %collective-permute-start.20 = (bf16[64,4096]{1,0:T(8,128)(2,1)S(1)}, bf16[64,4096]{1,0:T(8,128)(2,1)S(1)}, u32[]{:S(2)}, u32[]{:S(2)}) collective-permute-start(bf16[64,4096]{1,0:T(8,128)(2,1)S(1)} %shard_map.86), channel_id=1, source_target_pairs={{0,2},{1,3},{2,0},{3,1},{4,6},{5,7},{6,4},{7,5},{8,10},{9,11},{10,... | collective-permute-start | bytes 1572872 | tf_op jit(solution)/shard_map/ppermute | solution.py:194
  84.7 26.1 %collective-permute-start.22 = (bf16[64,4096]{1,0:T(8,128)(2,1)S(1)}, bf16[64,4096]{1,0:T(8,128)(2,1)S(1)}, u32[]{:S(2)}, u32[]{:S(2)}) collective-permute-start(bf16[64,4096]{1,0:T(8,128)(2,1)S(1)} %shard_map.87), channel_id=1, source_target_pairs={{0,1},{1,0},{2,3},{3,2},{4,5},{5,4},{6,7},{7,6},{8,9},{9,8},{10,11... | collective-permute-start | bytes 1572872 | tf_op jit(solution)/shard_map/ppermute | solution.py:194

commit v2 on v1

v2 whole, which is shorter than its diff:
```python
import functools
import math

import jax
import jax.numpy as jnp
from jax import lax
from jax.experimental import pallas as pl
from jax.experimental.pallas import tpu as pltpu
from jax.sharding import PartitionSpec as P

HD = 128
PAGE = 16
LANES = 128
HIDDEN = -1e30
BF16 = jnp.bfloat16
F32 = jnp.float32


def iota(shape, dim):
    return lax.broadcasted_iota(jnp.int32, shape, dim)


def pack_kernel(pages, k_ref, v_ref, q_ref, ck_ref, cv_ref, *outs):
    n_head = (len(outs) - 1) // 2
    head = lax.axis_index("head")
    width = k_ref.shape[1] // n_head
    q_width = q_ref.shape[1] // n_head
    for x in range(n_head):
        other = head ^ x
        columns = pl.ds(pl.multiple_of(other * width, width), width)
        outs[x][:, :width] = k_ref[:, columns]
        outs[x][:, width:] = v_ref[:, columns]
        outs[n_head + x][...] = q_ref[:, pl.ds(pl.multiple_of(other * q_width, q_width), q_width)]
    out = outs[-1]
    tokens = ck_ref.shape[0]
    count = tokens // PAGE
    out[:tokens, :width] = ck_ref[...]
    out[:tokens, width:] = cv_ref[...]
    page = iota((count, 2 * width), 0)
    owner = jnp.zeros((count, 2 * width), jnp.int32)
    for p in range(count):
        owner = jnp.where(page == p, pages[p], owner)
    out[tokens:, :] = owner.astype(F32).astype(BF16)


def vmem():
    return pl.BlockSpec(memory_space=pltpu.VMEM)


def smem():
    return pl.BlockSpec(memory_space=pltpu.SMEM)


class Layout:
    def __init__(self, lengths, rows, q_width, kv_width, n_ctx, n_head):
        self.rows, self.n_ctx, self.n_head = rows, n_ctx, n_head
        self.groups = kv_width // (2 * HD)
        self.repeat = q_width // (self.groups * HD)
        self.half = n_head * rows // 2
        self.c, self.h = lax.axis_index("ctx"), lax.axis_index("head")
        self.ends, end = [], 0
        for r in range(lengths.shape[0]):
            end = end + lengths[r]
            self.ends.append(end)
        self.lane = iota((rows, LANES), 1)
        self.row = iota((rows, LANES), 0)
        self.row_lane = self.lane - (LANES - rows)

    def start_of(self, rank, head):
        first = head * self.rows < self.half
        piece = jnp.where(first, rank, 2 * self.n_ctx - 1 - rank)
        return piece * self.half + lax.rem(head * self.rows, self.half)

    def request(self, position):
        request = jnp.zeros(position.shape, jnp.int32)
        for end in self.ends:
            request += (position >= end).astype(jnp.int32)
        return request

    def query_rows(self, q, x):
        own = self.lane == self.request(self.start_of(self.c, self.h ^ x) + self.row)
        mask = jnp.where(own | (self.row_lane == self.row), 1.0, 0.0).astype(BF16)
        result = []
        for g in range(self.groups):
            heads = [
                jnp.concatenate([q[:, n * HD:(n + 1) * HD], mask], axis=1)
                for n in range(g * self.repeat, (g + 1) * self.repeat)
            ]
            result.append(jnp.concatenate(heads, axis=0))
        return result

    def fresh_mask(self, b, x_query):
        p0 = self.start_of(self.c, self.h ^ x_query)
        parts = []
        for x in range(self.n_head):
            position = self.start_of(self.c ^ b, self.h ^ x) + self.row
            other = (self.lane < len(self.ends)) & (self.request(position) != self.lane)
            later = (self.row_lane >= 0) & (position > p0 + self.row_lane)
            parts.append(jnp.where(other | later, HIDDEN, 0.0))
        return jnp.concatenate(parts, axis=0).astype(BF16)

    def cache_mask(self, owner):
        pages = owner.shape[0]
        lane = iota((pages, LANES), 1)
        other = (lane < len(self.ends)) & (owner.astype(F32) != lane.astype(F32))
        bias = jnp.where(other, HIDDEN, 0.0)
        bias = jnp.broadcast_to(bias[:, None, :], (pages, PAGE, LANES))
        return bias.reshape(pages * PAGE, LANES).astype(BF16)


def attend(q_rows, blocks, masks, scores, tokens, g, groups):
    scale = math.log2(math.e) / math.sqrt(HD)
    largest = None
    for b, (block, mask) in enumerate(zip(blocks, masks)):
        keys = jnp.concatenate([block[:tokens, g * HD:(g + 1) * HD], mask[...]], axis=1)
        s = lax.dot_general(q_rows, keys, (((1,), (1,)), ((), ())), preferred_element_type=F32)
        scores[:, b * tokens:(b + 1) * tokens] = s
        for t in range(tokens // LANES):
            part = s[:, t * LANES:(t + 1) * LANES]
            largest = part if largest is None else jnp.maximum(largest, part)
    top = jnp.max(largest, axis=1, keepdims=True) * scale
    ones = jnp.ones((tokens, HD), BF16)
    summed = jnp.zeros((q_rows.shape[0], 2 * HD), F32)
    for b, block in enumerate(blocks):
        weights = jnp.exp2(scores[:, b * tokens:(b + 1) * tokens] * scale - top).astype(BF16)
        values = jnp.concatenate([block[:tokens, (groups + g) * HD:(groups + g + 1) * HD], ones], axis=1)
        summed += jnp.dot(weights, values, preferred_element_type=F32)
    return summed, jnp.broadcast_to(top, (q_rows.shape[0], LANES))


def cache_kernel(n_ctx, n_head, lengths, *refs):
    query, cache = refs[:n_head], refs[n_head:n_head + n_ctx]
    summed, tops, scores, masks = refs[n_head + n_ctx:]
    rows, q_width = query[0].shape
    kv_width = cache[0].shape[1]
    tokens = masks.shape[1]
    at = Layout(lengths, rows, q_width, kv_width, n_ctx, n_head)
    for b in range(n_ctx):
        masks[b] = at.cache_mask(cache[b][tokens:, :LANES])
    for x in range(n_head):
        q_rows = at.query_rows(query[x], x)
        for g in range(at.groups):
            summed[x, g], tops[x, g] = attend(
                q_rows[g], cache, [masks.at[b] for b in range(n_ctx)], scores.at[g], tokens, g, at.groups
            )


def fresh_kernel(x, n_ctx, n_head, lengths, q, *refs):
    fresh = refs[:n_ctx]
    summed, tops, weight, out, scores, masks, mixed = refs[n_ctx:]
    rows, q_width = q.shape
    tokens, kv_width = fresh[0].shape
    at = Layout(lengths, rows, q_width, kv_width, n_ctx, n_head)
    for b in range(n_ctx):
        masks[b] = at.fresh_mask(b, x)
    q_rows = at.query_rows(q, x)
    for g in range(at.groups):
        sum_b, top_b = attend(
            q_rows[g], fresh, [masks.at[b] for b in range(n_ctx)], scores.at[g], tokens, g, at.groups
        )
        top_a = tops[x, g]
        top = jnp.maximum(top_a, top_b)
        factor_a, factor_b = jnp.exp2(top_a - top), jnp.exp2(top_b - top)
        value = summed[x, g, :, :HD] * factor_a + sum_b[:, :HD] * factor_b
        total = summed[x, g, :, HD:] * factor_a + sum_b[:, HD:] * factor_b
        attended = (value / total).astype(BF16)
        for j in range(at.repeat):
            n = g * at.repeat + j
            mixed[:, n * HD:(n + 1) * HD] = attended[j * rows:(j + 1) * rows]
    step = min(1024, out.shape[1])
    for n in range(out.shape[1] // step):
        columns = slice(n * step, (n + 1) * step)
        out[:, columns] = jnp.dot(mixed[...], weight[:, columns], preferred_element_type=F32).astype(BF16)


def limit(scratch):
    return pltpu.CompilerParams(vmem_limit_bytes=scratch + 24 * 1024 * 1024)


def attend_cache(lengths, query, cache, tokens):
    n_head, n_ctx = len(query), len(cache)
    rows, q_width = query[0].shape
    kv_width = cache[0].shape[1]
    groups = kv_width // (2 * HD)
    stacked = q_width // (groups * HD) * rows
    keys = n_ctx * tokens
    return pl.pallas_call(
        functools.partial(cache_kernel, n_ctx, n_head),
        out_shape=(
            jax.ShapeDtypeStruct((n_head, groups, stacked, 2 * HD), F32),
            jax.ShapeDtypeStruct((n_head, groups, stacked, LANES), F32),
        ),
        in_specs=[smem()] + [vmem()] * (n_head + n_ctx),
        out_specs=(vmem(), vmem()),
        scratch_shapes=[
            pltpu.VMEM((groups, stacked, keys), F32),
            pltpu.VMEM((n_ctx, tokens, LANES), BF16),
        ],
        compiler_params=limit(4 * groups * stacked * keys),
        cost_estimate=pl.CostEstimate(
            flops=16 * n_head * rows * q_width * keys,
            bytes_accessed=2 * keys * kv_width,
            transcendentals=n_head * rows * (q_width // HD) * keys,
        ),
    )(lengths, *query, *cache)


def attend_fresh(x, lengths, q, fresh, summed, tops, weight, n_head):
    n_ctx = len(fresh)
    rows, q_width = q.shape
    tokens, kv_width = fresh[0].shape
    groups = kv_width // (2 * HD)
    stacked = q_width // (groups * HD) * rows
    keys = n_ctx * tokens
    columns = weight.shape[1]
    return pl.pallas_call(
        functools.partial(fresh_kernel, x, n_ctx, n_head),
        out_shape=jax.ShapeDtypeStruct((rows, columns), BF16),
        in_specs=[smem()] + [vmem()] * (n_ctx + 4),
        out_specs=vmem(),
        scratch_shapes=[
            pltpu.VMEM((groups, stacked, keys), F32),
            pltpu.VMEM((n_ctx, tokens, LANES), BF16),
            pltpu.VMEM((rows, q_width), BF16),
        ],
        compiler_params=limit(4 * groups * stacked * keys),
        cost_estimate=pl.CostEstimate(
            flops=16 * rows * q_width * keys + 8 * rows * q_width * columns,
            bytes_accessed=2 * keys * kv_width,
            transcendentals=rows * (q_width // HD) * keys,
        ),
    )(lengths, q, *fresh, summed, tops, weight)


def swap(value, axis, mask):
    return lax.ppermute(value, axis, [(i, i ^ mask) for i in range(lax.axis_size(axis))])


def gather_ctx(block):
    n_ctx = lax.axis_size("ctx")
    blocks = [None] * n_ctx
    for m in range(0, n_ctx, 2):
        blocks[m] = swap(block, "ctx", m) if m else block
    for m in range(0, n_ctx, 2):
        blocks[m + 1] = swap(blocks[m], "ctx", 1)
    return blocks


def send(value, pairs):
    return lax.ppermute(value, "head", pairs)


def scatter_line(part, head):
    first = send(part(2), [(0, 1), (1, 3), (2, 0), (3, 2)])
    far = part(3)
    ends = send(far, [(0, 3), (3, 0)])
    near = send(part(1), [(0, 1), (1, 0), (2, 3), (3, 2)])
    inner = (head == 1) | (head == 2)
    joined = (far.astype(F32) + first.astype(F32)).astype(BF16)
    middle = send(joined, [(1, 2), (2, 1)])
    total = part(0).astype(F32) + near.astype(F32)
    return total + jnp.where(inner, middle.astype(F32), ends.astype(F32) + first.astype(F32))


def scatter_direct(part, n_head):
    total = None
    for x in [*range(n_head - 1, 0, -1), 0]:
        got = (swap(part(x), "head", x) if x else part(x)).astype(F32)
        total = got if total is None else total + got
    return total


def shards(queries, fresh_keys, fresh_values, cache_keys, cache_values, page_request, prompt_lengths, output_weight):
    n_head = lax.axis_size("head")
    rows = queries.shape[0]
    tokens = cache_keys.shape[0]
    kv_width = 2 * fresh_keys.shape[1] // n_head
    q_width = queries.shape[1] // n_head
    packed = pl.pallas_call(
        pack_kernel,
        out_shape=[jax.ShapeDtypeStruct((rows, kv_width), BF16)] * n_head
        + [jax.ShapeDtypeStruct((rows, q_width), BF16)] * n_head
        + [jax.ShapeDtypeStruct((tokens + tokens // PAGE, kv_width), BF16)],
        in_specs=[smem()] + [vmem()] * 5,
        out_specs=[vmem()] * (2 * n_head + 1),
    )(page_request, fresh_keys, fresh_values, queries, cache_keys, cache_values)
    fresh, query, cache = packed[:n_head], packed[n_head:2 * n_head], packed[-1]

    fresh = [swap(fresh[x], "head", x) if x else fresh[x] for x in range(n_head)]
    cache = gather_ctx(cache)
    query = [swap(query[x], "head", x) if x else query[x] for x in range(n_head)]
    fresh = gather_ctx(jnp.concatenate(fresh, axis=0))

    summed, tops = attend_cache(prompt_lengths, query, cache, tokens)
    part = lambda x: attend_fresh(x, prompt_lengths, query[x], fresh, summed, tops, output_weight, n_head)
    if n_head == 4:
        total = scatter_line(part, lax.axis_index("head"))
    else:
        total = scatter_direct(part, n_head)
    return total.astype(BF16)


def solution(mesh):
    placed = (
        P(("ctx", "head"), None),
        P(("ctx", "head"), None),
        P(("ctx", "head"), None),
        P("ctx", "head"),
        P("ctx", "head"),
        P("ctx"),
        P(),
        P("head", None),
    )
    return jax.shard_map(
        shards, mesh=mesh, in_specs=placed, out_specs=P(("ctx", "head"), None), check_vma=False
    )
```

time: 112 us -> 113 us (level); the launches traced: 112 us -> 111 us
  Pallas kernels: 42.9 us -> 27.5 us
  starting transfers between devices: 23.8 us -> 30.1 us
  waiting for transfers between devices: 34.2 us -> 40.1 us
  local copies, waits for them, and re-layouts: 7.2 us -> 9.6 us
  between operations: 1.49 us -> 0.21 us
  other arithmetic: 2.32 us -> 3.48 us
    pallas_call x7 -> x6, Pallas kernels: 42.9 us -> 27.5 us  [the longest x4 18.4 us: attend_fresh(): pl.pallas_call(functools.partial(fresh_kernel, x, n_ctx, n_head), out_sha...]
    ppermute x0 -> x4, waiting for transfers between devices: none -> 8.52 us  [send(): return lax.ppermute(value, 'head', pairs)]
    ppermute x0 -> x4, starting transfers between devices: none -> 8.03 us  [send(): return lax.ppermute(value, 'head', pairs)]
    unnamed x17 -> x31, local copies, waits for them, and re-layouts: 5.81 us -> 9.6 us
    ppermute x23 -> x20, waiting for transfers between devices: 34.2 us -> 31.6 us  [swap(): lax.ppermute(value, axis, [(i, i ^ mask) for i in range(lax.axis_size(axi...]
    ppermute x23 -> x20, starting transfers between devices: 23.8 us -> 22 us  [swap(): lax.ppermute(value, axis, [(i, i ^ mask) for i in range(lax.axis_size(axi...]
    convert_element_type x1, other arithmetic: 1.06 us -> 2.49 us  [shards(): return total.astype(BF16)]
    slice x1 -> x0, local copies, waits for them, and re-layouts: 1.38 us -> none  [shards(): prompt_lengths[i]]
  transfers between devices with their start and end apart: 23 -> 24, of which waited for: 8 -> 7; matrix products, arithmetic and copies ran while one was open for 3% -> 2% of each run, Pallas kernels for 37% -> 19%
where the time goes in v2:
time: 113 us; the launch traced here: 111 us
  waiting for transfers between devices  40.1 us (35%)
  starting transfers between devices  30.1 us (27%)
  Pallas kernels  27.5 us (24%)
  local copies, waits for them, and re-layouts  9.6 us (8%)
  other arithmetic  3.48 us (3%)
    ppermute x20, waiting for transfers between devices, swap(): lax.ppermute(value, axis, [(i, i ^ mask) for i in range(lax.axis_size(axi...  31.6 us
    ppermute x20, starting transfers between devices, swap(): lax.ppermute(value, axis, [(i, i ^ mask) for i in range(lax.axis_size(axi...  22 us
    pallas_call x4, Pallas kernels, attend_fresh(): pl.pallas_call(functools.partial(fresh_kernel, x, n_ctx, n_head), out_sha...  18.4 us
    unnamed x31, local copies, waits for them, and re-layouts  9.6 us
    ppermute x4, waiting for transfers between devices, send(): return lax.ppermute(value, 'head', pairs)  8.52 us
    ppermute x4, starting transfers between devices, send(): return lax.ppermute(value, 'head', pairs)  8.03 us
    pallas_call x1, Pallas kernels, attend_cache(): pl.pallas_call(functools.partial(cache_kernel, n_ctx, n_head), out_shape=...  6.81 us
    convert_element_type x1, other arithmetic, shards(): return total.astype(BF16)  2.49 us
  transfers between devices with their start and end apart: 24, of which 7 were waited for; matrix products, arithmetic and copies ran while one was open for 2% of the time, Pallas kernels for 19%

profile of v2, /device:TPU:0, one launch (start us, length us, event | category | flops | bytes accessed | tf_op | source)
XLA Modules:
  0.0 111.0 jit_solution(5377685280486699719)
XLA Ops:
  0.0 2.3 %shard_map.82 = (bf16[64,512]{1,0:T(8,128)(2,1)}, bf16[64,512]{1,0:T(8,128)(2,1)}, bf16[64,512]{1,0:T(8,128)(2,1)}, bf16[64,512]{1,0:T(8,128)(2,1)}, bf16[64,102...) custom-call(s32[16]{0:T(128)} %pages.1, ...), custom_call_target="tpu_custom_call" | custom-call | tf_op jit(solution)/shard_map/pallas_call | solution.py:279
  2.3 2.9 %collective-permute-start.14 = (bf16[272,512]{1,0:T(8,128)(2,1)}, bf16[272,512]{1,0:T(8,128)(2,1)S(1)}, u32[]{:S(2)}, u32[]{:S(2)}) collective-permute-start(bf16[272,512]{1,0:T(8,128)(2,1)} %get-tuple-element.24.refs_4_), channel_id=1, source_target_pairs={{0,8},{4,12},{8,0},{12,4},{16,24},{20,28},{24,16},{28,20},{1,9},{5... | collective-permute-start | bytes 835592 | tf_op jit(solution)/shard_map/ppermute | solution.py:236
  5.2 1.6 %collective-permute-start.10 = (bf16[64,1024]{1,0:T(8,128)(2,1)}, bf16[64,1024]{1,0:T(8,128)(2,1)S(1)}, u32[]{:S(2)}, u32[]{:S(2)}) collective-permute-start(bf16[64,1024]{1,0:T(8,128)(2,1)} %get-tuple-element.21), channel_id=1, source_target_pairs={{0,1},{1,0},{2,3},{3,2},{4,5},{5,4},{6,7},{7,6},{8,9},{9,8},{10,11... | collective-permute-start | bytes 393224 | tf_op jit(solution)/shard_map/ppermute | solution.py:236
  6.8 2.6 %collective-permute-start.11 = (bf16[64,1024]{1,0:T(8,128)(2,1)}, bf16[64,1024]{1,0:T(8,128)(2,1)S(1)}, u32[]{:S(2)}, u32[]{:S(2)}) collective-permute-start(bf16[64,1024]{1,0:T(8,128)(2,1)} %get-tuple-element.22), channel_id=1, source_target_pairs={{0,2},{1,3},{2,0},{3,1},{4,6},{5,7},{6,4},{7,5},{8,10},{9,11},{10,... | collective-permute-start | bytes 393224 | tf_op jit(solution)/shard_map/ppermute | solution.py:236
  9.4 0.2 collective-permute-start.12
  9.6 0.7 collective-permute-start
  10.3 0.8 constant_dynamic-update-slice_fusion.3
  11.2 5.5 %collective-permute-done = bf16[64,512]{1,0:T(8,128)(2,1)S(1)} collective-permute-done((bf16[64,512]{1,0:T(8,128)(2,1)}, bf16[64,512]{1,0:T(8,128)(2,1)S(1)}, u32[]{:S(2)}, u32[]{:S(2)}) %collective-permute-start) | collective-permute-done | bytes 65568 | tf_op jit(solution)/shard_map/ppermute | solution.py:236
  16.6 3.4 %collective-permute-start.1 = (bf16[64,512]{1,0:T(8,128)(2,1)}, bf16[64,512]{1,0:T(8,128)(2,1)S(1)}, u32[]{:S(2)}, u32[]{:S(2)}) collective-permute-start(bf16[64,512]{1,0:T(8,128)(2,1)} %get-tuple-element.19), channel_id=1, source_target_pairs={{0,2},{1,3},{2,0},{3,1},{4,6},{5,7},{6,4},{7,5},{8,10},{9,11},{10,... | collective-permute-start | bytes 196616 | tf_op jit(solution)/shard_map/ppermute | solution.py:236
  20.0 3.2 %collective-permute-done.1 = bf16[64,512]{1,0:T(8,128)(2,1)S(1)} collective-permute-done((bf16[64,512]{1,0:T(8,128)(2,1)}, bf16[64,512]{1,0:T(8,128)(2,1)S(1)}, u32[]{:S(2)}, u32[]{:S(2)}) %collective-permute-start.1) | collective-permute-done | bytes 65568 | tf_op jit(solution)/shard_map/ppermute | solution.py:236
  23.2 2.5 %collective-permute-start.2 = (bf16[64,512]{1,0:T(8,128)(2,1)}, bf16[64,512]{1,0:T(8,128)(2,1)S(1)}, u32[]{:S(2)}, u32[]{:S(2)}) collective-permute-start(bf16[64,512]{1,0:T(8,128)(2,1)} %get-tuple-element.20), channel_id=1, source_target_pairs={{0,3},{1,2},{2,1},{3,0},{4,7},{5,6},{6,5},{7,4},{8,11},{9,10},{10,... | collective-permute-start | bytes 196616 | tf_op jit(solution)/shard_map/ppermute | solution.py:236
  25.7 3.8 %collective-permute-done.2 = bf16[64,512]{1,0:T(8,128)(2,1)S(1)} collective-permute-done((bf16[64,512]{1,0:T(8,128)(2,1)}, bf16[64,512]{1,0:T(8,128)(2,1)S(1)}, u32[]{:S(2)}, u32[]{:S(2)}) %collective-permute-start.2) | collective-permute-done | bytes 65568 | tf_op jit(solution)/shard_map/ppermute | solution.py:236
  29.5 1.5 %collective-permute-start.16 = (bf16[272,512]{1,0:T(8,128)(2,1)}, bf16[272,512]{1,0:T(8,128)(2,1)S(1)}, u32[]{:S(2)}, u32[]{:S(2)}) collective-permute-start(bf16[272,512]{1,0:T(8,128)(2,1)} %get-tuple-element.24.refs_4_), channel_id=1, source_target_pairs={{0,16},{4,20},{8,24},{12,28},{16,0},{20,4},{24,8},{28,12},{1,17},{... | collective-permute-start | bytes 835592 | tf_op jit(solution)/shard_map/ppermute | solution.py:236
  31.0 0.0 collective-permute-done.10.refs_1_.q
  31.0 0.5 collective-permute-start.18
  31.5 0.0 collective-permute-done.11.refs_2_.q
  31.5 0.0 collective-permute-start.13
  31.5 0.0 collective-permute-done.12.refs_3_.q
  31.5 1.6 %collective-permute-start.4 = (bf16[256,512]{1,0:T(8,128)(2,1)S(1)}, bf16[256,512]{1,0:T(8,128)(2,1)S(1)}, u32[]{:S(2)}, u32[]{:S(2)}) collective-permute-start(bf16[256,512]{1,0:T(8,128)(2,1)S(1)} %constant_dynamic-update-slice_fusion.refs_0_), channel_id=1, source_target_pairs={{0,8},{4,12},{8,0},{12,4},{16,24},{20,28},{24,16},{28,20},{1,9},{5... | collective-permute-start | bytes 786440 | tf_op jit(solution)/shard_map/ppermute | solution.py:236
  33.1 0.0 collective-permute-done.14.refs_6_
  33.1 0.2 collective-permute-start.15
  33.3 7.9 %collective-permute-done.16.refs_8_ = bf16[272,512]{1,0:T(8,128)(2,1)S(1)} collective-permute-done((bf16[272,512]{1,0:T(8,128)(2,1)}, bf16[272,512]{1,0:T(8,128)(2,1)S(1)}, u32[]{:S(2)}, u32[]{:S(2)}) %collective-permute-start.16) | collective-permute-done | bytes 278560 | tf_op jit(solution)/shard_map/ppermute | solution.py:236
  41.2 0.0 collective-permute-start.17
  41.2 0.2 collective-permute-done.18.refs_10_
  41.4 0.3 collective-permute-start.19
  41.7 0.0 collective-permute-done.13.refs_5_
  41.7 1.7 %collective-permute-start.6 = (bf16[256,512]{1,0:T(8,128)(2,1)S(1)}, bf16[256,512]{1,0:T(8,128)(2,1)S(1)}, u32[]{:S(2)}, u32[]{:S(2)}) collective-permute-start(bf16[256,512]{1,0:T(8,128)(2,1)S(1)} %constant_dynamic-update-slice_fusion.refs_0_), channel_id=1, source_target_pairs={{0,16},{4,20},{8,24},{12,28},{16,0},{20,4},{24,8},{28,12},{1,17},{... | collective-permute-start | bytes 786440 | tf_op jit(solution)/shard_map/ppermute | solution.py:236
  43.5 0.0 collective-permute-done.4.refs_2_
  43.5 1.3 %collective-permute-start.8 = (bf16[256,512]{1,0:T(8,128)(2,1)S(1)}, bf16[256,512]{1,0:T(8,128)(2,1)S(1)}, u32[]{:S(2)}, u32[]{:S(2)}) collective-permute-start(bf16[256,512]{1,0:T(8,128)(2,1)S(1)} %constant_dynamic-update-slice_fusion.refs_0_), channel_id=1, source_target_pairs={{0,24},{4,28},{8,16},{12,20},{16,8},{20,12},{24,0},{28,4},{1,25},{... | collective-permute-start | bytes 786440 | tf_op jit(solution)/shard_map/ppermute | solution.py:236
  44.8 11.0 %collective-permute-done.6.refs_4_ = bf16[256,512]{1,0:T(8,128)(2,1)S(1)} collective-permute-done((bf16[256,512]{1,0:T(8,128)(2,1)S(1)}, bf16[256,512]{1,0:T(8,128)(2,1)S(1)}, u32[]{:S(2)}, u32[]{:S(2)}) %collective-permute-start.6) | collective-permute-done | bytes 262176 | tf_op jit(solution)/shard_map/ppermute | solution.py:236
  55.8 0.0 collective-permute-start.3
  55.8 0.0 collective-permute-done.8.refs_6_
  55.8 0.5 collective-permute-start.5
  56.3 0.0 collective-permute-done.15.refs_7_
  56.3 0.1 collective-permute-start.7
  56.4 0.0 collective-permute-done.17.refs_9_
  56.4 0.4 collective-permute-start.9
  56.8 0.0 collective-permute-done.19.refs_11_
  56.8 1.0 copy-done.1
  57.8 0.9 copy-done.2
  58.7 0.7 copy-done.4
  59.3 6.8 %shard_map.83 = (f32[4,2,256,256]{3,2,1,0:T(8,128)S(1)}, f32[4,2,256,128]{3,2,1,0:T(8,128)S(1)}) custom-call(s32[2]{0:T(128)S(1)} %copy-done.4, bf16[64,1024]{1,0:T(8,128)(2,1)S(1)} %copy-done.2, bf16[64,1024]{1,0:T(8,128)(2,1)S(1)} %collective-permute-done.10.refs_1_.q, bf16[64,1024]{1,0:T(8,128)(2,1)S(1)} %collective-permute-done.11.refs_2_.q, ...), custom_call_target="tpu_custom_call" | custom-call | flops 8589934592 | bytes 2097152 | tf_op jit(solution)/shard_map/pallas_call | solution.py:187
  66.2 0.0 collective-permute-done.3.refs_1_
  66.2 0.0 collective-permute-done.5.refs_3_
  66.2 0.0 collective-permute-done.7.refs_5_
  66.2 0.0 collective-permute-done.9.refs_7_
  66.2 4.6 %shard_map.87 = bf16[64,4096]{1,0:T(8,128)(2,1)S(1)} custom-call(s32[2]{0:T(128)S(1)} %copy-done.5, bf16[64,1024]{1,0:T(8,128)(2,1)S(1)} %collective-permute-done.11.refs_2_.q, bf16[256,512]{1,0:T(8,128)(2,1)S(1)} %constant_dynamic-update-slice_fusion.refs_0_, bf16[256,512]{1,0:T(8,128)(2,1)S(1)} %collective-permute-done.3.refs_1_, ...), custom_call_target="tpu_custom_call" | custom-call | flops 4294967296 | bytes 2097152 | tf_op jit(solution)/shard_map/pallas_call | solution.py:216
  70.9 0.2 collective-permute-start.21
  71.1 4.6 %shard_map.85 = bf16[64,4096]{1,0:T(8,128)(2,1)S(1)} custom-call(s32[2]{0:T(128)S(1)} %copy-done.5, bf16[64,1024]{1,0:T(8,128)(2,1)S(1)} %collective-permute-done.10.refs_1_.q, bf16[256,512]{1,0:T(8,128)(2,1)S(1)} %constant_dynamic-update-slice_fusion.refs_0_, bf16[256,512]{1,0:T(8,128)(2,1)S(1)} %collective-permute-done.3.refs_1_, ...), custom_call_target="tpu_custom_call" | custom-call | flops 4294967296 | bytes 2097152 | tf_op jit(solution)/shard_map/pallas_call | solution.py:216
  75.7 3.2 %collective-permute-start.20 = (bf16[64,4096]{1,0:T(8,128)(2,1)S(1)}, bf16[64,4096]{1,0:T(8,128)(2,1)}, u32[]{:S(2)}, u32[]{:S(2)}) collective-permute-start(bf16[64,4096]{1,0:T(8,128)(2,1)S(1)} %shard_map.85), channel_id=1, source_target_pairs={{0,1},{1,0},{2,3},{3,2},{4,5},{5,4},{6,7},{7,6},{8,9},{9,8},{10,11... | collective-permute-start | bytes 1572872 | tf_op jit(solution)/shard_map/ppermute | solution.py:250
  78.9 4.6 %shard_map.86 = bf16[64,4096]{1,0:T(8,128)(2,1)S(1)} custom-call(s32[2]{0:T(128)S(1)} %copy-done.5, bf16[64,1024]{1,0:T(8,128)(2,1)S(1)} %collective-permute-done.12.refs_3_.q, bf16[256,512]{1,0:T(8,128)(2,1)S(1)} %constant_dynamic-update-slice_fusion.refs_0_, bf16[256,512]{1,0:T(8,128)(2,1)S(1)} %collective-permute-done.3.refs_1_, ...), custom_call_target="tpu_custom_call" | custom-call | flops 4294967296 | bytes 2097152 | tf_op jit(solution)/shard_map/pallas_call | solution.py:216
  83.5 3.2 %collective-permute-start.23 = (bf16[64,4096]{1,0:T(8,128)(2,1)S(1)}, bf16[64,4096]{1,0:T(8,128)(2,1)}, u32[]{:S(2)}, u32[]{:S(2)}) collective-permute-start(bf16[64,4096]{1,0:T(8,128)(2,1)S(1)} %shard_map.86), channel_id=1, source_target_pairs={{0,3},{3,0},{4,7},{7,4},{8,11},{11,8},{12,15},{15,12},{16,19},{19,... | collective-permute-start | bytes 1572872 | tf_op jit(solution)/shard_map/ppermute | solution.py:250
  86.7 0.0 collective-permute-done.21
  86.7 0.0 copy-start.10
  86.7 1.0 fusion
  87.7 1.5 %collective-permute-start.22 = (bf16[64,4096]{1,0:T(8,128)(2,1)}, bf16[64,4096]{1,0:T(8,128)(2,1)}, u32[]{:S(2)}, u32[]{:S(2)}) collective-permute-start(bf16[64,4096]{1,0:T(8,128)(2,1)} %fusion), channel_id=1, source_target_pairs={{1,2},{2,1},{5,6},{6,5},{9,10},{10,9},{13,14},{14,13},{17,18},{18,... | collective-permute-start | bytes 1572872 | tf_op jit(solution)/shard_map/ppermute | solution.py:250
  89.1 3.4 %copy-done = bf16[1024,4096]{1,0:T(8,128)(2,1)S(1)} copy-done((bf16[1024,4096]{1,0:T(8,128)(2,1)S(1)}, bf16[1024,4096]{1,0:T(8,128)(2,1)}, u32[]{:S(2)}) %copy-start) | copy-done | bytes 8388632
  92.5 1.6 %copy-done.7 = f32[4,2,256,256]{3,2,1,0:T(8,128)S(1)} copy-done((f32[4,2,256,256]{3,2,1,0:T(8,128)S(1)}, f32[4,2,256,256]{3,2,1,0:T(8,128)}, u32[]{:S(2)}) %copy-start.7) | copy-done | bytes 2097176
  94.1 1.2 %copy-done.9 = f32[4,2,256,128]{3,2,1,0:T(8,128)S(1)} copy-done((f32[4,2,256,128]{3,2,1,0:T(8,128)S(1)}, f32[4,2,256,128]{3,2,1,0:T(8,128)}, u32[]{:S(2)}) %copy-start.9) | copy-done | bytes 1048600
  95.3 4.6 %shard_map.84 = bf16[64,4096]{1,0:T(8,128)(2,1)S(1)} custom-call(s32[2]{0:T(128)S(1)} %copy-done.5, bf16[64,1024]{1,0:T(8,128)(2,1)S(1)} %copy-done.3, bf16[256,512]{1,0:T(8,128)(2,1)S(1)} %constant_dynamic-update-slice_fusion.refs_0_, bf16[256,512]{1,0:T(8,128)(2,1)S(1)} %collective-permute-done.3.refs_1_, ...), custom_call_target="tpu_custom_call" | custom-call | flops 4294967296 | bytes 2097152 | tf_op jit(solution)/shard_map/pallas_call | solution.py:216
  100.0 0.0 collective-permute-done.20
  100.0 8.5 %collective-permute-done.23 = bf16[64,4096]{1,0:T(8,128)(2,1)} collective-permute-done((bf16[64,4096]{1,0:T(8,128)(2,1)S(1)}, bf16[64,4096]{1,0:T(8,128)(2,1)}, u32[]{:S(2)}, u32[]{:S(2)}) %collective-permute-start.23) | collective-permute-done | bytes 524320 | tf_op jit(solution)/shard_map/ppermute | solution.py:250
  108.5 0.0 collective-permute-done.22
  108.5 2.5 %fusion.3 = bf16[64,4096]{1,0:T(8,128)(2,1)} fusion(bf16[64,4096]{1,0:T(8,128)(2,1)S(1)} %copy-done.11, bf16[64,4096]{1,0:T(8,128)(2,1)} %collective-permute-done.23, bf16[64,4096]{1,0:T(8,128)(2,1)} %collective-permute-done.22, bf16[64,4096]{1,0:T(8,128)(2,1)} %collective-permute-done.20, bf16[64,4096]{1,0:T(8,128)(2,1)S(1)} %shard_map.84, pred[]{:T(512)S(6)} %or.3), kind=kLoop, calls=%fused_computation.5 | loop fusion | flops 2621440 | bytes 3145729 | tf_op jit(solution)/shard_map/convert_element_type | solution.py:300
  (25 shorter events, 0.1 us)
Async XLA Ops:
  2.3 30.8 %collective-permute-start.14 = (bf16[272,512]{1,0:T(8,128)(2,1)}, bf16[272,512]{1,0:T(8,128)(2,1)S(1)}, u32[]{:S(2)}, u32[]{:S(2)}) collective-permute-start(bf16[272,512]{1,0:T(8,128)(2,1)} %get-tuple-element.24.refs_4_), channel_id=1, source_target_pairs={{0,8},{4,12},{8,0},{12,4},{16,24},{20,28},{24,16},{28,20},{1,9},{5... | collective-permute-start | bytes 835592 | tf_op jit(solution)/shard_map/ppermute | solution.py:236
  5.2 25.8 %collective-permute-start.10 = (bf16[64,1024]{1,0:T(8,128)(2,1)}, bf16[64,1024]{1,0:T(8,128)(2,1)S(1)}, u32[]{:S(2)}, u32[]{:S(2)}) collective-permute-start(bf16[64,1024]{1,0:T(8,128)(2,1)} %get-tuple-element.21), channel_id=1, source_target_pairs={{0,1},{1,0},{2,3},{3,2},{4,5},{5,4},{6,7},{7,6},{8,9},{9,8},{10,11... | collective-permute-start | bytes 393224 | tf_op jit(solution)/shard_map/ppermute | solution.py:236
  6.8 24.7 %collective-permute-start.11 = (bf16[64,1024]{1,0:T(8,128)(2,1)}, bf16[64,1024]{1,0:T(8,128)(2,1)S(1)}, u32[]{:S(2)}, u32[]{:S(2)}) collective-permute-start(bf16[64,1024]{1,0:T(8,128)(2,1)} %get-tuple-element.22), channel_id=1, source_target_pairs={{0,2},{1,3},{2,0},{3,1},{4,6},{5,7},{6,4},{7,5},{8,10},{9,11},{10,... | collective-permute-start | bytes 393224 | tf_op jit(solution)/shard_map/ppermute | solution.py:236
  9.4 22.1 %collective-permute-start.12 = (bf16[64,1024]{1,0:T(8,128)(2,1)}, bf16[64,1024]{1,0:T(8,128)(2,1)S(1)}, u32[]{:S(2)}, u32[]{:S(2)}) collective-permute-start(bf16[64,1024]{1,0:T(8,128)(2,1)} %get-tuple-element.23), channel_id=1, source_target_pairs={{0,3},{1,2},{2,1},{3,0},{4,7},{5,6},{6,5},{7,4},{8,11},{9,10},{10,... | collective-permute-start | bytes 393224 | tf_op jit(solution)/shard_map/ppermute | solution.py:236
  9.6 7.0 %collective-permute-start = (bf16[64,512]{1,0:T(8,128)(2,1)}, bf16[64,512]{1,0:T(8,128)(2,1)S(1)}, u32[]{:S(2)}, u32[]{:S(2)}) collective-permute-start(bf16[64,512]{1,0:T(8,128)(2,1)} %get-tuple-element.18), channel_id=1, source_target_pairs={{0,1},{1,0},{2,3},{3,2},{4,5},{5,4},{6,7},{7,6},{8,9},{9,8},{10,11... | collective-permute-start | bytes 196616 | tf_op jit(solution)/shard_map/ppermute | solution.py:236
  16.6 6.6 %collective-permute-start.1 = (bf16[64,512]{1,0:T(8,128)(2,1)}, bf16[64,512]{1,0:T(8,128)(2,1)S(1)}, u32[]{:S(2)}, u32[]{:S(2)}) collective-permute-start(bf16[64,512]{1,0:T(8,128)(2,1)} %get-tuple-element.19), channel_id=1, source_target_pairs={{0,2},{1,3},{2,0},{3,1},{4,6},{5,7},{6,4},{7,5},{8,10},{9,11},{10,... | collective-permute-start | bytes 196616 | tf_op jit(solution)/shard_map/ppermute | solution.py:236
  20.0 46.2 %slice-start = ((s8[8388608]{0:T(1024)(128)(4,1)}), s8[4194304]{0:T(1024)(128)(4,1)S(1)}, s32[]{:S(2)}) async-start(s8[8388608]{0:T(1024)(128)(4,1)} %bitcast), calls=%async_computation | async-start | bytes 8388608
  23.2 6.3 %collective-permute-start.2 = (bf16[64,512]{1,0:T(8,128)(2,1)}, bf16[64,512]{1,0:T(8,128)(2,1)S(1)}, u32[]{:S(2)}, u32[]{:S(2)}) collective-permute-start(bf16[64,512]{1,0:T(8,128)(2,1)} %get-tuple-element.20), channel_id=1, source_target_pairs={{0,3},{1,2},{2,1},{3,0},{4,7},{5,6},{6,5},{7,4},{8,11},{9,10},{10,... | collective-permute-start | bytes 196616 | tf_op jit(solution)/shard_map/ppermute | solution.py:236
  29.5 11.7 %collective-permute-start.16 = (bf16[272,512]{1,0:T(8,128)(2,1)}, bf16[272,512]{1,0:T(8,128)(2,1)S(1)}, u32[]{:S(2)}, u32[]{:S(2)}) collective-permute-start(bf16[272,512]{1,0:T(8,128)(2,1)} %get-tuple-element.24.refs_4_), channel_id=1, source_target_pairs={{0,16},{4,20},{8,24},{12,28},{16,0},{20,4},{24,8},{28,12},{1,17},{... | collective-permute-start | bytes 835592 | tf_op jit(solution)/shard_map/ppermute | solution.py:236
  31.0 10.4 %collective-permute-start.18 = (bf16[272,512]{1,0:T(8,128)(2,1)}, bf16[272,512]{1,0:T(8,128)(2,1)S(1)}, u32[]{:S(2)}, u32[]{:S(2)}) collective-permute-start(bf16[272,512]{1,0:T(8,128)(2,1)} %get-tuple-element.24.refs_4_), channel_id=1, source_target_pairs={{0,24},{4,28},{8,16},{12,20},{16,8},{20,12},{24,0},{28,4},{1,25},{... | collective-permute-start | bytes 835592 | tf_op jit(solution)/shard_map/ppermute | solution.py:236
  31.5 10.2 %collective-permute-start.13 = (bf16[272,512]{1,0:T(8,128)(2,1)}, bf16[272,512]{1,0:T(8,128)(2,1)S(1)}, u32[]{:S(2)}, u32[]{:S(2)}) collective-permute-start(bf16[272,512]{1,0:T(8,128)(2,1)} %get-tuple-element.24.refs_4_), channel_id=1, source_target_pairs={{0,4},{4,0},{8,12},{12,8},{16,20},{20,16},{24,28},{28,24},{1,5},{5... | collective-permute-start | bytes 835592 | tf_op jit(solution)/shard_map/ppermute | solution.py:236
  31.5 12.0 %collective-permute-start.4 = (bf16[256,512]{1,0:T(8,128)(2,1)S(1)}, bf16[256,512]{1,0:T(8,128)(2,1)S(1)}, u32[]{:S(2)}, u32[]{:S(2)}) collective-permute-start(bf16[256,512]{1,0:T(8,128)(2,1)S(1)} %constant_dynamic-update-slice_fusion.refs_0_), channel_id=1, source_target_pairs={{0,8},{4,12},{8,0},{12,4},{16,24},{20,28},{24,16},{28,20},{1,9},{5... | collective-permute-start | bytes 786440 | tf_op jit(solution)/shard_map/ppermute | solution.py:236
  33.1 23.2 %collective-permute-start.15 = (bf16[272,512]{1,0:T(8,128)(2,1)S(1)}, bf16[272,512]{1,0:T(8,128)(2,1)S(1)}, u32[]{:S(2)}, u32[]{:S(2)}) collective-permute-start(bf16[272,512]{1,0:T(8,128)(2,1)S(1)} %collective-permute-done.14.refs_6_), channel_id=1, source_target_pairs={{0,4},{4,0},{8,12},{12,8},{16,20},{20,16},{24,28},{28,24},{1,5},{5... | collective-permute-start | bytes 835592 | tf_op jit(solution)/shard_map/ppermute | solution.py:236
  41.2 15.2 %collective-permute-start.17 = (bf16[272,512]{1,0:T(8,128)(2,1)S(1)}, bf16[272,512]{1,0:T(8,128)(2,1)S(1)}, u32[]{:S(2)}, u32[]{:S(2)}) collective-permute-start(bf16[272,512]{1,0:T(8,128)(2,1)S(1)} %collective-permute-done.16.refs_8_), channel_id=1, source_target_pairs={{0,4},{4,0},{8,12},{12,8},{16,20},{20,16},{24,28},{28,24},{1,5},{5... | collective-permute-start | bytes 835592 | tf_op jit(solution)/shard_map/ppermute | solution.py:236
  41.4 15.4 %collective-permute-start.19 = (bf16[272,512]{1,0:T(8,128)(2,1)S(1)}, bf16[272,512]{1,0:T(8,128)(2,1)S(1)}, u32[]{:S(2)}, u32[]{:S(2)}) collective-permute-start(bf16[272,512]{1,0:T(8,128)(2,1)S(1)} %collective-permute-done.18.refs_10_), channel_id=1, source_target_pairs={{0,4},{4,0},{8,12},{12,8},{16,20},{20,16},{24,28},{28,24},{1,5},{5... | collective-permute-start | bytes 835592 | tf_op jit(solution)/shard_map/ppermute | solution.py:236
  41.7 14.0 %collective-permute-start.6 = (bf16[256,512]{1,0:T(8,128)(2,1)S(1)}, bf16[256,512]{1,0:T(8,128)(2,1)S(1)}, u32[]{:S(2)}, u32[]{:S(2)}) collective-permute-start(bf16[256,512]{1,0:T(8,128)(2,1)S(1)} %constant_dynamic-update-slice_fusion.refs_0_), channel_id=1, source_target_pairs={{0,16},{4,20},{8,24},{12,28},{16,0},{20,4},{24,8},{28,12},{1,17},{... | collective-permute-start | bytes 786440 | tf_op jit(solution)/shard_map/ppermute | solution.py:236
  43.5 12.3 %collective-permute-start.8 = (bf16[256,512]{1,0:T(8,128)(2,1)S(1)}, bf16[256,512]{1,0:T(8,128)(2,1)S(1)}, u32[]{:S(2)}, u32[]{:S(2)}) collective-permute-start(bf16[256,512]{1,0:T(8,128)(2,1)S(1)} %constant_dynamic-update-slice_fusion.refs_0_), channel_id=1, source_target_pairs={{0,24},{4,28},{8,16},{12,20},{16,8},{20,12},{24,0},{28,4},{1,25},{... | collective-permute-start | bytes 786440 | tf_op jit(solution)/shard_map/ppermute | solution.py:236
  55.8 10.4 %collective-permute-start.3 = (bf16[256,512]{1,0:T(8,128)(2,1)S(1)}, bf16[256,512]{1,0:T(8,128)(2,1)S(1)}, u32[]{:S(2)}, u32[]{:S(2)}) collective-permute-start(bf16[256,512]{1,0:T(8,128)(2,1)S(1)} %constant_dynamic-update-slice_fusion.refs_0_), channel_id=1, source_target_pairs={{0,4},{4,0},{8,12},{12,8},{16,20},{20,16},{24,28},{28,24},{1,5},{5... | collective-permute-start | bytes 786440 | tf_op jit(solution)/shard_map/ppermute | solution.py:236
  55.8 10.4 %collective-permute-start.5 = (bf16[256,512]{1,0:T(8,128)(2,1)S(1)}, bf16[256,512]{1,0:T(8,128)(2,1)S(1)}, u32[]{:S(2)}, u32[]{:S(2)}) collective-permute-start(bf16[256,512]{1,0:T(8,128)(2,1)S(1)} %collective-permute-done.4.refs_2_), channel_id=1, source_target_pairs={{0,4},{4,0},{8,12},{12,8},{16,20},{20,16},{24,28},{28,24},{1,5},{5... | collective-permute-start | bytes 786440 | tf_op jit(solution)/shard_map/ppermute | solution.py:236
  56.3 9.9 %collective-permute-start.7 = (bf16[256,512]{1,0:T(8,128)(2,1)S(1)}, bf16[256,512]{1,0:T(8,128)(2,1)S(1)}, u32[]{:S(2)}, u32[]{:S(2)}) collective-permute-start(bf16[256,512]{1,0:T(8,128)(2,1)S(1)} %collective-permute-done.6.refs_4_), channel_id=1, source_target_pairs={{0,4},{4,0},{8,12},{12,8},{16,20},{20,16},{24,28},{28,24},{1,5},{5... | collective-permute-start | bytes 786440 | tf_op jit(solution)/shard_map/ppermute | solution.py:236
  56.4 9.8 %collective-permute-start.9 = (bf16[256,512]{1,0:T(8,128)(2,1)S(1)}, bf16[256,512]{1,0:T(8,128)(2,1)S(1)}, u32[]{:S(2)}, u32[]{:S(2)}) collective-permute-start(bf16[256,512]{1,0:T(8,128)(2,1)S(1)} %collective-permute-done.8.refs_6_), channel_id=1, source_target_pairs={{0,4},{4,0},{8,12},{12,8},{16,20},{20,16},{24,28},{28,24},{1,5},{5... | collective-permute-start | bytes 786440 | tf_op jit(solution)/shard_map/ppermute | solution.py:236
  56.8 1.0 copy-start.1
  57.8 0.9 copy-start.2
  58.7 0.7 copy-start.4
  59.3 6.9 %slice-start.1 = ((s8[8388608]{0:T(1024)(128)(4,1)}), s8[4194304]{0:T(1024)(128)(4,1)S(1)}, s32[]{:S(2)}) async-start(s8[8388608]{0:T(1024)(128)(4,1)} %bitcast), calls=%async_computation.1 | async-start | bytes 8388608
  59.3 6.9 %copy-start.5 = (s32[2]{0:T(128)S(1)}, s32[2]{0:T(128)}, u32[]{:S(2)}) copy-start(s32[2]{0:T(128)} %lengths.9) | copy-start | bytes 28
  66.1 12.8 %copy-start.6 = (f32[4,2,256,256]{3,2,1,0:T(8,128)}, f32[4,2,256,256]{3,2,1,0:T(8,128)S(1)}, u32[]{:S(2)}) copy-start(f32[4,2,256,256]{3,2,1,0:T(8,128)S(1)} %get-tuple-element.25.refs_8_) | copy-start | bytes 6291460
  66.2 12.8 %copy-start.8 = (f32[4,2,256,128]{3,2,1,0:T(8,128)}, f32[4,2,256,128]{3,2,1,0:T(8,128)S(1)}, u32[]{:S(2)}) copy-start(f32[4,2,256,128]{3,2,1,0:T(8,128)S(1)} %get-tuple-element.26.refs_9_) | copy-start | bytes 3145732
  70.9 15.8 %collective-permute-start.21 = (bf16[64,4096]{1,0:T(8,128)(2,1)S(1)}, bf16[64,4096]{1,0:T(8,128)(2,1)S(1)}, u32[]{:S(2)}, u32[]{:S(2)}) collective-permute-start(bf16[64,4096]{1,0:T(8,128)(2,1)S(1)} %shard_map.87), channel_id=1, source_target_pairs={{0,1},{1,3},{2,0},{3,2},{4,5},{5,7},{6,4},{7,6},{8,9},{9,11},{10,8... | collective-permute-start | bytes 1572872 | tf_op jit(solution)/shard_map/ppermute | solution.py:250
  75.7 13.4 %copy-start.3 = (bf16[64,1024]{1,0:T(8,128)(2,1)S(1)}, bf16[64,1024]{1,0:T(8,128)(2,1)}, u32[]{:S(2)}) copy-start(bf16[64,1024]{1,0:T(8,128)(2,1)} %get-tuple-element.16.refs_0_.q) | copy-start | bytes 393220
  75.7 24.2 %collective-permute-start.20 = (bf16[64,4096]{1,0:T(8,128)(2,1)S(1)}, bf16[64,4096]{1,0:T(8,128)(2,1)}, u32[]{:S(2)}, u32[]{:S(2)}) collective-permute-start(bf16[64,4096]{1,0:T(8,128)(2,1)S(1)} %shard_map.85), channel_id=1, source_target_pairs={{0,1},{1,0},{2,3},{3,2},{4,5},{5,4},{6,7},{7,6},{8,9},{9,8},{10,11... | collective-permute-start | bytes 1572872 | tf_op jit(solution)/shard_map/ppermute | solution.py:250
  83.5 25.0 %collective-permute-start.23 = (bf16[64,4096]{1,0:T(8,128)(2,1)S(1)}, bf16[64,4096]{1,0:T(8,128)(2,1)}, u32[]{:S(2)}, u32[]{:S(2)}) collective-permute-start(bf16[64,4096]{1,0:T(8,128)(2,1)S(1)} %shard_map.86), channel_id=1, source_target_pairs={{0,3},{3,0},{4,7},{7,4},{8,11},{11,8},{12,15},{15,12},{16,19},{19,... | collective-permute-start | bytes 1572872 | tf_op jit(solution)/shard_map/ppermute | solution.py:250
  86.7 1.0 copy-start.10
  87.7 20.8 %collective-permute-start.22 = (bf16[64,4096]{1,0:T(8,128)(2,1)}, bf16[64,4096]{1,0:T(8,128)(2,1)}, u32[]{:S(2)}, u32[]{:S(2)}) collective-permute-start(bf16[64,4096]{1,0:T(8,128)(2,1)} %fusion), channel_id=1, source_target_pairs={{1,2},{2,1},{5,6},{6,5},{9,10},{10,9},{13,14},{14,13},{17,18},{18,... | collective-permute-start | bytes 1572872 | tf_op jit(solution)/shard_map/ppermute | solution.py:250
  89.1 3.4 %copy-start = (bf16[1024,4096]{1,0:T(8,128)(2,1)S(1)}, bf16[1024,4096]{1,0:T(8,128)(2,1)}, u32[]{:S(2)}) copy-start(bf16[1024,4096]{1,0:T(8,128)(2,1)} %refs_10_.7) | copy-start | bytes 25165828
  92.5 1.6 %copy-start.7 = (f32[4,2,256,256]{3,2,1,0:T(8,128)S(1)}, f32[4,2,256,256]{3,2,1,0:T(8,128)}, u32[]{:S(2)}) copy-start(f32[4,2,256,256]{3,2,1,0:T(8,128)} %copy-done.6) | copy-start | bytes 6291460
  94.1 1.2 %copy-start.9 = (f32[4,2,256,128]{3,2,1,0:T(8,128)S(1)}, f32[4,2,256,128]{3,2,1,0:T(8,128)}, u32[]{:S(2)}) copy-start(f32[4,2,256,128]{3,2,1,0:T(8,128)} %copy-done.8) | copy-start | bytes 3145732
  95.3 13.2 %copy-start.11 = (bf16[64,4096]{1,0:T(8,128)(2,1)S(1)}, bf16[64,4096]{1,0:T(8,128)(2,1)}, u32[]{:S(2)}) copy-start(bf16[64,4096]{1,0:T(8,128)(2,1)} %copy-done.10) | copy-start | bytes 1572868

commit v3 on v2

v3 whole, which is shorter than its diff:
```python
import functools
import math

import jax
import jax.numpy as jnp
from jax import lax
from jax.experimental import pallas as pl
from jax.experimental.pallas import tpu as pltpu
from jax.sharding import PartitionSpec as P

HD = 128
PAGE = 16
LANES = 128
HIDDEN = -1e30
MIB = 1024 * 1024
BF16 = jnp.bfloat16
F32 = jnp.float32


def iota(shape, dim):
    return lax.broadcasted_iota(jnp.int32, shape, dim)


def shaped(rows, columns, dtype=BF16):
    return jax.ShapeDtypeStruct((rows, columns), dtype)


def call(kernel, outs, ins, after=(), scratch=(), room=6 * MIB, cost=None):
    count = len(ins)

    def body(*refs):
        kernel(*refs[:count], *refs[count + len(after):])

    integers = lambda a: a.ndim == 1 and a.dtype == jnp.int32
    specs = [pl.BlockSpec(memory_space=pltpu.SMEM if integers(a) else pltpu.VMEM) for a in ins]
    return pl.pallas_call(
        body,
        out_shape=outs,
        in_specs=specs + [pl.BlockSpec(memory_space=pl.ANY)] * len(after),
        out_specs=[pl.BlockSpec(memory_space=pltpu.VMEM)] * len(outs),
        scratch_shapes=list(scratch),
        compiler_params=pltpu.CompilerParams(vmem_limit_bytes=room),
        cost_estimate=cost,
    )(*ins, *after)


def part_of(ref, index, count):
    width = ref.shape[1] // count
    return ref[:, pl.ds(pl.multiple_of(index * width, width), width)]


def pack_kernel(pages, k_ref, v_ref, ck_ref, cv_ref, *outs):
    *fresh, cache = outs
    head = lax.axis_index("head")
    tokens, width = ck_ref.shape
    for x, out in enumerate(fresh):
        out[:, :width] = part_of(k_ref, head ^ x, len(fresh))
        out[:, width:] = part_of(v_ref, head ^ x, len(fresh))
    cache[:tokens, :width] = ck_ref[...]
    cache[:tokens, width:] = cv_ref[...]
    count = pages.shape[0]
    page = iota((count, 2 * width), 0)
    owner = jnp.zeros((count, 2 * width), jnp.int32)
    for p in range(count):
        owner = jnp.where(page == p, pages[p], owner)
    cache[tokens:, :] = owner.astype(F32).astype(BF16)


def stage_kernel(lengths, q_ref, fresh_ref, cache_ref, fresh, cache, ends, *query):
    head = lax.axis_index("head")
    for x, out in enumerate(query):
        out[...] = part_of(q_ref, head ^ x, len(query))
    fresh[...] = fresh_ref[...]
    cache[...] = cache_ref[...]
    row = iota(ends.shape, 0)
    end, filled = 0, jnp.zeros(ends.shape, jnp.int32)
    for r in range(lengths.shape[0]):
        end = end + lengths[r]
        filled = jnp.where(row == r, end, filled)
    ends[...] = filled


def stack_kernel(*refs):
    out, rows = refs[-1], refs[0].shape[0]
    for i, ref in enumerate(refs[:-1]):
        out[i * rows:(i + 1) * rows, :] = ref[...]


class Layout:
    def __init__(self, ends, rows, q_width, kv_width, n_ctx, n_head):
        self.rows, self.n_ctx, self.n_head = rows, n_ctx, n_head
        self.groups = kv_width // (2 * HD)
        self.repeat = q_width // (self.groups * HD)
        self.half = n_head * rows // 2
        self.c, self.h = lax.axis_index("ctx"), lax.axis_index("head")
        self.ends = [ends[r:r + 1, :] for r in range(ends.shape[0])]
        self.lane = iota((rows, LANES), 1)
        self.row = iota((rows, LANES), 0)
        self.row_lane = self.lane - (LANES - rows)

    def start_of(self, rank, head):
        first = head * self.rows < self.half
        piece = jnp.where(first, rank, 2 * self.n_ctx - 1 - rank)
        return piece * self.half + lax.rem(head * self.rows, self.half)

    def step_of(self, b):
        if self.n_ctx != 8:
            return b
        near = jnp.where(lax.rem(self.c, 2) == 0, 2, 4)
        return [0, near, 6 - near, 6, 1, 7 - near, 1 + near, 7][b]

    def request(self, position):
        request = jnp.zeros(position.shape, jnp.int32)
        for end in self.ends:
            request += (position >= end).astype(jnp.int32)
        return request

    def query_rows(self, query, x):
        q = query[...]
        own = self.lane == self.request(self.start_of(self.c, self.h ^ x) + self.row)
        mask = jnp.where(own | (self.row_lane == self.row), 1.0, 0.0).astype(BF16)
        result = []
        for g in range(self.groups):
            heads = [
                jnp.concatenate([q[:, n * HD:(n + 1) * HD], mask], axis=1)
                for n in range(g * self.repeat, (g + 1) * self.repeat)
            ]
            result.append(jnp.concatenate(heads, axis=0))
        return result

    def fresh_mask(self, b, head):
        p0 = self.start_of(self.c, head)
        parts = []
        for x in range(self.n_head):
            position = self.start_of(self.c ^ self.step_of(b), self.h ^ x) + self.row
            other = (self.lane < len(self.ends)) & (self.request(position) != self.lane)
            later = (self.row_lane >= 0) & (position > p0 + self.row_lane)
            parts.append(jnp.where(other | later, HIDDEN, 0.0))
        return jnp.concatenate(parts, axis=0).astype(BF16)

    def cache_mask(self, owner):
        pages = owner.shape[0]
        lane = iota((pages, LANES), 1)
        other = (lane < len(self.ends)) & (owner.astype(F32) != lane.astype(F32))
        bias = jnp.where(other, HIDDEN, 0.0)
        bias = jnp.broadcast_to(bias[:, None, :], (pages, PAGE, LANES))
        return bias.reshape(pages * PAGE, LANES).astype(BF16)


def attend(q_rows, blocks, masks, scores, tokens, g, groups):
    scale = math.log2(math.e) / math.sqrt(HD)
    largest = None
    for b, (block, mask) in enumerate(zip(blocks, masks)):
        keys = jnp.concatenate([block[:tokens, g * HD:(g + 1) * HD], mask[...]], axis=1)
        s = lax.dot_general(q_rows, keys, (((1,), (1,)), ((), ())), preferred_element_type=F32)
        scores[:, b * tokens:(b + 1) * tokens] = s
        for t in range(tokens // LANES):
            part = s[:, t * LANES:(t + 1) * LANES]
            largest = part if largest is None else jnp.maximum(largest, part)
    top = jnp.max(largest, axis=1, keepdims=True) * scale
    ones = jnp.ones((tokens, HD), BF16)
    summed = jnp.zeros((q_rows.shape[0], 2 * HD), F32)
    for b, block in enumerate(blocks):
        weights = jnp.exp2(scores[:, b * tokens:(b + 1) * tokens] * scale - top).astype(BF16)
        values = jnp.concatenate([block[:tokens, (groups + g) * HD:(groups + g + 1) * HD], ones], axis=1)
        summed += jnp.dot(weights, values, preferred_element_type=F32)
    return summed, jnp.broadcast_to(top, (q_rows.shape[0], LANES))


def views(refs, tokens):
    return [ref.at[pl.ds(i, tokens)] for ref in refs for i in range(0, ref.shape[0], tokens)]


def cache_kernel(xs, count, n_ctx, n_head, q_width, ends, *refs):
    query, refs = refs[:len(xs)], refs[len(xs):]
    outs, (scores, masks) = refs[count:-2], refs[-2:]
    tokens = masks.shape[1]
    cache = views(refs[:count], tokens + tokens // PAGE)
    at = Layout(ends, query[0].shape[0], q_width, cache[0].shape[1], n_ctx, n_head)
    for b in range(n_ctx):
        masks[b] = at.cache_mask(cache[b][tokens:, :LANES])
    for i, x in enumerate(xs):
        summed, tops = outs[2 * i:2 * i + 2]
        q_rows = at.query_rows(query[i], x)
        for g in range(at.groups):
            summed[g], tops[g] = attend(
                q_rows[g], cache, [masks.at[b] for b in range(n_ctx)], scores.at[g], tokens, g, at.groups
            )


def fresh_kernel(xs, count, n_ctx, n_head, q_width, ends, *refs):
    query, refs = refs[:len(xs)], refs[len(xs):]
    fresh, state, refs = refs[:count], refs[count:count + 2 * len(xs)], refs[count + 2 * len(xs):]
    weight, outs, (scores, masks, mixed) = refs[0], refs[1:-3], refs[-3:]
    rows, tokens = query[0].shape[0], masks.shape[1]
    fresh = views(fresh, tokens)
    at = Layout(ends, rows, q_width, fresh[0].shape[1], n_ctx, n_head)
    for i, x in enumerate(xs):
        summed, tops = state[2 * i:2 * i + 2]
        for b in range(n_ctx):
            masks[b] = at.fresh_mask(b, at.h ^ x)
        q_rows = at.query_rows(query[i], x)
        for g in range(at.groups):
            sum_b, top_b = attend(
                q_rows[g], fresh, [masks.at[b] for b in range(n_ctx)], scores.at[g], tokens, g, at.groups
            )
            top = jnp.maximum(tops[g], top_b)
            factor_a, factor_b = jnp.exp2(tops[g] - top), jnp.exp2(top_b - top)
            value = summed[g, :, :HD] * factor_a + sum_b[:, :HD] * factor_b
            total = summed[g, :, HD:] * factor_a + sum_b[:, HD:] * factor_b
            attended = (value / total).astype(BF16)
            for j in range(at.repeat):
                n = g * at.repeat + j
                mixed[i * rows:(i + 1) * rows, n * HD:(n + 1) * HD] = attended[j * rows:(j + 1) * rows]
    width = outs[0].shape[1]
    step = min(1024, width)
    for n in range(width // step):
        columns = slice(n * step, (n + 1) * step)
        y = jnp.dot(mixed[...], weight[:, columns], preferred_element_type=F32).astype(BF16)
        for i, out in enumerate(outs):
            out[:, columns] = y[i * rows:(i + 1) * rows]


def add_kernel(count, *refs):
    out, rest = refs[-1], refs[count:-1]
    total = refs[0][...].astype(F32)
    for ref in refs[1:count]:
        total += ref[...].astype(F32)
    out[...] = total.astype(BF16)
    for ref in rest:
        head = lax.axis_index("head")

        @pl.when((head == 0) | (head == lax.axis_size("head") - 1))
        def _():
            out[...] = (total + ref[...].astype(F32)).astype(BF16)


def add(parts, at_ends=()):
    return call(functools.partial(add_kernel, len(parts)), [shaped(*parts[0].shape)], [*parts, *at_ends])[0]


def swap(value, axis, mask):
    return lax.ppermute(value, axis, [(i, i ^ mask) for i in range(lax.axis_size(axis))])


def gather(block, join):
    n_ctx = lax.axis_size("ctx")
    if n_ctx != 8:
        blocks = [block if m == 0 else swap(block, "ctx", m) for m in range(0, n_ctx, 2)]
        return [b for pair in blocks for b in (pair, swap(pair, "ctx", 1))]
    pair = join(lax.ppermute(block, "ctx", [(i, i ^ (4 if i % 2 else 2)) for i in range(8)]))
    far = lax.ppermute(pair, "ctx", [(i, i ^ (2 if i % 2 else 4)) for i in range(8)])
    return [pair, far, swap(pair, "ctx", 1), swap(far, "ctx", 1)]


def send(value, pairs):
    return lax.ppermute(value, "head", pairs)


def scatter_line(part):
    first = send(part((2,))[0], [(0, 1), (1, 3), (2, 0), (3, 2)])
    far, = part((3,))
    ends = send(far, [(0, 3), (3, 0)])
    near, own = part((1, 0), far)
    near = send(near, [(0, 1), (1, 0), (2, 3), (3, 2)])
    middle = send(add([far, first]), [(1, 2), (2, 1)])
    return add([own, near, ends, middle], [first])


def scatter_direct(part, n_head):
    parts = []
    for x in [*range(n_head - 1, 0, -1), 0]:
        got, = part((x,))
        parts.append(swap(got, "head", x) if x else got)
    return add(parts)


def shards(queries, fresh_keys, fresh_values, cache_keys, cache_values, page_request, prompt_lengths, output_weight):
    n_ctx, n_head = lax.axis_size("ctx"), lax.axis_size("head")
    rows, columns = queries.shape[0], output_weight.shape[1]
    tokens, pages = cache_keys.shape[0], page_request.shape[0]
    kv_width = 2 * fresh_keys.shape[1] // n_head
    q_width = queries.shape[1] // n_head
    groups = kv_width // (2 * HD)
    stacked = q_width // (groups * HD) * rows
    keys = n_ctx * tokens

    *packed, sent = call(
        pack_kernel, [shaped(rows, kv_width)] * n_head + [shaped(tokens + pages, kv_width)],
        [page_request, fresh_keys, fresh_values, cache_keys, cache_values], room=58 * MIB,
    )
    fresh, cache, ends, *query = call(
        stage_kernel,
        [shaped(rows, kv_width), shaped(tokens + pages, kv_width), shaped(prompt_lengths.shape[0], LANES, jnp.int32)]
        + [shaped(rows, q_width)] * n_head,
        [prompt_lengths, queries, packed[0], sent],
    )

    def stack(parts, *after):
        rows, columns = parts[0].shape
        return call(stack_kernel, [shaped(len(parts) * rows, columns)], parts, after=after)[0]

    fresh = stack([fresh, *(swap(packed[x], "head", x) for x in range(1, n_head))])
    cache = gather(sent, lambda got: stack([cache, got], fresh))
    for x in range(1, n_head):
        query[x] = swap(stack([query[x]], fresh) if x > 1 else query[x], "head", x)
    fresh = gather(fresh, lambda got: stack([fresh, got], *query[1:3]))

    scratch = [pltpu.VMEM((groups, stacked, keys), F32), pltpu.VMEM((n_ctx, tokens, LANES), BF16)]
    room = 4 * groups * stacked * keys + 6 * MIB
    xs = range(n_head)
    state = call(
        functools.partial(cache_kernel, xs, len(cache), n_ctx, n_head, q_width),
        [jax.ShapeDtypeStruct((groups, stacked, lanes), F32) for _ in xs for lanes in (2 * HD, LANES)],
        [ends, *query, *cache], scratch=scratch, room=room,
        cost=pl.CostEstimate(
            flops=16 * n_head * rows * q_width * keys,
            bytes_accessed=2 * keys * kv_width,
            transcendentals=n_head * rows * (q_width // HD) * keys,
        ),
    )

    def part(xs, *after):
        return call(
            functools.partial(fresh_kernel, xs, len(fresh), n_ctx, n_head, q_width), [shaped(rows, columns)] * len(xs),
            [ends, *(query[x] for x in xs), *fresh, *(a for x in xs for a in state[2 * x:2 * x + 2]), output_weight],
            after=after, scratch=[*scratch, pltpu.VMEM((len(xs) * rows, q_width), BF16)], room=room,
            cost=pl.CostEstimate(
                flops=len(xs) * (16 * rows * q_width * keys + 8 * rows * q_width * columns),
                bytes_accessed=2 * keys * kv_width,
                transcendentals=len(xs) * rows * (q_width // HD) * keys,
            ),
        )

    return scatter_line(part) if n_head == 4 else scatter_direct(part, n_head)


def solution(mesh):
    placed = (
        P(("ctx", "head"), None),
        P(("ctx", "head"), None),
        P(("ctx", "head"), None),
        P("ctx", "head"),
        P("ctx", "head"),
        P("ctx"),
        P(),
        P("head", None),
    )
    return jax.shard_map(
        shards, mesh=mesh, in_specs=placed, out_specs=P(("ctx", "head"), None), check_vma=False
    )
```

time: 113 us -> 86.6 us (0.77); the launches traced: 111 us -> 86.3 us
  starting transfers between devices: 30.1 us -> 22.6 us
  local copies, waits for them, and re-layouts: 9.6 us -> 3.5 us
  waiting for transfers between devices: 40.1 us -> 36.1 us
  Pallas kernels: 27.5 us -> 23.9 us
  other arithmetic: 3.48 us -> 0.01 us
    ppermute x20 -> x10, waiting for transfers between devices: 31.6 us -> 1.97 us  [swap(): lax.ppermute(value, axis, [(i, i ^ mask) for i in range(lax.axis_size(axi...]
    ppermute x4, waiting for transfers between devices: 8.52 us -> 22.3 us  [send(): return lax.ppermute(value, 'head', pairs)]
    ppermute x20 -> x10, starting transfers between devices: 22 us -> 8.96 us  [swap(): lax.ppermute(value, axis, [(i, i ^ mask) for i in range(lax.axis_size(axi...]
    ppermute x0 -> x4, waiting for transfers between devices: none -> 11.8 us  [the longest x2 11.8 us: gather(): lax.ppermute(pair, 'ctx', [(i, i ^ (2 if i % 2 else 4)) for i in range(8)])]
    ppermute x0 -> x4, starting transfers between devices: none -> 6.46 us  [the longest x2 3.47 us: gather(): lax.ppermute(block, 'ctx', [(i, i ^ (4 if i % 2 else 2)) for i in range(8)])]
    unnamed x31 -> x12, local copies, waits for them, and re-layouts: 9.6 us -> 3.5 us
    pallas_call x6 -> x13, Pallas kernels: 27.5 us -> 23.9 us  [call(): pl.pallas_call(body, out_shape=outs, in_specs=specs + [pl.BlockSpec(memor...]
    convert_element_type x2 -> x0, other arithmetic: 3.48 us -> none  [the longest x1 2.49 us: shards(): return total.astype(BF16)]
  transfers between devices with their start and end apart: 24 -> 18, of which waited for: 7 -> 5; matrix products, arithmetic and copies ran while one was open for 2% -> 0% of each run, Pallas kernels for 19% -> 19%
where the time goes in v3:
time: 86.6 us; the launch traced here: 86.3 us
  waiting for transfers between devices  36.1 us (42%)
  Pallas kernels  23.9 us (28%)
  starting transfers between devices  22.6 us (26%)
  local copies, waits for them, and re-layouts  3.5 us (4%)
    pallas_call x13, Pallas kernels, call(): pl.pallas_call(body, out_shape=outs, in_specs=specs + [pl.BlockSpec(memor...  23.9 us
    ppermute x4, waiting for transfers between devices, send(): return lax.ppermute(value, 'head', pairs)  22.3 us
    ppermute x2, waiting for transfers between devices, gather(): lax.ppermute(pair, 'ctx', [(i, i ^ (2 if i % 2 else 4)) for i in range(8)])  11.8 us
    ppermute x10, starting transfers between devices, swap(): lax.ppermute(value, axis, [(i, i ^ mask) for i in range(lax.axis_size(axi...  8.96 us
    ppermute x4, starting transfers between devices, send(): return lax.ppermute(value, 'head', pairs)  7.17 us
    unnamed x12, local copies, waits for them, and re-layouts  3.5 us
    ppermute x2, starting transfers between devices, gather(): lax.ppermute(block, 'ctx', [(i, i ^ (4 if i % 2 else 2)) for i in range(8)])  3.47 us
    ppermute x2, starting transfers between devices, gather(): lax.ppermute(pair, 'ctx', [(i, i ^ (2 if i % 2 else 4)) for i in range(8)])  2.99 us
  transfers between devices with their start and end apart: 18, of which 5 were waited for; matrix products, arithmetic and copies ran while one was open for 0% of the time, Pallas kernels for 19%

profile of v3, /device:TPU:0, one launch (start us, length us, event | category | flops | bytes accessed | tf_op | source)
XLA Modules:
  0.0 86.3 jit_solution(11375756970268324074)
XLA Ops:
  0.0 1.9 %shard_map.82 = (bf16[64,512]{1,0:T(8,128)(2,1)}, bf16[64,512]{1,0:T(8,128)(2,1)}, bf16[64,512]{1,0:T(8,128)(2,1)}, bf16[64,512]{1,0:T(8,128)(2,1)}, bf16[272,512]{1,0:T(8,128)(2,1)}) custom-call(s32[16]{0:T(128)} %refs_0_.2, bf16[64,1024]{1,0:T(8,128)(2,1)} %refs_1_.2, bf16[64,1024]{1,0:T(8,128)(2,1)} %refs_2_.1, bf16[256,256]{1,0:T(8,128)(2,1)} %refs_3_.1, ...), custom_call_target="tpu_custom_call" | custom-call | tf_op jit(solution)/shard_map/pallas_call | solution.py:36
  1.9 2.9 %collective-permute-start.10 = (bf16[272,512]{1,0:T(8,128)(2,1)}, bf16[272,512]{1,0:T(8,128)(2,1)S(1)}, u32[]{:S(2)}, u32[]{:S(2)}) collective-permute-start(bf16[272,512]{1,0:T(8,128)(2,1)} %get-tuple-element.28.refs_3_), channel_id=1, source_target_pairs={{0,8},{4,20},{8,0},{12,28},{16,24},{20,4},{24,16},{28,12},{1,9},{5... | collective-permute-start | bytes 835592 | tf_op jit(solution)/shard_map/ppermute | solution.py:251
  4.9 1.6 %collective-permute-start.1 = (bf16[64,512]{1,0:T(8,128)(2,1)}, bf16[64,512]{1,0:T(8,128)(2,1)S(1)}, u32[]{:S(2)}, u32[]{:S(2)}) collective-permute-start(bf16[64,512]{1,0:T(8,128)(2,1)} %get-tuple-element.33), channel_id=1, source_target_pairs={{0,1},{1,0},{2,3},{3,2},{4,5},{5,4},{6,7},{7,6},{8,9},{9,8},{10,11... | collective-permute-start | bytes 196616 | tf_op jit(solution)/shard_map/ppermute | solution.py:243
  6.5 2.6 %collective-permute-start.2 = (bf16[64,512]{1,0:T(8,128)(2,1)}, bf16[64,512]{1,0:T(8,128)(2,1)S(1)}, u32[]{:S(2)}, u32[]{:S(2)}) collective-permute-start(bf16[64,512]{1,0:T(8,128)(2,1)} %get-tuple-element.34), channel_id=1, source_target_pairs={{0,2},{1,3},{2,0},{3,1},{4,6},{5,7},{6,4},{7,5},{8,10},{9,11},{10,... | collective-permute-start | bytes 196616 | tf_op jit(solution)/shard_map/ppermute | solution.py:243
  9.1 0.2 collective-permute-start.3
  9.3 0.0 copy-start
  9.3 1.0 %copy-done = bf16[64,4096]{1,0:T(8,128)(2,1)S(1)} copy-done((bf16[64,4096]{1,0:T(8,128)(2,1)S(1)}, bf16[64,4096]{1,0:T(8,128)(2,1)}, u32[]{:S(2)}) %copy-start) | copy-done | bytes 524312
  10.3 0.0 copy-start.1
  10.3 1.0 %copy-done.1 = bf16[272,512]{1,0:T(8,128)(2,1)S(1)} copy-done((bf16[272,512]{1,0:T(8,128)(2,1)S(1)}, bf16[272,512]{1,0:T(8,128)(2,1)}, u32[]{:S(2)}) %copy-start.1) | copy-done | bytes 278552
  11.3 0.0 copy-start.2
  11.3 0.8 copy-done.2
  12.1 0.0 copy-start.3
  12.1 0.7 copy-done.3
  12.8 0.6 shard_map.83
  13.4 0.0 collective-permute-done.1.refs_1_
  13.4 0.3 collective-permute-done.2.refs_2_
  13.7 1.6 %collective-permute-done.3.refs_3_ = bf16[64,512]{1,0:T(8,128)(2,1)S(1)} collective-permute-done((bf16[64,512]{1,0:T(8,128)(2,1)}, bf16[64,512]{1,0:T(8,128)(2,1)S(1)}, u32[]{:S(2)}, u32[]{:S(2)}) %collective-permute-start.3) | collective-permute-done | bytes 65568 | tf_op jit(solution)/shard_map/ppermute | solution.py:243
  15.3 0.0 collective-permute-done.10.refs_1_
  15.4 1.6 %collective-permute-start.11 = (bf16[544,512]{1,0:T(8,128)(2,1)S(1)}, bf16[544,512]{1,0:T(8,128)(2,1)S(1)}, u32[]{:S(2)}, u32[]{:S(2)}) collective-permute-start(bf16[544,512]{1,0:T(8,128)(2,1)S(1)} %shard_map.88.refs_5_), channel_id=1, source_target_pairs={{0,16},{4,12},{8,24},{12,4},{16,0},{20,28},{24,8},{28,20},{1,17},{... | collective-permute-start | bytes 1671176 | tf_op jit(solution)/shard_map/ppermute | solution.py:252
  17.0 0.5 collective-permute-start.4
  17.5 0.0 collective-permute-start
  17.5 2.3 %collective-permute-start.5 = (bf16[64,1024]{1,0:T(8,128)(2,1)S(1)}, bf16[64,1024]{1,0:T(8,128)(2,1)S(1)}, u32[]{:S(2)}, u32[]{:S(2)}) collective-permute-start(bf16[64,1024]{1,0:T(8,128)(2,1)S(1)} %shard_map.85), channel_id=1, source_target_pairs={{0,2},{1,3},{2,0},{3,1},{4,6},{5,7},{6,4},{7,5},{8,10},{9,11},{10,... | collective-permute-start | bytes 393224 | tf_op jit(solution)/shard_map/ppermute | solution.py:243
  19.9 0.0 collective-permute-start.12
  19.9 6.2 %collective-permute-done.11.refs_6_ = bf16[544,512]{1,0:T(8,128)(2,1)S(1)} collective-permute-done((bf16[544,512]{1,0:T(8,128)(2,1)S(1)}, bf16[544,512]{1,0:T(8,128)(2,1)S(1)}, u32[]{:S(2)}, u32[]{:S(2)}) %collective-permute-start.11) | collective-permute-done | bytes 557088 | tf_op jit(solution)/shard_map/ppermute | solution.py:252
  26.0 0.0 collective-permute-start.13
  26.0 0.0 collective-permute-done.refs_2_.refs_1_
  26.0 0.0 collective-permute-done.5.refs_3_.refs_1_
  26.0 0.0 collective-permute-done.4.refs_1_
  26.1 1.4 %collective-permute-start.6 = (bf16[512,512]{1,0:T(8,128)(2,1)S(1)}, bf16[512,512]{1,0:T(8,128)(2,1)S(1)}, u32[]{:S(2)}, u32[]{:S(2)}) collective-permute-start(bf16[512,512]{1,0:T(8,128)(2,1)S(1)} %shard_map.86.refs_2_.refs_3_), channel_id=1, source_target_pairs={{0,16},{4,12},{8,24},{12,4},{16,0},{20,28},{24,8},{28,20},{1,17},{... | collective-permute-start | bytes 1572872 | tf_op jit(solution)/shard_map/ppermute | solution.py:252
  27.5 0.0 slice-start
  27.5 2.2 %collective-permute-start.9 = (bf16[64,1024]{1,0:T(8,128)(2,1)S(1)}, bf16[64,1024]{1,0:T(8,128)(2,1)S(1)}, u32[]{:S(2)}, u32[]{:S(2)}) collective-permute-start(bf16[64,1024]{1,0:T(8,128)(2,1)S(1)} %shard_map.87), channel_id=1, source_target_pairs={{0,3},{1,2},{2,1},{3,0},{4,7},{5,6},{6,5},{7,4},{8,11},{9,10},{10,... | collective-permute-start | bytes 393224 | tf_op jit(solution)/shard_map/ppermute | solution.py:243
  29.8 0.0 collective-permute-start.7
  29.8 5.6 %collective-permute-done.6.refs_3_.refs_4_ = bf16[512,512]{1,0:T(8,128)(2,1)S(1)} collective-permute-done((bf16[512,512]{1,0:T(8,128)(2,1)S(1)}, bf16[512,512]{1,0:T(8,128)(2,1)S(1)}, u32[]{:S(2)}, u32[]{:S(2)}) %collective-permute-start.6) | collective-permute-done | bytes 524320 | tf_op jit(solution)/shard_map/ppermute | solution.py:252
  35.4 0.0 collective-permute-start.8
  35.4 0.0 collective-permute-done.9.refs_4_.refs_1_
  35.4 0.0 collective-permute-done.12.refs_7_
  35.4 0.0 collective-permute-done.13.refs_8_
  35.4 0.0 slice-start.1
  35.4 6.3 %shard_map.89 = (f32[2,256,256]{2,1,0:T(8,128)S(1)}, f32[2,256,128]{2,1,0:T(8,128)S(1)}, f32[2,256,256]{2,1,0:T(8,128)S(1)}, f32[2,256,128]{2,1,0:T(8,128)S(1)},...) custom-call(s32[2,128]{1,0:T(2,128)S(1)} %get-tuple-element.29.refs_, ...), custom_call_target="tpu_custom_call" | custom-call | flops 8589934592 | bytes 2097152 | tf_op jit(solution)/shard_map/pallas_call | solution.py:36
  41.7 0.0 collective-permute-done.7.refs_4_.refs_5_
  41.7 0.0 collective-permute-done.8.refs_5_.refs_6_
  41.7 0.0 slice-done
  41.7 0.0 slice-done.1
  41.8 4.1 %shard_map.92 = bf16[64,4096]{1,0:T(8,128)(2,1)S(1)} custom-call(s32[2,128]{1,0:T(2,128)S(1)} %get-tuple-element.29.refs_0_, bf16[64,1024]{1,0:T(8,128)(2,1)S(1)} %collective-permute-done.5.refs_3_.refs_1_, bf16[512,512]{1,0:T(8,128)(2,1)S(1)} %shard_map.86.refs_2_.refs_3_, bf16[512,512]{1,0:T(8,128)(2,1)S(1)} %collective-permute-done.6.refs_3_.refs_4_, ...), custom_call_target="tpu_custom_call" | custom-call | flops 4294967296 | bytes 2097152 | tf_op jit(solution)/shard_map/pallas_call | solution.py:36
  45.9 2.0 %collective-permute-start.16 = (bf16[64,4096]{1,0:T(8,128)(2,1)S(1)}, bf16[64,4096]{1,0:T(8,128)(2,1)S(1)}, u32[]{:S(2)}, u32[]{:S(2)}) collective-permute-start(bf16[64,4096]{1,0:T(8,128)(2,1)S(1)} %shard_map.92), channel_id=1, source_target_pairs={{0,1},{1,3},{2,0},{3,2},{4,5},{5,7},{6,4},{7,6},{8,9},{9,11},{10,8... | collective-permute-start | bytes 1572872 | tf_op jit(solution)/shard_map/ppermute | solution.py:257
  47.8 4.0 %shard_map.90.refs_12_.refs_0_ = bf16[64,4096]{1,0:T(8,128)(2,1)S(1)} custom-call(s32[2,128]{1,0:T(2,128)S(1)} %get-tuple-element.29.refs_0_, bf16[64,1024]{1,0:T(8,128)(2,1)S(1)} %collective-permute-done.9.refs_4_.refs_1_, bf16[512,512]{1,0:T(8,128)(2,1)S(1)} %shard_map.86.refs_2_.refs_3_, bf16[512,512]{1,0:T(8,128)(2,1)S(1)} %collective-permute-done.6.refs_3_.refs_4_, ...), custom_call_target="tpu_custom_call" | custom-call | flops 4294967296 | bytes 2097152 | tf_op jit(solution)/shard_map/pallas_call | solution.py:36
  51.9 4.4 %collective-permute-start.15 = (bf16[64,4096]{1,0:T(8,128)(2,1)S(1)}, bf16[64,4096]{1,0:T(8,128)(2,1)S(1)}, u32[]{:S(2)}, u32[]{:S(2)}) collective-permute-start(bf16[64,4096]{1,0:T(8,128)(2,1)S(1)} %shard_map.90.refs_12_.refs_0_), channel_id=1, source_target_pairs={{0,3},{3,0},{4,7},{7,4},{8,11},{11,8},{12,15},{15,12},{16,19},{19,... | collective-permute-start | bytes 1572872 | tf_op jit(solution)/shard_map/ppermute | solution.py:257
  56.3 5.5 %shard_map.91 = (bf16[64,4096]{1,0:T(8,128)(2,1)S(1)}, bf16[64,4096]{1,0:T(8,128)(2,1)S(1)}) custom-call(s32[2,128]{1,0:T(2,128)S(1)} %get-tuple-element.29.refs_0_, bf16[64,1024]{1,0:T(8,128)(2,1)S(1)} %collective-permute-done.refs_2_.refs_1_, bf16[64,1024]{1,0:T(8,128)(2,1)S(1)} %get-tuple-element.31.refs_1_.refs_2_, ...), custom_call_target="tpu_custom_call" | custom-call | flops 8589934592 | bytes 2097152 | tf_op jit(solution)/shard_map/pallas_call | solution.py:36
  61.9 0.1 collective-permute-start.14
  61.9 0.0 collective-permute-done.16.refs_1_.refs_4_
  62.0 0.1 shard_map.93
  62.1 0.7 collective-permute-start.17
  62.8 22.3 %collective-permute-done.14.refs_1_ = bf16[64,4096]{1,0:T(8,128)(2,1)S(1)} collective-permute-done((bf16[64,4096]{1,0:T(8,128)(2,1)S(1)}, bf16[64,4096]{1,0:T(8,128)(2,1)S(1)}, u32[]{:S(2)}, u32[]{:S(2)}) %collective-permute-start.14) | collective-permute-done | bytes 524320 | tf_op jit(solution)/shard_map/ppermute | solution.py:257
  85.1 0.0 collective-permute-done.15.refs_2_
  85.1 0.0 collective-permute-done.17.refs_3_
  85.1 1.1 %shard_map.94 = bf16[64,4096]{1,0:T(8,128)(2,1)} custom-call(bf16[64,4096]{1,0:T(8,128)(2,1)S(1)} %get-tuple-element.45.refs_0_, bf16[64,4096]{1,0:T(8,128)(2,1)S(1)} %collective-permute-done.14.refs_1_, bf16[64,4096]{1,0:T(8,128)(2,1)S(1)} %collective-permute-done.15.refs_2_, bf16[64,4096]{1,0:T(8,128)(2,1)S(1)} %collective-permute-done.17.refs_3_, ...), custom_call_target="tpu_custom_call" | custom-call | tf_op jit(solution)/shard_map/pallas_call | solution.py:36
  (6 shorter events, 0.1 us)
Async XLA Ops:
  1.9 13.4 %collective-permute-start.10 = (bf16[272,512]{1,0:T(8,128)(2,1)}, bf16[272,512]{1,0:T(8,128)(2,1)S(1)}, u32[]{:S(2)}, u32[]{:S(2)}) collective-permute-start(bf16[272,512]{1,0:T(8,128)(2,1)} %get-tuple-element.28.refs_3_), channel_id=1, source_target_pairs={{0,8},{4,20},{8,0},{12,28},{16,24},{20,4},{24,16},{28,12},{1,9},{5... | collective-permute-start | bytes 835592 | tf_op jit(solution)/shard_map/ppermute | solution.py:251
  4.9 8.5 %collective-permute-start.1 = (bf16[64,512]{1,0:T(8,128)(2,1)}, bf16[64,512]{1,0:T(8,128)(2,1)S(1)}, u32[]{:S(2)}, u32[]{:S(2)}) collective-permute-start(bf16[64,512]{1,0:T(8,128)(2,1)} %get-tuple-element.33), channel_id=1, source_target_pairs={{0,1},{1,0},{2,3},{3,2},{4,5},{5,4},{6,7},{7,6},{8,9},{9,8},{10,11... | collective-permute-start | bytes 196616 | tf_op jit(solution)/shard_map/ppermute | solution.py:243
  6.5 7.2 %collective-permute-start.2 = (bf16[64,512]{1,0:T(8,128)(2,1)}, bf16[64,512]{1,0:T(8,128)(2,1)S(1)}, u32[]{:S(2)}, u32[]{:S(2)}) collective-permute-start(bf16[64,512]{1,0:T(8,128)(2,1)} %get-tuple-element.34), channel_id=1, source_target_pairs={{0,2},{1,3},{2,0},{3,1},{4,6},{5,7},{6,4},{7,5},{8,10},{9,11},{10,... | collective-permute-start | bytes 196616 | tf_op jit(solution)/shard_map/ppermute | solution.py:243
  9.1 6.3 %collective-permute-start.3 = (bf16[64,512]{1,0:T(8,128)(2,1)}, bf16[64,512]{1,0:T(8,128)(2,1)S(1)}, u32[]{:S(2)}, u32[]{:S(2)}) collective-permute-start(bf16[64,512]{1,0:T(8,128)(2,1)} %get-tuple-element.35), channel_id=1, source_target_pairs={{0,3},{1,2},{2,1},{3,0},{4,7},{5,6},{6,5},{7,4},{8,11},{9,10},{10,... | collective-permute-start | bytes 196616 | tf_op jit(solution)/shard_map/ppermute | solution.py:243
  9.3 1.0 %copy-start = (bf16[64,4096]{1,0:T(8,128)(2,1)S(1)}, bf16[64,4096]{1,0:T(8,128)(2,1)}, u32[]{:S(2)}) copy-start(bf16[64,4096]{1,0:T(8,128)(2,1)} %refs_1_.3) | copy-start | bytes 1572868
  10.3 1.0 %copy-start.1 = (bf16[272,512]{1,0:T(8,128)(2,1)S(1)}, bf16[272,512]{1,0:T(8,128)(2,1)}, u32[]{:S(2)}) copy-start(bf16[272,512]{1,0:T(8,128)(2,1)} %get-tuple-element.28.refs_3_) | copy-start | bytes 835588
  11.3 0.8 copy-start.2
  12.1 0.7 copy-start.3
  15.4 10.6 %collective-permute-start.11 = (bf16[544,512]{1,0:T(8,128)(2,1)S(1)}, bf16[544,512]{1,0:T(8,128)(2,1)S(1)}, u32[]{:S(2)}, u32[]{:S(2)}) collective-permute-start(bf16[544,512]{1,0:T(8,128)(2,1)S(1)} %shard_map.88.refs_5_), channel_id=1, source_target_pairs={{0,16},{4,12},{8,24},{12,4},{16,0},{20,28},{24,8},{28,20},{1,17},{... | collective-permute-start | bytes 1671176 | tf_op jit(solution)/shard_map/ppermute | solution.py:252
  17.0 9.1 %collective-permute-start.4 = (bf16[256,512]{1,0:T(8,128)(2,1)S(1)}, bf16[256,512]{1,0:T(8,128)(2,1)S(1)}, u32[]{:S(2)}, u32[]{:S(2)}) collective-permute-start(bf16[256,512]{1,0:T(8,128)(2,1)S(1)} %shard_map.84.refs_1_.refs_0_.refs_2_), channel_id=1, source_target_pairs={{0,8},{4,20},{8,0},{12,28},{16,24},{20,4},{24,16},{28,12},{1,9},{5... | collective-permute-start | bytes 786440 | tf_op jit(solution)/shard_map/ppermute | solution.py:251
  17.5 8.5 %collective-permute-start = (bf16[64,1024]{1,0:T(8,128)(2,1)S(1)}, bf16[64,1024]{1,0:T(8,128)(2,1)S(1)}, u32[]{:S(2)}, u32[]{:S(2)}) collective-permute-start(bf16[64,1024]{1,0:T(8,128)(2,1)S(1)} %get-tuple-element.30), channel_id=1, source_target_pairs={{0,1},{1,0},{2,3},{3,2},{4,5},{5,4},{6,7},{7,6},{8,9},{9,8},{10,11... | collective-permute-start | bytes 393224 | tf_op jit(solution)/shard_map/ppermute | solution.py:243
  17.5 8.5 %collective-permute-start.5 = (bf16[64,1024]{1,0:T(8,128)(2,1)S(1)}, bf16[64,1024]{1,0:T(8,128)(2,1)S(1)}, u32[]{:S(2)}, u32[]{:S(2)}) collective-permute-start(bf16[64,1024]{1,0:T(8,128)(2,1)S(1)} %shard_map.85), channel_id=1, source_target_pairs={{0,2},{1,3},{2,0},{3,1},{4,6},{5,7},{6,4},{7,5},{8,10},{9,11},{10,... | collective-permute-start | bytes 393224 | tf_op jit(solution)/shard_map/ppermute | solution.py:243
  19.9 15.5 %collective-permute-start.12 = (bf16[544,512]{1,0:T(8,128)(2,1)S(1)}, bf16[544,512]{1,0:T(8,128)(2,1)S(1)}, u32[]{:S(2)}, u32[]{:S(2)}) collective-permute-start(bf16[544,512]{1,0:T(8,128)(2,1)S(1)} %shard_map.88.refs_5_), channel_id=1, source_target_pairs={{0,4},{4,0},{8,12},{12,8},{16,20},{20,16},{24,28},{28,24},{1,5},{5... | collective-permute-start | bytes 1671176 | tf_op jit(solution)/shard_map/ppermute | solution.py:243
  26.0 9.3 %collective-permute-start.13 = (bf16[544,512]{1,0:T(8,128)(2,1)S(1)}, bf16[544,512]{1,0:T(8,128)(2,1)S(1)}, u32[]{:S(2)}, u32[]{:S(2)}) collective-permute-start(bf16[544,512]{1,0:T(8,128)(2,1)S(1)} %collective-permute-done.11.refs_6_), channel_id=1, source_target_pairs={{0,4},{4,0},{8,12},{12,8},{16,20},{20,16},{24,28},{28,24},{1,5},{5... | collective-permute-start | bytes 1671176 | tf_op jit(solution)/shard_map/ppermute | solution.py:243
  26.1 9.2 %collective-permute-start.6 = (bf16[512,512]{1,0:T(8,128)(2,1)S(1)}, bf16[512,512]{1,0:T(8,128)(2,1)S(1)}, u32[]{:S(2)}, u32[]{:S(2)}) collective-permute-start(bf16[512,512]{1,0:T(8,128)(2,1)S(1)} %shard_map.86.refs_2_.refs_3_), channel_id=1, source_target_pairs={{0,16},{4,12},{8,24},{12,4},{16,0},{20,28},{24,8},{28,20},{1,17},{... | collective-permute-start | bytes 1572872 | tf_op jit(solution)/shard_map/ppermute | solution.py:252
  27.5 14.2 %slice-start = ((s8[8388608]{0:T(1024)(128)(4,1)}), s8[4194304]{0:T(1024)(128)(4,1)S(1)}, s32[]{:S(2)}) async-start(s8[8388608]{0:T(1024)(128)(4,1)} %bitcast), calls=%async_computation | async-start | bytes 8388608
  27.5 7.8 %collective-permute-start.9 = (bf16[64,1024]{1,0:T(8,128)(2,1)S(1)}, bf16[64,1024]{1,0:T(8,128)(2,1)S(1)}, u32[]{:S(2)}, u32[]{:S(2)}) collective-permute-start(bf16[64,1024]{1,0:T(8,128)(2,1)S(1)} %shard_map.87), channel_id=1, source_target_pairs={{0,3},{1,2},{2,1},{3,0},{4,7},{5,6},{6,5},{7,4},{8,11},{9,10},{10,... | collective-permute-start | bytes 393224 | tf_op jit(solution)/shard_map/ppermute | solution.py:243
  29.8 11.9 %collective-permute-start.7 = (bf16[512,512]{1,0:T(8,128)(2,1)S(1)}, bf16[512,512]{1,0:T(8,128)(2,1)S(1)}, u32[]{:S(2)}, u32[]{:S(2)}) collective-permute-start(bf16[512,512]{1,0:T(8,128)(2,1)S(1)} %shard_map.86.refs_2_.refs_3_), channel_id=1, source_target_pairs={{0,4},{4,0},{8,12},{12,8},{16,20},{20,16},{24,28},{28,24},{1,5},{5... | collective-permute-start | bytes 1572872 | tf_op jit(solution)/shard_map/ppermute | solution.py:243
  35.4 6.4 %collective-permute-start.8 = (bf16[512,512]{1,0:T(8,128)(2,1)S(1)}, bf16[512,512]{1,0:T(8,128)(2,1)S(1)}, u32[]{:S(2)}, u32[]{:S(2)}) collective-permute-start(bf16[512,512]{1,0:T(8,128)(2,1)S(1)} %collective-permute-done.6.refs_3_.refs_4_), channel_id=1, source_target_pairs={{0,4},{4,0},{8,12},{12,8},{16,20},{20,16},{24,28},{28,24},{1,5},{5... | collective-permute-start | bytes 1572872 | tf_op jit(solution)/shard_map/ppermute | solution.py:243
  35.4 6.4 %slice-start.1 = ((s8[8388608]{0:T(1024)(128)(4,1)}), s8[4194304]{0:T(1024)(128)(4,1)S(1)}, s32[]{:S(2)}) async-start(s8[8388608]{0:T(1024)(128)(4,1)} %bitcast), calls=%async_computation.1 | async-start | bytes 8388608
  45.9 16.1 %collective-permute-start.16 = (bf16[64,4096]{1,0:T(8,128)(2,1)S(1)}, bf16[64,4096]{1,0:T(8,128)(2,1)S(1)}, u32[]{:S(2)}, u32[]{:S(2)}) collective-permute-start(bf16[64,4096]{1,0:T(8,128)(2,1)S(1)} %shard_map.92), channel_id=1, source_target_pairs={{0,1},{1,3},{2,0},{3,2},{4,5},{5,7},{6,4},{7,6},{8,9},{9,11},{10,8... | collective-permute-start | bytes 1572872 | tf_op jit(solution)/shard_map/ppermute | solution.py:257
  51.9 33.2 %collective-permute-start.15 = (bf16[64,4096]{1,0:T(8,128)(2,1)S(1)}, bf16[64,4096]{1,0:T(8,128)(2,1)S(1)}, u32[]{:S(2)}, u32[]{:S(2)}) collective-permute-start(bf16[64,4096]{1,0:T(8,128)(2,1)S(1)} %shard_map.90.refs_12_.refs_0_), channel_id=1, source_target_pairs={{0,3},{3,0},{4,7},{7,4},{8,11},{11,8},{12,15},{15,12},{16,19},{19,... | collective-permute-start | bytes 1572872 | tf_op jit(solution)/shard_map/ppermute | solution.py:257
  61.9 23.3 %collective-permute-start.14 = (bf16[64,4096]{1,0:T(8,128)(2,1)S(1)}, bf16[64,4096]{1,0:T(8,128)(2,1)S(1)}, u32[]{:S(2)}, u32[]{:S(2)}) collective-permute-start(bf16[64,4096]{1,0:T(8,128)(2,1)S(1)} %get-tuple-element.46), channel_id=1, source_target_pairs={{0,1},{1,0},{2,3},{3,2},{4,5},{5,4},{6,7},{7,6},{8,9},{9,8},{10,11... | collective-permute-start | bytes 1572872 | tf_op jit(solution)/shard_map/ppermute | solution.py:257
  62.1 23.0 %collective-permute-start.17 = (bf16[64,4096]{1,0:T(8,128)(2,1)S(1)}, bf16[64,4096]{1,0:T(8,128)(2,1)S(1)}, u32[]{:S(2)}, u32[]{:S(2)}) collective-permute-start(bf16[64,4096]{1,0:T(8,128)(2,1)S(1)} %shard_map.93), channel_id=1, source_target_pairs={{1,2},{2,1},{5,6},{6,5},{9,10},{10,9},{13,14},{14,13},{17,18},{18,... | collective-permute-start | bytes 1572872 | tf_op jit(solution)/shard_map/ppermute | solution.py:257

commit v4 on v3

--- a/solution.py
+++ b/solution.py
@@ -86,6 +86,11 @@
         out[i * rows:(i + 1) * rows, :] = ref[...]
 
 
+def stack(parts, *after):
+    rows, columns = parts[0].shape
+    return call(stack_kernel, [shaped(len(parts) * rows, columns)], parts, after=after)[0]
+
+
 class Layout:
     def __init__(self, ends, rows, q_width, kv_width, n_ctx, n_head):
         self.rows, self.n_ctx, self.n_head = rows, n_ctx, n_head
@@ -104,10 +109,10 @@
         return piece * self.half + lax.rem(head * self.rows, self.half)
 
     def step_of(self, b):
-        if self.n_ctx != 8:
+        if self.n_ctx != 8 or self.n_head != 4:
             return b
         near = jnp.where(lax.rem(self.c, 2) == 0, 2, 4)
-        return [0, near, 6 - near, 6, 1, 7 - near, 1 + near, 7][b]
+        return [0, near, 1, 7 - near, 6 - near, 6, 1 + near, 7][b]
 
     def request(self, position):
         request = jnp.zeros(position.shape, jnp.int32)
@@ -171,24 +176,27 @@
     return [ref.at[pl.ds(i, tokens)] for ref in refs for i in range(0, ref.shape[0], tokens)]
 
 
-def cache_kernel(xs, count, n_ctx, n_head, q_width, ends, *refs):
+def first_kernel(xs, cached, count, n_ctx, n_head, q_width, ends, *refs):
     query, refs = refs[:len(xs)], refs[len(xs):]
     outs, (scores, masks) = refs[count:-2], refs[-2:]
     tokens = masks.shape[1]
-    cache = views(refs[:count], tokens + tokens // PAGE)
+    cache = views(refs[:cached], tokens + tokens // PAGE)
+    fresh = views(refs[cached:count], tokens)
     at = Layout(ends, query[0].shape[0], q_width, cache[0].shape[1], n_ctx, n_head)
     for b in range(n_ctx):
         masks[b] = at.cache_mask(cache[b][tokens:, :LANES])
     for i, x in enumerate(xs):
         summed, tops = outs[2 * i:2 * i + 2]
+        for b in range(len(fresh)):
+            masks[n_ctx + b] = at.fresh_mask(b, at.h ^ x)
         q_rows = at.query_rows(query[i], x)
         for g in range(at.groups):
             summed[g], tops[g] = attend(
-                q_rows[g], cache, [masks.at[b] for b in range(n_ctx)], scores.at[g], tokens, g, at.groups
+                q_rows[g], cache + fresh, [masks.at[b] for b in range(n_ctx + len(fresh))], scores.at[g], tokens, g, at.groups
             )
 
 
-def fresh_kernel(xs, count, n_ctx, n_head, q_width, ends, *refs):
+def last_kernel(xs, count, n_ctx, n_head, q_width, ends, *refs):
     query, refs = refs[:len(xs)], refs[len(xs):]
     fresh, state, refs = refs[:count], refs[count:count + 2 * len(xs)], refs[count + 2 * len(xs):]
     weight, outs, (scores, masks, mixed) = refs[0], refs[1:-3], refs[-3:]
@@ -197,12 +205,12 @@
     at = Layout(ends, rows, q_width, fresh[0].shape[1], n_ctx, n_head)
     for i, x in enumerate(xs):
         summed, tops = state[2 * i:2 * i + 2]
-        for b in range(n_ctx):
-            masks[b] = at.fresh_mask(b, at.h ^ x)
+        for b in range(len(fresh)):
+            masks[b] = at.fresh_mask(n_ctx - len(fresh) + b, at.h ^ x)
         q_rows = at.query_rows(query[i], x)
         for g in range(at.groups):
             sum_b, top_b = attend(
-                q_rows[g], fresh, [masks.at[b] for b in range(n_ctx)], scores.at[g], tokens, g, at.groups
+                q_rows[g], fresh, [masks.at[b] for b in range(len(fresh))], scores.at[g], tokens, g, at.groups
             )
             top = jnp.maximum(tops[g], top_b)
             factor_a, factor_b = jnp.exp2(tops[g] - top), jnp.exp2(top_b - top)
@@ -243,14 +251,15 @@
     return lax.ppermute(value, axis, [(i, i ^ mask) for i in range(lax.axis_size(axis))])
 
 
-def gather(block, join):
+def leg(block, first):
+    odd, even = (4, 2) if first else (2, 4)
+    return lax.ppermute(block, "ctx", [(i, i ^ (odd if i % 2 else even)) for i in range(8)])
+
+
+def gather(block):
     n_ctx = lax.axis_size("ctx")
-    if n_ctx != 8:
-        blocks = [block if m == 0 else swap(block, "ctx", m) for m in range(0, n_ctx, 2)]
-        return [b for pair in blocks for b in (pair, swap(pair, "ctx", 1))]
-    pair = join(lax.ppermute(block, "ctx", [(i, i ^ (4 if i % 2 else 2)) for i in range(8)]))
-    far = lax.ppermute(pair, "ctx", [(i, i ^ (2 if i % 2 else 4)) for i in range(8)])
-    return [pair, far, swap(pair, "ctx", 1), swap(far, "ctx", 1)]
+    blocks = [block if m == 0 else swap(block, "ctx", m) for m in range(0, n_ctx, 2)]
+    return [b for pair in blocks for b in (pair, swap(pair, "ctx", 1))]
 
 
 def send(value, pairs):
@@ -258,8 +267,9 @@
 
 
 def scatter_line(part):
-    first = send(part((2,))[0], [(0, 1), (1, 3), (2, 0), (3, 2)])
-    far, = part((3,))
+    next_inner, = part((2,))
+    first = send(next_inner, [(0, 1), (1, 3), (2, 0), (3, 2)])
+    far, = part((3,), next_inner)
     ends = send(far, [(0, 3), (3, 0)])
     near, own = part((1, 0), far)
     near = send(near, [(0, 1), (1, 0), (2, 3), (3, 2)])
@@ -296,43 +306,70 @@
         [prompt_lengths, queries, packed[0], sent],
     )
 
-    def stack(parts, *after):
-        rows, columns = parts[0].shape
-        return call(stack_kernel, [shaped(len(parts) * rows, columns)], parts, after=after)[0]
-
     fresh = stack([fresh, *(swap(packed[x], "head", x) for x in range(1, n_head))])
-    cache = gather(sent, lambda got: stack([cache, got], fresh))
     for x in range(1, n_head):
         query[x] = swap(stack([query[x]], fresh) if x > 1 else query[x], "head", x)
-    fresh = gather(fresh, lambda got: stack([fresh, got], *query[1:3]))
-
-    scratch = [pltpu.VMEM((groups, stacked, keys), F32), pltpu.VMEM((n_ctx, tokens, LANES), BF16)]
-    room = 4 * groups * stacked * keys + 6 * MIB
-    xs = range(n_head)
-    state = call(
-        functools.partial(cache_kernel, xs, len(cache), n_ctx, n_head, q_width),
-        [jax.ShapeDtypeStruct((groups, stacked, lanes), F32) for _ in xs for lanes in (2 * HD, LANES)],
-        [ends, *query, *cache], scratch=scratch, room=room,
-        cost=pl.CostEstimate(
-            flops=16 * n_head * rows * q_width * keys,
-            bytes_accessed=2 * keys * kv_width,
-            transcendentals=n_head * rows * (q_width // HD) * keys,
-        ),
-    )
-
-    def part(xs, *after):
-        return call(
-            functools.partial(fresh_kernel, xs, len(fresh), n_ctx, n_head, q_width), [shaped(rows, columns)] * len(xs),
-            [ends, *(query[x] for x in xs), *fresh, *(a for x in xs for a in state[2 * x:2 * x + 2]), output_weight],
-            after=after, scratch=[*scratch, pltpu.VMEM((len(xs) * rows, q_width), BF16)], room=room,
+    square = n_ctx == 8 and n_head == 4
+    if square:
+        pair = stack([cache, leg(sent, True)], fresh)
+        far = leg(pair, False)
+        got = leg(fresh, True)
+        cache = stack([pair, far], got, *query[1:3])
+        cache = [cache, swap(cache, "ctx", 1)]
+        fresh = stack([fresh, got])
+        early, late = [fresh, swap(fresh, "ctx", 1)], [leg(fresh, False)]
+    else:
+        cache, fresh = gather(sent), gather(fresh)
+        early, late = fresh[:n_ctx // 2], fresh[n_ctx // 2:]
+
+    attend_keys = lambda n: dict(
+        scratch=[pltpu.VMEM((groups, stacked, n * tokens), F32), pltpu.VMEM((n, tokens, LANES), BF16)],
+        room=4 * groups * stacked * n * tokens + 6 * MIB,
+    )
+
+    state = {}
+
+    def first(xs, *after):
+        n = n_ctx + n_ctx // 2
+        found = call(
+            functools.partial(first_kernel, xs, len(cache), len(cache) + len(early), n_ctx, n_head, q_width),
+            [jax.ShapeDtypeStruct((groups, stacked, lanes), F32) for _ in xs for lanes in (2 * HD, LANES)],
+            [ends, *(query[x] for x in xs), *cache, *early], after=after, **attend_keys(n),
             cost=pl.CostEstimate(
-                flops=len(xs) * (16 * rows * q_width * keys + 8 * rows * q_width * columns),
-                bytes_accessed=2 * keys * kv_width,
-                transcendentals=len(xs) * rows * (q_width // HD) * keys,
+                flops=16 * len(xs) * rows * q_width * n * tokens,
+                bytes_accessed=2 * n * tokens * kv_width,
+                transcendentals=len(xs) * rows * (q_width // HD) * n * tokens,
             ),
         )
-
-    return scatter_line(part) if n_head == 4 else scatter_direct(part, n_head)
+        state.update((x, found[2 * i:2 * i + 2]) for i, x in enumerate(xs))
+
+    def part(xs, *after):
+        n = n_ctx - n_ctx // 2
+        options = attend_keys(n)
+        options["scratch"].append(pltpu.VMEM((len(xs) * rows, q_width), BF16))
+        return call(
+            functools.partial(last_kernel, xs, len(late), n_ctx, n_head, q_width), [shaped(rows, columns)] * len(xs),
+            [ends, *(query[x] for x in xs), *late, *(a for x in xs for a in state[x]), output_weight],
+            after=after, **options,
+            cost=pl.CostEstimate(
+                flops=len(xs) * (16 * rows * q_width * n * tokens + 8 * rows * q_width * columns),
+                bytes_accessed=2 * n * tokens * kv_width,
+                transcendentals=len(xs) * rows * (q_width // HD) * n * tokens,
+            ),
+        )
+
+    if square:
+        first((2,))
+        late = [stack(late, state[2][1], query[3])]
+        late.append(swap(late[0], "ctx", 1))
+
+    def chunks(xs, *after):
+        todo = tuple(x for x in xs if x not in state)
+        if todo:
+            first(todo, *after)
+        return part(xs)
+
+    return scatter_line(chunks) if square else scatter_direct(chunks, n_head)
 
 
 def solution(mesh):

time: 86.6 us -> 81.2 us (0.938)
  waiting for transfers between devices: 36.1 us -> 29 us
  Pallas kernels: 23.9 us -> 25 us
    ppermute x4, waiting for transfers between devices: 11.8 us -> 1.23 us  [leg(): lax.ppermute(block, 'ctx', [(i, i ^ (odd if i % 2 else even)) for i in ra...]
    ppermute x10 -> x9, waiting for transfers between devices: 1.97 us -> 11.2 us  [swap(): lax.ppermute(value, axis, [(i, i ^ mask) for i in range(lax.axis_size(axi...]
    ppermute x4, waiting for transfers between devices: 22.3 us -> 16.5 us  [send(): return lax.ppermute(value, 'head', pairs)]
    pallas_call x13 -> x17, Pallas kernels: 23.9 us -> 25 us  [call(): pl.pallas_call(body, out_shape=outs, in_specs=specs + [pl.BlockSpec(memor...]
    ppermute x10 -> x9, starting transfers between devices: 8.96 us -> 9.65 us  [swap(): lax.ppermute(value, axis, [(i, i ^ mask) for i in range(lax.axis_size(axi...]
  transfers between devices with their start and end apart: 18 -> 17, of which waited for: 5 -> 9; matrix products, arithmetic and copies ran while one was open for 0% -> 0% of each run, Pallas kernels for 19% -> 23%
where the time goes in v4:
time: 81.2 us; the launch traced here: 80.9 us
  waiting for transfers between devices  29 us (36%)
  Pallas kernels  25 us (31%)
  starting transfers between devices  23.3 us (29%)
  local copies, waits for them, and re-layouts  3.5 us (4%)
    pallas_call x17, Pallas kernels, call(): pl.pallas_call(body, out_shape=outs, in_specs=specs + [pl.BlockSpec(memor...  25 us
    ppermute x4, waiting for transfers between devices, send(): return lax.ppermute(value, 'head', pairs)  16.5 us
    ppermute x9, waiting for transfers between devices, swap(): lax.ppermute(value, axis, [(i, i ^ mask) for i in range(lax.axis_size(axi...  11.2 us
    ppermute x9, starting transfers between devices, swap(): lax.ppermute(value, axis, [(i, i ^ mask) for i in range(lax.axis_size(axi...  9.65 us
    ppermute x4, starting transfers between devices, send(): return lax.ppermute(value, 'head', pairs)  7.17 us
    ppermute x4, starting transfers between devices, leg(): lax.ppermute(block, 'ctx', [(i, i ^ (odd if i % 2 else even)) for i in ra...  6.44 us
    unnamed x12, local copies, waits for them, and re-layouts  3.5 us
  transfers between devices with their start and end apart: 17, of which 9 were waited for; matrix products, arithmetic and copies ran while one was open for 0% of the time, Pallas kernels for 23%

profile of v4, /device:TPU:0, one launch (start us, length us, event | category | flops | bytes accessed | tf_op | source)
XLA Modules:
  0.0 80.9 jit_solution(16942548422603781688)
XLA Ops:
  0.0 1.9 %shard_map.82 = (bf16[64,512]{1,0:T(8,128)(2,1)}, bf16[64,512]{1,0:T(8,128)(2,1)}, bf16[64,512]{1,0:T(8,128)(2,1)}, bf16[64,512]{1,0:T(8,128)(2,1)}, bf16[272,512]{1,0:T(8,128)(2,1)}) custom-call(s32[16]{0:T(128)} %refs_0_.2, bf16[64,1024]{1,0:T(8,128)(2,1)} %refs_1_.2, bf16[64,1024]{1,0:T(8,128)(2,1)} %refs_2_.1, bf16[256,256]{1,0:T(8,128)(2,1)} %refs_3_.1, ...), custom_call_target="tpu_custom_call" | custom-call | tf_op jit(solution)/shard_map/pallas_call | solution.py:36
  1.9 2.9 %collective-permute-start.7 = (bf16[272,512]{1,0:T(8,128)(2,1)}, bf16[272,512]{1,0:T(8,128)(2,1)S(1)}, u32[]{:S(2)}, u32[]{:S(2)}) collective-permute-start(bf16[272,512]{1,0:T(8,128)(2,1)} %get-tuple-element.28.refs_3_), channel_id=1, source_target_pairs={{0,8},{4,20},{8,0},{12,28},{16,24},{20,4},{24,16},{28,12},{1,9},{5... | collective-permute-start | bytes 835592 | tf_op jit(solution)/shard_map/ppermute | solution.py:256
  4.9 1.6 %collective-permute-start.1 = (bf16[64,512]{1,0:T(8,128)(2,1)}, bf16[64,512]{1,0:T(8,128)(2,1)S(1)}, u32[]{:S(2)}, u32[]{:S(2)}) collective-permute-start(bf16[64,512]{1,0:T(8,128)(2,1)} %get-tuple-element.33), channel_id=1, source_target_pairs={{0,1},{1,0},{2,3},{3,2},{4,5},{5,4},{6,7},{7,6},{8,9},{9,8},{10,11... | collective-permute-start | bytes 196616 | tf_op jit(solution)/shard_map/ppermute | solution.py:251
  6.5 2.6 %collective-permute-start.2 = (bf16[64,512]{1,0:T(8,128)(2,1)}, bf16[64,512]{1,0:T(8,128)(2,1)S(1)}, u32[]{:S(2)}, u32[]{:S(2)}) collective-permute-start(bf16[64,512]{1,0:T(8,128)(2,1)} %get-tuple-element.34), channel_id=1, source_target_pairs={{0,2},{1,3},{2,0},{3,1},{4,6},{5,7},{6,4},{7,5},{8,10},{9,11},{10,... | collective-permute-start | bytes 196616 | tf_op jit(solution)/shard_map/ppermute | solution.py:251
  9.1 0.2 collective-permute-start.3
  9.3 0.0 copy-start
  9.3 1.0 %copy-done = bf16[64,4096]{1,0:T(8,128)(2,1)S(1)} copy-done((bf16[64,4096]{1,0:T(8,128)(2,1)S(1)}, bf16[64,4096]{1,0:T(8,128)(2,1)}, u32[]{:S(2)}) %copy-start) | copy-done | bytes 524312
  10.3 0.0 copy-start.1
  10.3 1.0 %copy-done.1 = bf16[272,512]{1,0:T(8,128)(2,1)S(1)} copy-done((bf16[272,512]{1,0:T(8,128)(2,1)S(1)}, bf16[272,512]{1,0:T(8,128)(2,1)}, u32[]{:S(2)}) %copy-start.1) | copy-done | bytes 278552
  11.3 0.0 copy-start.2
  11.3 0.8 %copy-done.2 = bf16[64,512]{1,0:T(8,128)(2,1)S(1)} copy-done((bf16[64,512]{1,0:T(8,128)(2,1)S(1)}, bf16[64,512]{1,0:T(8,128)(2,1)}, u32[]{:S(2)}) %copy-start.2) | copy-done | bytes 65560
  12.1 0.0 copy-start.3
  12.1 0.7 copy-done.3
  12.8 0.6 shard_map.83
  13.4 0.0 collective-permute-done.1.refs_1_
  13.4 0.3 collective-permute-done.2.refs_2_
  13.7 1.6 %collective-permute-done.3.refs_3_ = bf16[64,512]{1,0:T(8,128)(2,1)S(1)} collective-permute-done((bf16[64,512]{1,0:T(8,128)(2,1)}, bf16[64,512]{1,0:T(8,128)(2,1)S(1)}, u32[]{:S(2)}, u32[]{:S(2)}) %collective-permute-start.3) | collective-permute-done | bytes 65568 | tf_op jit(solution)/shard_map/ppermute | solution.py:251
  15.3 0.0 collective-permute-done.7.refs_1_
  15.4 1.6 %collective-permute-start.8 = (bf16[544,512]{1,0:T(8,128)(2,1)S(1)}, bf16[544,512]{1,0:T(8,128)(2,1)S(1)}, u32[]{:S(2)}, u32[]{:S(2)}) collective-permute-start(bf16[544,512]{1,0:T(8,128)(2,1)S(1)} %shard_map.87.refs_0_), channel_id=1, source_target_pairs={{0,16},{4,12},{8,24},{12,4},{16,0},{20,28},{24,8},{28,20},{1,17},{... | collective-permute-start | bytes 1671176 | tf_op jit(solution)/shard_map/ppermute | solution.py:256
  17.0 0.5 collective-permute-start.4
  17.5 0.0 collective-permute-start
  17.5 2.3 %collective-permute-start.6 = (bf16[64,1024]{1,0:T(8,128)(2,1)S(1)}, bf16[64,1024]{1,0:T(8,128)(2,1)S(1)}, u32[]{:S(2)}, u32[]{:S(2)}) collective-permute-start(bf16[64,1024]{1,0:T(8,128)(2,1)S(1)} %shard_map.86), channel_id=1, source_target_pairs={{0,2},{1,3},{2,0},{3,1},{4,6},{5,7},{6,4},{7,5},{8,10},{9,11},{10,... | collective-permute-start | bytes 393224 | tf_op jit(solution)/shard_map/ppermute | solution.py:251
  19.9 3.0 %collective-permute-done.refs_3_.refs_1_ = bf16[64,1024]{1,0:T(8,128)(2,1)S(1)} collective-permute-done((bf16[64,1024]{1,0:T(8,128)(2,1)S(1)}, bf16[64,1024]{1,0:T(8,128)(2,1)S(1)}, u32[]{:S(2)}, u32[]{:S(2)}) %collective-permute-start) | collective-permute-done | bytes 131104 | tf_op jit(solution)/shard_map/ppermute | solution.py:251
  22.9 2.8 %collective-permute-done.6.refs_4_.refs_1_ = bf16[64,1024]{1,0:T(8,128)(2,1)S(1)} collective-permute-done((bf16[64,1024]{1,0:T(8,128)(2,1)S(1)}, bf16[64,1024]{1,0:T(8,128)(2,1)S(1)}, u32[]{:S(2)}, u32[]{:S(2)}) %collective-permute-start.6) | collective-permute-done | bytes 131104 | tf_op jit(solution)/shard_map/ppermute | solution.py:251
  25.7 0.0 collective-permute-done.4.refs_1_.refs_2_
  25.7 0.4 collective-permute-done.8.refs_1_
  26.0 0.0 slice-start
  26.0 0.1 shard_map.88.refs_2_.refs_3_
  26.1 0.1 collective-permute-start.9
  26.2 0.6 collective-permute-start.10
  26.8 1.4 %collective-permute-start.5 = (bf16[512,512]{1,0:T(8,128)(2,1)S(1)}, bf16[512,512]{1,0:T(8,128)(2,1)S(1)}, u32[]{:S(2)}, u32[]{:S(2)}) collective-permute-start(bf16[512,512]{1,0:T(8,128)(2,1)S(1)} %shard_map.85.refs_4_.refs_5_), channel_id=1, source_target_pairs={{0,16},{4,12},{8,24},{12,4},{16,0},{20,28},{24,8},{28,20},{1,17},{... | collective-permute-start | bytes 1572872 | tf_op jit(solution)/shard_map/ppermute | solution.py:256
  28.2 2.2 %collective-permute-start.11 = (bf16[64,1024]{1,0:T(8,128)(2,1)S(1)}, bf16[64,1024]{1,0:T(8,128)(2,1)S(1)}, u32[]{:S(2)}, u32[]{:S(2)}) collective-permute-start(bf16[64,1024]{1,0:T(8,128)(2,1)S(1)} %shard_map.90), channel_id=1, source_target_pairs={{0,3},{1,2},{2,1},{3,0},{4,7},{5,6},{6,5},{7,4},{8,11},{9,10},{10,... | collective-permute-start | bytes 393224 | tf_op jit(solution)/shard_map/ppermute | solution.py:251
  30.4 0.0 collective-permute-done.10.refs_5_.refs_6_
  30.4 0.0 collective-permute-done.9.refs_3_.refs_4_
  30.4 0.0 slice-start.1
  30.4 3.1 %shard_map.89 = (f32[2,256,256]{2,1,0:T(8,128)S(1)}, f32[2,256,128]{2,1,0:T(8,128)S(1)}) custom-call(s32[2,128]{1,0:T(2,128)S(1)} %get-tuple-element.29.refs_0_, bf16[64,1024]{1,0:T(8,128)(2,1)S(1)} %collective-permute-done.6.refs_4_.refs_1_, bf16[1088,512]{1,0:T(8,128)(2,1)S(1)} %shard_map.88.refs_2_.refs_3_, ...), custom_call_target="tpu_custom_call" | custom-call | flops 3221225472 | bytes 3145728 | tf_op jit(solution)/shard_map/pallas_call | solution.py:36
  33.5 1.6 %collective-permute-done.11.refs_2_.refs_1_ = bf16[64,1024]{1,0:T(8,128)(2,1)S(1)} collective-permute-done((bf16[64,1024]{1,0:T(8,128)(2,1)S(1)}, bf16[64,1024]{1,0:T(8,128)(2,1)S(1)}, u32[]{:S(2)}, u32[]{:S(2)}) %collective-permute-start.11) | collective-permute-done | bytes 131104 | tf_op jit(solution)/shard_map/ppermute | solution.py:251
  35.1 0.9 %collective-permute-done.5.refs_0_ = bf16[512,512]{1,0:T(8,128)(2,1)S(1)} collective-permute-done((bf16[512,512]{1,0:T(8,128)(2,1)S(1)}, bf16[512,512]{1,0:T(8,128)(2,1)S(1)}, u32[]{:S(2)}, u32[]{:S(2)}) %collective-permute-start.5) | collective-permute-done | bytes 524320 | tf_op jit(solution)/shard_map/ppermute | solution.py:256
  36.0 0.1 collective-permute-start.12
  36.1 1.9 %collective-permute-done.12.refs_3_.refs_4_ = bf16[512,512]{1,0:T(8,128)(2,1)S(1)} collective-permute-done((bf16[512,512]{1,0:T(8,128)(2,1)S(1)}, bf16[512,512]{1,0:T(8,128)(2,1)S(1)}, u32[]{:S(2)}, u32[]{:S(2)}) %collective-permute-start.12) | collective-permute-done | bytes 524320 | tf_op jit(solution)/shard_map/ppermute | solution.py:251
  38.0 0.0 slice-done
  38.0 0.0 slice-done.1
  38.0 3.0 %shard_map.92.refs_6_ = bf16[64,4096]{1,0:T(8,128)(2,1)S(1)} custom-call(s32[2,128]{1,0:T(2,128)S(1)} %get-tuple-element.29.refs_0_, bf16[64,1024]{1,0:T(8,128)(2,1)S(1)} %collective-permute-done.6.refs_4_.refs_1_, bf16[512,512]{1,0:T(8,128)(2,1)S(1)} %shard_map.91.refs_2_.refs_3_, bf16[512,512]{1,0:T(8,128)(2,1)S(1)} %collective-permute-done.12.refs_3_.refs_4_, ...), custom_call_target="tpu_custom_call" | custom-call | flops 3221225472 | bytes 1048576 | tf_op jit(solution)/shard_map/pallas_call | solution.py:36
  41.0 1.5 %collective-permute-start.15 = (bf16[64,4096]{1,0:T(8,128)(2,1)S(1)}, bf16[64,4096]{1,0:T(8,128)(2,1)S(1)}, u32[]{:S(2)}, u32[]{:S(2)}) collective-permute-start(bf16[64,4096]{1,0:T(8,128)(2,1)S(1)} %shard_map.92.refs_6_), channel_id=1, source_target_pairs={{0,1},{1,3},{2,0},{3,2},{4,5},{5,7},{6,4},{7,6},{8,9},{9,11},{10,8... | collective-permute-start | bytes 1572872 | tf_op jit(solution)/shard_map/ppermute | solution.py:266
  42.4 3.1 %shard_map.93 = (f32[2,256,256]{2,1,0:T(8,128)S(1)}, f32[2,256,128]{2,1,0:T(8,128)S(1)}) custom-call(s32[2,128]{1,0:T(2,128)S(1)} %get-tuple-element.29.refs_0_, bf16[64,1024]{1,0:T(8,128)(2,1)S(1)} %collective-permute-done.11.refs_2_.refs_1_, bf16[1088,512]{1,0:T(8,128)(2,1)S(1)} %shard_map.88.refs_2_.refs_3_, ...), custom_call_target="tpu_custom_call" | custom-call | flops 3221225472 | bytes 3145728 | tf_op jit(solution)/shard_map/pallas_call | solution.py:36
  45.5 3.0 %shard_map.94.refs_7_.refs_0_ = bf16[64,4096]{1,0:T(8,128)(2,1)S(1)} custom-call(s32[2,128]{1,0:T(2,128)S(1)} %get-tuple-element.29.refs_0_, bf16[64,1024]{1,0:T(8,128)(2,1)S(1)} %collective-permute-done.11.refs_2_.refs_1_, bf16[512,512]{1,0:T(8,128)(2,1)S(1)} %shard_map.91.refs_2_.refs_3_, bf16[512,512]{1,0:T(8,128)(2,1)S(1)} %collective-permute-done.12.refs_3_.refs_4_, ...), custom_call_target="tpu_custom_call" | custom-call | flops 3221225472 | bytes 1048576 | tf_op jit(solution)/shard_map/pallas_call | solution.py:36
  48.5 5.0 %collective-permute-start.14 = (bf16[64,4096]{1,0:T(8,128)(2,1)S(1)}, bf16[64,4096]{1,0:T(8,128)(2,1)S(1)}, u32[]{:S(2)}, u32[]{:S(2)}) collective-permute-start(bf16[64,4096]{1,0:T(8,128)(2,1)S(1)} %shard_map.94.refs_7_.refs_0_), channel_id=1, source_target_pairs={{0,3},{3,0},{4,7},{7,4},{8,11},{11,8},{12,15},{15,12},{16,19},{19,... | collective-permute-start | bytes 1572872 | tf_op jit(solution)/shard_map/ppermute | solution.py:266
  53.5 5.2 %shard_map.95 = (f32[2,256,256]{2,1,0:T(8,128)S(1)}, f32[2,256,128]{2,1,0:T(8,128)S(1)}, f32[2,256,256]{2,1,0:T(8,128)S(1)}, f32[2,256,128]{2,1,0:T(8,128)S(1)}) custom-call(s32[2,128]{1,0:T(2,128)S(1)} %get-tuple-element.29.refs_0_, bf16[64,1024]{1,0:T(8,128)(2,1)S(1)} %collective-permute-done.refs_3_.refs_1_, ...), custom_call_target="tpu_custom_call" | custom-call | flops 6442450944 | bytes 3145728 | tf_op jit(solution)/shard_map/pallas_call | solution.py:36
  58.7 3.6 %shard_map.96 = (bf16[64,4096]{1,0:T(8,128)(2,1)S(1)}, bf16[64,4096]{1,0:T(8,128)(2,1)S(1)}) custom-call(s32[2,128]{1,0:T(2,128)S(1)} %get-tuple-element.29.refs_0_, bf16[64,1024]{1,0:T(8,128)(2,1)S(1)} %collective-permute-done.refs_3_.refs_1_, bf16[64,1024]{1,0:T(8,128)(2,1)S(1)} %get-tuple-element.31.refs_2_, ...), custom_call_target="tpu_custom_call" | custom-call | flops 6442450944 | bytes 1048576 | tf_op jit(solution)/shard_map/pallas_call | solution.py:36
  62.3 0.1 collective-permute-start.13
  62.4 0.0 collective-permute-done.15.refs_1_.refs_4_
  62.4 0.1 shard_map.97
  62.5 0.7 collective-permute-start.16
  63.2 16.5 %collective-permute-done.13.refs_1_ = bf16[64,4096]{1,0:T(8,128)(2,1)S(1)} collective-permute-done((bf16[64,4096]{1,0:T(8,128)(2,1)S(1)}, bf16[64,4096]{1,0:T(8,128)(2,1)S(1)}, u32[]{:S(2)}, u32[]{:S(2)}) %collective-permute-start.13) | collective-permute-done | bytes 524320 | tf_op jit(solution)/shard_map/ppermute | solution.py:266
  79.7 0.0 collective-permute-done.14.refs_2_
  79.7 0.0 collective-permute-done.16.refs_3_
  79.7 1.1 %shard_map.98 = bf16[64,4096]{1,0:T(8,128)(2,1)} custom-call(bf16[64,4096]{1,0:T(8,128)(2,1)S(1)} %get-tuple-element.47.refs_0_, bf16[64,4096]{1,0:T(8,128)(2,1)S(1)} %collective-permute-done.13.refs_1_, bf16[64,4096]{1,0:T(8,128)(2,1)S(1)} %collective-permute-done.14.refs_2_, bf16[64,4096]{1,0:T(8,128)(2,1)S(1)} %collective-permute-done.16.refs_3_, ...), custom_call_target="tpu_custom_call" | custom-call | tf_op jit(solution)/shard_map/pallas_call | solution.py:36
  (7 shorter events, 0.1 us)
Async XLA Ops:
  1.9 13.4 %collective-permute-start.7 = (bf16[272,512]{1,0:T(8,128)(2,1)}, bf16[272,512]{1,0:T(8,128)(2,1)S(1)}, u32[]{:S(2)}, u32[]{:S(2)}) collective-permute-start(bf16[272,512]{1,0:T(8,128)(2,1)} %get-tuple-element.28.refs_3_), channel_id=1, source_target_pairs={{0,8},{4,20},{8,0},{12,28},{16,24},{20,4},{24,16},{28,12},{1,9},{5... | collective-permute-start | bytes 835592 | tf_op jit(solution)/shard_map/ppermute | solution.py:256
  4.9 8.5 %collective-permute-start.1 = (bf16[64,512]{1,0:T(8,128)(2,1)}, bf16[64,512]{1,0:T(8,128)(2,1)S(1)}, u32[]{:S(2)}, u32[]{:S(2)}) collective-permute-start(bf16[64,512]{1,0:T(8,128)(2,1)} %get-tuple-element.33), channel_id=1, source_target_pairs={{0,1},{1,0},{2,3},{3,2},{4,5},{5,4},{6,7},{7,6},{8,9},{9,8},{10,11... | collective-permute-start | bytes 196616 | tf_op jit(solution)/shard_map/ppermute | solution.py:251
  6.5 7.2 %collective-permute-start.2 = (bf16[64,512]{1,0:T(8,128)(2,1)}, bf16[64,512]{1,0:T(8,128)(2,1)S(1)}, u32[]{:S(2)}, u32[]{:S(2)}) collective-permute-start(bf16[64,512]{1,0:T(8,128)(2,1)} %get-tuple-element.34), channel_id=1, source_target_pairs={{0,2},{1,3},{2,0},{3,1},{4,6},{5,7},{6,4},{7,5},{8,10},{9,11},{10,... | collective-permute-start | bytes 196616 | tf_op jit(solution)/shard_map/ppermute | solution.py:251
  9.1 6.3 %collective-permute-start.3 = (bf16[64,512]{1,0:T(8,128)(2,1)}, bf16[64,512]{1,0:T(8,128)(2,1)S(1)}, u32[]{:S(2)}, u32[]{:S(2)}) collective-permute-start(bf16[64,512]{1,0:T(8,128)(2,1)} %get-tuple-element.35), channel_id=1, source_target_pairs={{0,3},{1,2},{2,1},{3,0},{4,7},{5,6},{6,5},{7,4},{8,11},{9,10},{10,... | collective-permute-start | bytes 196616 | tf_op jit(solution)/shard_map/ppermute | solution.py:251
  9.3 1.0 %copy-start = (bf16[64,4096]{1,0:T(8,128)(2,1)S(1)}, bf16[64,4096]{1,0:T(8,128)(2,1)}, u32[]{:S(2)}) copy-start(bf16[64,4096]{1,0:T(8,128)(2,1)} %refs_1_.3) | copy-start | bytes 1572868
  10.3 1.0 %copy-start.1 = (bf16[272,512]{1,0:T(8,128)(2,1)S(1)}, bf16[272,512]{1,0:T(8,128)(2,1)}, u32[]{:S(2)}) copy-start(bf16[272,512]{1,0:T(8,128)(2,1)} %get-tuple-element.28.refs_3_) | copy-start | bytes 835588
  11.3 0.8 %copy-start.2 = (bf16[64,512]{1,0:T(8,128)(2,1)S(1)}, bf16[64,512]{1,0:T(8,128)(2,1)}, u32[]{:S(2)}) copy-start(bf16[64,512]{1,0:T(8,128)(2,1)} %get-tuple-element.27.refs_2_) | copy-start | bytes 196612
  12.1 0.7 copy-start.3
  15.4 10.6 %collective-permute-start.8 = (bf16[544,512]{1,0:T(8,128)(2,1)S(1)}, bf16[544,512]{1,0:T(8,128)(2,1)S(1)}, u32[]{:S(2)}, u32[]{:S(2)}) collective-permute-start(bf16[544,512]{1,0:T(8,128)(2,1)S(1)} %shard_map.87.refs_0_), channel_id=1, source_target_pairs={{0,16},{4,12},{8,24},{12,4},{16,0},{20,28},{24,8},{28,20},{1,17},{... | collective-permute-start | bytes 1671176 | tf_op jit(solution)/shard_map/ppermute | solution.py:256
  17.0 8.7 %collective-permute-start.4 = (bf16[256,512]{1,0:T(8,128)(2,1)S(1)}, bf16[256,512]{1,0:T(8,128)(2,1)S(1)}, u32[]{:S(2)}, u32[]{:S(2)}) collective-permute-start(bf16[256,512]{1,0:T(8,128)(2,1)S(1)} %shard_map.84.refs_0_.refs_1_.refs_2_), channel_id=1, source_target_pairs={{0,8},{4,20},{8,0},{12,28},{16,24},{20,4},{24,16},{28,12},{1,9},{5... | collective-permute-start | bytes 786440 | tf_op jit(solution)/shard_map/ppermute | solution.py:256
  17.5 5.4 %collective-permute-start = (bf16[64,1024]{1,0:T(8,128)(2,1)S(1)}, bf16[64,1024]{1,0:T(8,128)(2,1)S(1)}, u32[]{:S(2)}, u32[]{:S(2)}) collective-permute-start(bf16[64,1024]{1,0:T(8,128)(2,1)S(1)} %get-tuple-element.30), channel_id=1, source_target_pairs={{0,1},{1,0},{2,3},{3,2},{4,5},{5,4},{6,7},{7,6},{8,9},{9,8},{10,11... | collective-permute-start | bytes 393224 | tf_op jit(solution)/shard_map/ppermute | solution.py:251
  17.5 8.1 %collective-permute-start.6 = (bf16[64,1024]{1,0:T(8,128)(2,1)S(1)}, bf16[64,1024]{1,0:T(8,128)(2,1)S(1)}, u32[]{:S(2)}, u32[]{:S(2)}) collective-permute-start(bf16[64,1024]{1,0:T(8,128)(2,1)S(1)} %shard_map.86), channel_id=1, source_target_pairs={{0,2},{1,3},{2,0},{3,1},{4,6},{5,7},{6,4},{7,5},{8,10},{9,11},{10,... | collective-permute-start | bytes 393224 | tf_op jit(solution)/shard_map/ppermute | solution.py:251
  26.0 12.0 %slice-start = ((s8[8388608]{0:T(1024)(128)(4,1)}), s8[4194304]{0:T(1024)(128)(4,1)S(1)}, s32[]{:S(2)}) async-start(s8[8388608]{0:T(1024)(128)(4,1)} %bitcast), calls=%async_computation | async-start | bytes 8388608
  26.1 4.3 %collective-permute-start.9 = (bf16[1088,512]{1,0:T(8,128)(2,1)S(1)}, bf16[1088,512]{1,0:T(8,128)(2,1)S(1)}, u32[]{:S(2)}, u32[]{:S(2)}) collective-permute-start(bf16[1088,512]{1,0:T(8,128)(2,1)S(1)} %shard_map.88.refs_2_.refs_3_), channel_id=1, source_target_pairs={{0,4},{4,0},{8,12},{12,8},{16,20},{20,16},{24,28},{28,24},{1,5},{5... | collective-permute-start | bytes 3342344 | tf_op jit(solution)/shard_map/ppermute | solution.py:251
  26.2 4.2 %collective-permute-start.10 = (bf16[512,512]{1,0:T(8,128)(2,1)S(1)}, bf16[512,512]{1,0:T(8,128)(2,1)S(1)}, u32[]{:S(2)}, u32[]{:S(2)}) collective-permute-start(bf16[512,512]{1,0:T(8,128)(2,1)S(1)} %shard_map.85.refs_4_.refs_5_), channel_id=1, source_target_pairs={{0,4},{4,0},{8,12},{12,8},{16,20},{20,16},{24,28},{28,24},{1,5},{5... | collective-permute-start | bytes 1572872 | tf_op jit(solution)/shard_map/ppermute | solution.py:251
  26.8 9.2 %collective-permute-start.5 = (bf16[512,512]{1,0:T(8,128)(2,1)S(1)}, bf16[512,512]{1,0:T(8,128)(2,1)S(1)}, u32[]{:S(2)}, u32[]{:S(2)}) collective-permute-start(bf16[512,512]{1,0:T(8,128)(2,1)S(1)} %shard_map.85.refs_4_.refs_5_), channel_id=1, source_target_pairs={{0,16},{4,12},{8,24},{12,4},{16,0},{20,28},{24,8},{28,20},{1,17},{... | collective-permute-start | bytes 1572872 | tf_op jit(solution)/shard_map/ppermute | solution.py:256
  28.2 6.9 %collective-permute-start.11 = (bf16[64,1024]{1,0:T(8,128)(2,1)S(1)}, bf16[64,1024]{1,0:T(8,128)(2,1)S(1)}, u32[]{:S(2)}, u32[]{:S(2)}) collective-permute-start(bf16[64,1024]{1,0:T(8,128)(2,1)S(1)} %shard_map.90), channel_id=1, source_target_pairs={{0,3},{1,2},{2,1},{3,0},{4,7},{5,6},{6,5},{7,4},{8,11},{9,10},{10,... | collective-permute-start | bytes 393224 | tf_op jit(solution)/shard_map/ppermute | solution.py:251
  30.4 7.6 %slice-start.1 = ((s8[8388608]{0:T(1024)(128)(4,1)}), s8[4194304]{0:T(1024)(128)(4,1)S(1)}, s32[]{:S(2)}) async-start(s8[8388608]{0:T(1024)(128)(4,1)} %bitcast), calls=%async_computation.1 | async-start | bytes 8388608
  36.0 2.0 %collective-permute-start.12 = (bf16[512,512]{1,0:T(8,128)(2,1)S(1)}, bf16[512,512]{1,0:T(8,128)(2,1)S(1)}, u32[]{:S(2)}, u32[]{:S(2)}) collective-permute-start(bf16[512,512]{1,0:T(8,128)(2,1)S(1)} %shard_map.91.refs_2_.refs_3_), channel_id=1, source_target_pairs={{0,4},{4,0},{8,12},{12,8},{16,20},{20,16},{24,28},{28,24},{1,5},{5... | collective-permute-start | bytes 1572872 | tf_op jit(solution)/shard_map/ppermute | solution.py:251
  41.0 21.4 %collective-permute-start.15 = (bf16[64,4096]{1,0:T(8,128)(2,1)S(1)}, bf16[64,4096]{1,0:T(8,128)(2,1)S(1)}, u32[]{:S(2)}, u32[]{:S(2)}) collective-permute-start(bf16[64,4096]{1,0:T(8,128)(2,1)S(1)} %shard_map.92.refs_6_), channel_id=1, source_target_pairs={{0,1},{1,3},{2,0},{3,2},{4,5},{5,7},{6,4},{7,6},{8,9},{9,11},{10,8... | collective-permute-start | bytes 1572872 | tf_op jit(solution)/shard_map/ppermute | solution.py:266
  48.5 31.2 %collective-permute-start.14 = (bf16[64,4096]{1,0:T(8,128)(2,1)S(1)}, bf16[64,4096]{1,0:T(8,128)(2,1)S(1)}, u32[]{:S(2)}, u32[]{:S(2)}) collective-permute-start(bf16[64,4096]{1,0:T(8,128)(2,1)S(1)} %shard_map.94.refs_7_.refs_0_), channel_id=1, source_target_pairs={{0,3},{3,0},{4,7},{7,4},{8,11},{11,8},{12,15},{15,12},{16,19},{19,... | collective-permute-start | bytes 1572872 | tf_op jit(solution)/shard_map/ppermute | solution.py:266
  62.3 17.4 %collective-permute-start.13 = (bf16[64,4096]{1,0:T(8,128)(2,1)S(1)}, bf16[64,4096]{1,0:T(8,128)(2,1)S(1)}, u32[]{:S(2)}, u32[]{:S(2)}) collective-permute-start(bf16[64,4096]{1,0:T(8,128)(2,1)S(1)} %get-tuple-element.48), channel_id=1, source_target_pairs={{0,1},{1,0},{2,3},{3,2},{4,5},{5,4},{6,7},{7,6},{8,9},{9,8},{10,11... | collective-permute-start | bytes 1572872 | tf_op jit(solution)/shard_map/ppermute | solution.py:266
  62.5 17.2 %collective-permute-start.16 = (bf16[64,4096]{1,0:T(8,128)(2,1)S(1)}, bf16[64,4096]{1,0:T(8,128)(2,1)S(1)}, u32[]{:S(2)}, u32[]{:S(2)}) collective-permute-start(bf16[64,4096]{1,0:T(8,128)(2,1)S(1)} %shard_map.97), channel_id=1, source_target_pairs={{1,2},{2,1},{5,6},{6,5},{9,10},{10,9},{13,14},{14,13},{17,18},{18,... | collective-permute-start | bytes 1572872 | tf_op jit(solution)/shard_map/ppermute | solution.py:266

commit v5 on v4

--- a/solution.py
+++ b/solution.py
@@ -271,7 +271,8 @@
     first = send(next_inner, [(0, 1), (1, 3), (2, 0), (3, 2)])
     far, = part((3,), next_inner)
     ends = send(far, [(0, 3), (3, 0)])
-    near, own = part((1, 0), far)
+    near, = part((1,), far)
+    own, = part((0,), near)
     near = send(near, [(0, 1), (1, 0), (2, 3), (3, 2)])
     middle = send(add([far, first]), [(1, 2), (2, 1)])
     return add([own, near, ends, middle], [first])
@@ -311,10 +312,10 @@
         query[x] = swap(stack([query[x]], fresh) if x > 1 else query[x], "head", x)
     square = n_ctx == 8 and n_head == 4
     if square:
-        pair = stack([cache, leg(sent, True)], fresh)
-        far = leg(pair, False)
+        beside, across = leg(sent, True), leg(sent, False)
+        corner = leg(stack([beside], fresh), False)
         got = leg(fresh, True)
-        cache = stack([pair, far], got, *query[1:3])
+        cache = stack([cache, beside, across, corner], got, *query[1:3])
         cache = [cache, swap(cache, "ctx", 1)]
         fresh = stack([fresh, got])
         early, late = [fresh, swap(fresh, "ctx", 1)], [leg(fresh, False)]
@@ -367,7 +368,7 @@
         todo = tuple(x for x in xs if x not in state)
         if todo:
             first(todo, *after)
-        return part(xs)
+        return part(xs, *after)
 
     return scatter_line(chunks) if square else scatter_direct(chunks, n_head)
 

time: 81.2 us -> 79.5 us (0.979)
  waiting for transfers between devices: 29 us -> 23.3 us
  Pallas kernels: 25 us -> 28.3 us
    pallas_call x17 -> x19, Pallas kernels: 25 us -> 28.3 us  [call(): pl.pallas_call(body, out_shape=outs, in_specs=specs + [pl.BlockSpec(memor...]
    ppermute x4, waiting for transfers between devices: 16.5 us -> 13.5 us  [send(): return lax.ppermute(value, 'head', pairs)]
    ppermute x9, waiting for transfers between devices: 11.2 us -> 9.21 us  [swap(): lax.ppermute(value, axis, [(i, i ^ mask) for i in range(lax.axis_size(axi...]
    ppermute x4 -> x5, starting transfers between devices: 6.44 us -> 8.32 us  [leg(): lax.ppermute(block, 'ctx', [(i, i ^ (odd if i % 2 else even)) for i in ra...]
    ppermute x4, starting transfers between devices: 7.17 us -> 5.44 us  [send(): return lax.ppermute(value, 'head', pairs)]
  transfers between devices with their start and end apart: 17 -> 18, of which waited for: 9 -> 8; matrix products, arithmetic and copies ran while one was open for 0% -> 0% of each run, Pallas kernels for 23% -> 28%
where the time goes in v5:
time: 79.5 us; the launch traced here: 79.2 us
  Pallas kernels  28.3 us (36%)
  starting transfers between devices  23.9 us (30%)
  waiting for transfers between devices  23.3 us (29%)
  local copies, waits for them, and re-layouts  3.5 us (4%)
    pallas_call x19, Pallas kernels, call(): pl.pallas_call(body, out_shape=outs, in_specs=specs + [pl.BlockSpec(memor...  28.3 us
    ppermute x4, waiting for transfers between devices, send(): return lax.ppermute(value, 'head', pairs)  13.5 us
    ppermute x9, starting transfers between devices, swap(): lax.ppermute(value, axis, [(i, i ^ mask) for i in range(lax.axis_size(axi...  10.2 us
    ppermute x9, waiting for transfers between devices, swap(): lax.ppermute(value, axis, [(i, i ^ mask) for i in range(lax.axis_size(axi...  9.21 us
    ppermute x5, starting transfers between devices, leg(): lax.ppermute(block, 'ctx', [(i, i ^ (odd if i % 2 else even)) for i in ra...  8.32 us
    ppermute x4, starting transfers between devices, send(): return lax.ppermute(value, 'head', pairs)  5.44 us
    unnamed x12, local copies, waits for them, and re-layouts  3.5 us
  transfers between devices with their start and end apart: 18, of which 8 were waited for; matrix products, arithmetic and copies ran while one was open for 0% of the time, Pallas kernels for 28%

profile of v5, /device:TPU:0, one launch (start us, length us, event | category | flops | bytes accessed | tf_op | source)
XLA Modules:
  0.0 79.2 jit_solution(11938233911782549862)
XLA Ops:
  0.0 1.9 %shard_map.82 = (bf16[64,512]{1,0:T(8,128)(2,1)}, bf16[64,512]{1,0:T(8,128)(2,1)}, bf16[64,512]{1,0:T(8,128)(2,1)}, bf16[64,512]{1,0:T(8,128)(2,1)}, bf16[272,512]{1,0:T(8,128)(2,1)}) custom-call(s32[16]{0:T(128)} %refs_0_.2, bf16[64,1024]{1,0:T(8,128)(2,1)} %refs_1_.2, bf16[64,1024]{1,0:T(8,128)(2,1)} %refs_2_.1, bf16[256,256]{1,0:T(8,128)(2,1)} %refs_3_.1, ...), custom_call_target="tpu_custom_call" | custom-call | tf_op jit(solution)/shard_map/pallas_call | solution.py:36
  1.9 2.9 %collective-permute-start.6 = (bf16[272,512]{1,0:T(8,128)(2,1)}, bf16[272,512]{1,0:T(8,128)(2,1)S(1)}, u32[]{:S(2)}, u32[]{:S(2)}) collective-permute-start(bf16[272,512]{1,0:T(8,128)(2,1)} %get-tuple-element.26.refs_3_), channel_id=1, source_target_pairs={{0,8},{4,20},{8,0},{12,28},{16,24},{20,4},{24,16},{28,12},{1,9},{5... | collective-permute-start | bytes 835592 | tf_op jit(solution)/shard_map/ppermute | solution.py:256
  4.9 1.6 %collective-permute-start = (bf16[64,512]{1,0:T(8,128)(2,1)}, bf16[64,512]{1,0:T(8,128)(2,1)S(1)}, u32[]{:S(2)}, u32[]{:S(2)}) collective-permute-start(bf16[64,512]{1,0:T(8,128)(2,1)} %get-tuple-element.30), channel_id=1, source_target_pairs={{0,1},{1,0},{2,3},{3,2},{4,5},{5,4},{6,7},{7,6},{8,9},{9,8},{10,11... | collective-permute-start | bytes 196616 | tf_op jit(solution)/shard_map/ppermute | solution.py:251
  6.5 2.6 %collective-permute-start.1 = (bf16[64,512]{1,0:T(8,128)(2,1)}, bf16[64,512]{1,0:T(8,128)(2,1)S(1)}, u32[]{:S(2)}, u32[]{:S(2)}) collective-permute-start(bf16[64,512]{1,0:T(8,128)(2,1)} %get-tuple-element.31), channel_id=1, source_target_pairs={{0,2},{1,3},{2,0},{3,1},{4,6},{5,7},{6,4},{7,5},{8,10},{9,11},{10,... | collective-permute-start | bytes 196616 | tf_op jit(solution)/shard_map/ppermute | solution.py:251
  9.1 0.2 collective-permute-start.2
  9.3 1.5 %collective-permute-start.7 = (bf16[272,512]{1,0:T(8,128)(2,1)}, bf16[272,512]{1,0:T(8,128)(2,1)S(1)}, u32[]{:S(2)}, u32[]{:S(2)}) collective-permute-start(bf16[272,512]{1,0:T(8,128)(2,1)} %get-tuple-element.26.refs_3_), channel_id=1, source_target_pairs={{0,16},{4,12},{8,24},{12,4},{16,0},{20,28},{24,8},{28,20},{1,17},{... | collective-permute-start | bytes 835592 | tf_op jit(solution)/shard_map/ppermute | solution.py:256
  10.8 0.0 copy-start
  10.8 1.0 %copy-done = bf16[64,4096]{1,0:T(8,128)(2,1)S(1)} copy-done((bf16[64,4096]{1,0:T(8,128)(2,1)S(1)}, bf16[64,4096]{1,0:T(8,128)(2,1)}, u32[]{:S(2)}) %copy-start) | copy-done | bytes 524312
  11.8 0.0 copy-start.1
  11.8 1.0 %copy-done.1 = bf16[272,512]{1,0:T(8,128)(2,1)S(1)} copy-done((bf16[272,512]{1,0:T(8,128)(2,1)S(1)}, bf16[272,512]{1,0:T(8,128)(2,1)}, u32[]{:S(2)}) %copy-start.1) | copy-done | bytes 278552
  12.8 0.0 copy-start.2
  12.8 0.8 %copy-done.2 = bf16[64,512]{1,0:T(8,128)(2,1)S(1)} copy-done((bf16[64,512]{1,0:T(8,128)(2,1)S(1)}, bf16[64,512]{1,0:T(8,128)(2,1)}, u32[]{:S(2)}) %copy-start.2) | copy-done | bytes 65560
  13.6 0.0 copy-start.3
  13.6 0.7 copy-done.3
  14.3 0.6 shard_map.83
  14.9 0.0 collective-permute-done.refs_1_
  14.9 0.0 collective-permute-done.1.refs_2_
  14.9 0.4 collective-permute-done.2.refs_3_
  15.3 0.0 collective-permute-done.6.refs_0_.refs_1_
  15.4 1.6 %collective-permute-start.8 = (bf16[272,512]{1,0:T(8,128)(2,1)S(1)}, bf16[272,512]{1,0:T(8,128)(2,1)S(1)}, u32[]{:S(2)}, u32[]{:S(2)}) collective-permute-start(bf16[272,512]{1,0:T(8,128)(2,1)S(1)} %shard_map.87), channel_id=1, source_target_pairs={{0,16},{4,12},{8,24},{12,4},{16,0},{20,28},{24,8},{28,20},{1,17},{... | collective-permute-start | bytes 835592 | tf_op jit(solution)/shard_map/ppermute | solution.py:256
  17.0 0.5 collective-permute-start.3
  17.5 0.0 collective-permute-start.9
  17.5 2.8 %collective-permute-start.5 = (bf16[64,1024]{1,0:T(8,128)(2,1)S(1)}, bf16[64,1024]{1,0:T(8,128)(2,1)S(1)}, u32[]{:S(2)}, u32[]{:S(2)}) collective-permute-start(bf16[64,1024]{1,0:T(8,128)(2,1)S(1)} %shard_map.86), channel_id=1, source_target_pairs={{0,2},{1,3},{2,0},{3,1},{4,6},{5,7},{6,4},{7,5},{8,10},{9,11},{10,... | collective-permute-start | bytes 393224 | tf_op jit(solution)/shard_map/ppermute | solution.py:251
  20.3 2.5 %collective-permute-done.9.refs_5_.refs_1_ = bf16[64,1024]{1,0:T(8,128)(2,1)S(1)} collective-permute-done((bf16[64,1024]{1,0:T(8,128)(2,1)S(1)}, bf16[64,1024]{1,0:T(8,128)(2,1)S(1)}, u32[]{:S(2)}, u32[]{:S(2)}) %collective-permute-start.9) | collective-permute-done | bytes 131104 | tf_op jit(solution)/shard_map/ppermute | solution.py:251
  22.9 2.8 %collective-permute-done.5.refs_6_.refs_1_ = bf16[64,1024]{1,0:T(8,128)(2,1)S(1)} collective-permute-done((bf16[64,1024]{1,0:T(8,128)(2,1)S(1)}, bf16[64,1024]{1,0:T(8,128)(2,1)S(1)}, u32[]{:S(2)}, u32[]{:S(2)}) %collective-permute-start.5) | collective-permute-done | bytes 131104 | tf_op jit(solution)/shard_map/ppermute | solution.py:251
  25.6 0.0 collective-permute-done.7.refs_2_
  25.6 0.0 collective-permute-done.3.refs_1_.refs_4_
  25.6 0.0 collective-permute-done.8.refs_3_
  25.7 0.0 slice-start
  25.7 0.1 shard_map.88.refs_2_
  25.8 0.1 collective-permute-start.10
  25.9 0.6 collective-permute-start.11
  26.4 1.7 %collective-permute-start.4 = (bf16[512,512]{1,0:T(8,128)(2,1)S(1)}, bf16[512,512]{1,0:T(8,128)(2,1)S(1)}, u32[]{:S(2)}, u32[]{:S(2)}) collective-permute-start(bf16[512,512]{1,0:T(8,128)(2,1)S(1)} %shard_map.85.refs_4_), channel_id=1, source_target_pairs={{0,16},{4,12},{8,24},{12,4},{16,0},{20,28},{24,8},{28,20},{1,17},{... | collective-permute-start | bytes 1572872 | tf_op jit(solution)/shard_map/ppermute | solution.py:256
  28.2 2.2 %collective-permute-start.12 = (bf16[64,1024]{1,0:T(8,128)(2,1)S(1)}, bf16[64,1024]{1,0:T(8,128)(2,1)S(1)}, u32[]{:S(2)}, u32[]{:S(2)}) collective-permute-start(bf16[64,1024]{1,0:T(8,128)(2,1)S(1)} %shard_map.90), channel_id=1, source_target_pairs={{0,3},{1,2},{2,1},{3,0},{4,7},{5,6},{6,5},{7,4},{8,11},{9,10},{10,... | collective-permute-start | bytes 393224 | tf_op jit(solution)/shard_map/ppermute | solution.py:251
  30.4 0.0 collective-permute-done.11.refs_5_
  30.4 0.0 collective-permute-done.10.refs_3_
  30.4 0.0 slice-start.1
  30.4 3.1 %shard_map.89 = (f32[2,256,256]{2,1,0:T(8,128)S(1)}, f32[2,256,128]{2,1,0:T(8,128)S(1)}) custom-call(s32[2,128]{1,0:T(2,128)S(1)} %get-tuple-element.27.refs_0_, bf16[64,1024]{1,0:T(8,128)(2,1)S(1)} %collective-permute-done.5.refs_6_.refs_1_, bf16[1088,512]{1,0:T(8,128)(2,1)S(1)} %shard_map.88.refs_2_, ...), custom_call_target="tpu_custom_call" | custom-call | flops 3221225472 | bytes 3145728 | tf_op jit(solution)/shard_map/pallas_call | solution.py:36
  33.5 1.6 %collective-permute-done.12.refs_2_.refs_1_ = bf16[64,1024]{1,0:T(8,128)(2,1)S(1)} collective-permute-done((bf16[64,1024]{1,0:T(8,128)(2,1)S(1)}, bf16[64,1024]{1,0:T(8,128)(2,1)S(1)}, u32[]{:S(2)}, u32[]{:S(2)}) %collective-permute-start.12) | collective-permute-done | bytes 131104 | tf_op jit(solution)/shard_map/ppermute | solution.py:251
  35.1 0.5 collective-permute-done.4.refs_0_
  35.7 0.1 collective-permute-start.13
  35.7 1.9 %collective-permute-done.13.refs_3_ = bf16[512,512]{1,0:T(8,128)(2,1)S(1)} collective-permute-done((bf16[512,512]{1,0:T(8,128)(2,1)S(1)}, bf16[512,512]{1,0:T(8,128)(2,1)S(1)}, u32[]{:S(2)}, u32[]{:S(2)}) %collective-permute-start.13) | collective-permute-done | bytes 524320 | tf_op jit(solution)/shard_map/ppermute | solution.py:251
  37.6 0.0 slice-done
  37.6 0.0 slice-done.1
  37.6 3.0 %shard_map.92.refs_6_.refs_7_ = bf16[64,4096]{1,0:T(8,128)(2,1)S(1)} custom-call(s32[2,128]{1,0:T(2,128)S(1)} %get-tuple-element.27.refs_0_, bf16[64,1024]{1,0:T(8,128)(2,1)S(1)} %collective-permute-done.5.refs_6_.refs_1_, bf16[512,512]{1,0:T(8,128)(2,1)S(1)} %shard_map.91.refs_2_, bf16[512,512]{1,0:T(8,128)(2,1)S(1)} %collective-permute-done.13.refs_3_, ...), custom_call_target="tpu_custom_call" | custom-call | flops 3221225472 | bytes 1048576 | tf_op jit(solution)/shard_map/pallas_call | solution.py:36
  40.6 0.3 collective-permute-start.16
  40.9 3.1 %shard_map.93 = (f32[2,256,256]{2,1,0:T(8,128)S(1)}, f32[2,256,128]{2,1,0:T(8,128)S(1)}) custom-call(s32[2,128]{1,0:T(2,128)S(1)} %get-tuple-element.27.refs_0_, bf16[64,1024]{1,0:T(8,128)(2,1)S(1)} %collective-permute-done.12.refs_2_.refs_1_, bf16[1088,512]{1,0:T(8,128)(2,1)S(1)} %shard_map.88.refs_2_, ...), custom_call_target="tpu_custom_call" | custom-call | flops 3221225472 | bytes 3145728 | tf_op jit(solution)/shard_map/pallas_call | solution.py:36
  44.0 3.0 %shard_map.94.refs_6_.refs_7_.refs_0_ = bf16[64,4096]{1,0:T(8,128)(2,1)S(1)} custom-call(s32[2,128]{1,0:T(2,128)S(1)} %get-tuple-element.27.refs_0_, bf16[64,1024]{1,0:T(8,128)(2,1)S(1)} %collective-permute-done.12.refs_2_.refs_1_, bf16[512,512]{1,0:T(8,128)(2,1)S(1)} %shard_map.91.refs_2_, bf16[512,512]{1,0:T(8,128)(2,1)S(1)} %collective-permute-done.13.refs_3_, ...), custom_call_target="tpu_custom_call" | custom-call | flops 3221225472 | bytes 1048576 | tf_op jit(solution)/shard_map/pallas_call | solution.py:36
  47.0 4.4 %collective-permute-start.15 = (bf16[64,4096]{1,0:T(8,128)(2,1)S(1)}, bf16[64,4096]{1,0:T(8,128)(2,1)S(1)}, u32[]{:S(2)}, u32[]{:S(2)}) collective-permute-start(bf16[64,4096]{1,0:T(8,128)(2,1)S(1)} %shard_map.94.refs_6_.refs_7_.refs_0_), channel_id=1, source_target_pairs={{0,3},{3,0},{4,7},{7,4},{8,11},{11,8},{12,15},{15,12},{16,19},{19,... | collective-permute-start | bytes 1572872 | tf_op jit(solution)/shard_map/ppermute | solution.py:266
  51.4 3.1 %shard_map.95 = (f32[2,256,256]{2,1,0:T(8,128)S(1)}, f32[2,256,128]{2,1,0:T(8,128)S(1)}) custom-call(s32[2,128]{1,0:T(2,128)S(1)} %get-tuple-element.27.refs_0_, bf16[64,1024]{1,0:T(8,128)(2,1)S(1)} %collective-permute-done.9.refs_5_.refs_1_, bf16[1088,512]{1,0:T(8,128)(2,1)S(1)} %shard_map.88.refs_2_, ...), custom_call_target="tpu_custom_call" | custom-call | flops 3221225472 | bytes 3145728 | tf_op jit(solution)/shard_map/pallas_call | solution.py:36
  54.5 3.0 %shard_map.96.refs_6_.refs_7_ = bf16[64,4096]{1,0:T(8,128)(2,1)S(1)} custom-call(s32[2,128]{1,0:T(2,128)S(1)} %get-tuple-element.27.refs_0_, bf16[64,1024]{1,0:T(8,128)(2,1)S(1)} %collective-permute-done.9.refs_5_.refs_1_, bf16[512,512]{1,0:T(8,128)(2,1)S(1)} %shard_map.91.refs_2_, bf16[512,512]{1,0:T(8,128)(2,1)S(1)} %collective-permute-done.13.refs_3_, ...), custom_call_target="tpu_custom_call" | custom-call | flops 3221225472 | bytes 1048576 | tf_op jit(solution)/shard_map/pallas_call | solution.py:36
  57.5 0.1 collective-permute-start.14
  57.6 9.3 %collective-permute-done.16.refs_1_.refs_4_ = bf16[64,4096]{1,0:T(8,128)(2,1)S(1)} collective-permute-done((bf16[64,4096]{1,0:T(8,128)(2,1)S(1)}, bf16[64,4096]{1,0:T(8,128)(2,1)S(1)}, u32[]{:S(2)}, u32[]{:S(2)}) %collective-permute-start.16) | collective-permute-done | bytes 524320 | tf_op jit(solution)/shard_map/ppermute | solution.py:266
  66.8 0.1 shard_map.99
  66.9 0.7 collective-permute-start.17
  67.6 3.1 %shard_map.97 = (f32[2,256,256]{2,1,0:T(8,128)S(1)}, f32[2,256,128]{2,1,0:T(8,128)S(1)}) custom-call(s32[2,128]{1,0:T(2,128)S(1)} %get-tuple-element.27.refs_0_, bf16[64,1024]{1,0:T(8,128)(2,1)S(1)} %get-tuple-element.28.refs_1_, bf16[1088,512]{1,0:T(8,128)(2,1)S(1)} %shard_map.88.refs_2_, bf16[1088,512]{1,0:T(8,128)(2,1)S(1)} %collective-permute-done.10.refs_3_, ...), custom_call_target="tpu_custom_call" | custom-call | flops 3221225472 | bytes 3145728 | tf_op jit(solution)/shard_map/pallas_call | solution.py:36
  70.7 3.0 %shard_map.98.refs_0_ = bf16[64,4096]{1,0:T(8,128)(2,1)S(1)} custom-call(s32[2,128]{1,0:T(2,128)S(1)} %get-tuple-element.27.refs_0_, bf16[64,1024]{1,0:T(8,128)(2,1)S(1)} %get-tuple-element.28.refs_1_, bf16[512,512]{1,0:T(8,128)(2,1)S(1)} %shard_map.91.refs_2_, bf16[512,512]{1,0:T(8,128)(2,1)S(1)} %collective-permute-done.13.refs_3_, ...), custom_call_target="tpu_custom_call" | custom-call | flops 3221225472 | bytes 1048576 | tf_op jit(solution)/shard_map/pallas_call | solution.py:36
  73.7 4.3 %collective-permute-done.14.refs_1_ = bf16[64,4096]{1,0:T(8,128)(2,1)S(1)} collective-permute-done((bf16[64,4096]{1,0:T(8,128)(2,1)S(1)}, bf16[64,4096]{1,0:T(8,128)(2,1)S(1)}, u32[]{:S(2)}, u32[]{:S(2)}) %collective-permute-start.14) | collective-permute-done | bytes 524320 | tf_op jit(solution)/shard_map/ppermute | solution.py:266
  78.0 0.0 collective-permute-done.15.refs_2_
  78.0 0.0 collective-permute-done.17.refs_3_
  78.0 1.1 %shard_map.100 = bf16[64,4096]{1,0:T(8,128)(2,1)} custom-call(bf16[64,4096]{1,0:T(8,128)(2,1)S(1)} %shard_map.98.refs_0_, bf16[64,4096]{1,0:T(8,128)(2,1)S(1)} %collective-permute-done.14.refs_1_, bf16[64,4096]{1,0:T(8,128)(2,1)S(1)} %collective-permute-done.15.refs_2_, bf16[64,4096]{1,0:T(8,128)(2,1)S(1)} %collective-permute-done.17.refs_3_, ...), custom_call_target="tpu_custom_call" | custom-call | tf_op jit(solution)/shard_map/pallas_call | solution.py:36
  (7 shorter events, 0.1 us)
Async XLA Ops:
  1.9 13.4 %collective-permute-start.6 = (bf16[272,512]{1,0:T(8,128)(2,1)}, bf16[272,512]{1,0:T(8,128)(2,1)S(1)}, u32[]{:S(2)}, u32[]{:S(2)}) collective-permute-start(bf16[272,512]{1,0:T(8,128)(2,1)} %get-tuple-element.26.refs_3_), channel_id=1, source_target_pairs={{0,8},{4,20},{8,0},{12,28},{16,24},{20,4},{24,16},{28,12},{1,9},{5... | collective-permute-start | bytes 835592 | tf_op jit(solution)/shard_map/ppermute | solution.py:256
  4.9 10.0 %collective-permute-start = (bf16[64,512]{1,0:T(8,128)(2,1)}, bf16[64,512]{1,0:T(8,128)(2,1)S(1)}, u32[]{:S(2)}, u32[]{:S(2)}) collective-permute-start(bf16[64,512]{1,0:T(8,128)(2,1)} %get-tuple-element.30), channel_id=1, source_target_pairs={{0,1},{1,0},{2,3},{3,2},{4,5},{5,4},{6,7},{7,6},{8,9},{9,8},{10,11... | collective-permute-start | bytes 196616 | tf_op jit(solution)/shard_map/ppermute | solution.py:251
  6.5 8.4 %collective-permute-start.1 = (bf16[64,512]{1,0:T(8,128)(2,1)}, bf16[64,512]{1,0:T(8,128)(2,1)S(1)}, u32[]{:S(2)}, u32[]{:S(2)}) collective-permute-start(bf16[64,512]{1,0:T(8,128)(2,1)} %get-tuple-element.31), channel_id=1, source_target_pairs={{0,2},{1,3},{2,0},{3,1},{4,6},{5,7},{6,4},{7,5},{8,10},{9,11},{10,... | collective-permute-start | bytes 196616 | tf_op jit(solution)/shard_map/ppermute | solution.py:251
  9.1 6.3 %collective-permute-start.2 = (bf16[64,512]{1,0:T(8,128)(2,1)}, bf16[64,512]{1,0:T(8,128)(2,1)S(1)}, u32[]{:S(2)}, u32[]{:S(2)}) collective-permute-start(bf16[64,512]{1,0:T(8,128)(2,1)} %get-tuple-element.32), channel_id=1, source_target_pairs={{0,3},{1,2},{2,1},{3,0},{4,7},{5,6},{6,5},{7,4},{8,11},{9,10},{10,... | collective-permute-start | bytes 196616 | tf_op jit(solution)/shard_map/ppermute | solution.py:251
  9.3 16.4 %collective-permute-start.7 = (bf16[272,512]{1,0:T(8,128)(2,1)}, bf16[272,512]{1,0:T(8,128)(2,1)S(1)}, u32[]{:S(2)}, u32[]{:S(2)}) collective-permute-start(bf16[272,512]{1,0:T(8,128)(2,1)} %get-tuple-element.26.refs_3_), channel_id=1, source_target_pairs={{0,16},{4,12},{8,24},{12,4},{16,0},{20,28},{24,8},{28,20},{1,17},{... | collective-permute-start | bytes 835592 | tf_op jit(solution)/shard_map/ppermute | solution.py:256
  10.8 1.0 %copy-start = (bf16[64,4096]{1,0:T(8,128)(2,1)S(1)}, bf16[64,4096]{1,0:T(8,128)(2,1)}, u32[]{:S(2)}) copy-start(bf16[64,4096]{1,0:T(8,128)(2,1)} %refs_1_.3) | copy-start | bytes 1572868
  11.8 1.0 %copy-start.1 = (bf16[272,512]{1,0:T(8,128)(2,1)S(1)}, bf16[272,512]{1,0:T(8,128)(2,1)}, u32[]{:S(2)}) copy-start(bf16[272,512]{1,0:T(8,128)(2,1)} %get-tuple-element.26.refs_3_) | copy-start | bytes 835588
  12.8 0.8 %copy-start.2 = (bf16[64,512]{1,0:T(8,128)(2,1)S(1)}, bf16[64,512]{1,0:T(8,128)(2,1)}, u32[]{:S(2)}) copy-start(bf16[64,512]{1,0:T(8,128)(2,1)} %get-tuple-element.25.refs_2_) | copy-start | bytes 196612
  13.6 0.7 copy-start.3
  15.4 10.3 %collective-permute-start.8 = (bf16[272,512]{1,0:T(8,128)(2,1)S(1)}, bf16[272,512]{1,0:T(8,128)(2,1)S(1)}, u32[]{:S(2)}, u32[]{:S(2)}) collective-permute-start(bf16[272,512]{1,0:T(8,128)(2,1)S(1)} %shard_map.87), channel_id=1, source_target_pairs={{0,16},{4,12},{8,24},{12,4},{16,0},{20,28},{24,8},{28,20},{1,17},{... | collective-permute-start | bytes 835592 | tf_op jit(solution)/shard_map/ppermute | solution.py:256
  17.0 8.7 %collective-permute-start.3 = (bf16[256,512]{1,0:T(8,128)(2,1)S(1)}, bf16[256,512]{1,0:T(8,128)(2,1)S(1)}, u32[]{:S(2)}, u32[]{:S(2)}) collective-permute-start(bf16[256,512]{1,0:T(8,128)(2,1)S(1)} %shard_map.84.refs_0_.refs_1_), channel_id=1, source_target_pairs={{0,8},{4,20},{8,0},{12,28},{16,24},{20,4},{24,16},{28,12},{1,9},{5... | collective-permute-start | bytes 786440 | tf_op jit(solution)/shard_map/ppermute | solution.py:256
  17.5 5.4 %collective-permute-start.9 = (bf16[64,1024]{1,0:T(8,128)(2,1)S(1)}, bf16[64,1024]{1,0:T(8,128)(2,1)S(1)}, u32[]{:S(2)}, u32[]{:S(2)}) collective-permute-start(bf16[64,1024]{1,0:T(8,128)(2,1)S(1)} %get-tuple-element.35), channel_id=1, source_target_pairs={{0,1},{1,0},{2,3},{3,2},{4,5},{5,4},{6,7},{7,6},{8,9},{9,8},{10,11... | collective-permute-start | bytes 393224 | tf_op jit(solution)/shard_map/ppermute | solution.py:251
  17.5 8.1 %collective-permute-start.5 = (bf16[64,1024]{1,0:T(8,128)(2,1)S(1)}, bf16[64,1024]{1,0:T(8,128)(2,1)S(1)}, u32[]{:S(2)}, u32[]{:S(2)}) collective-permute-start(bf16[64,1024]{1,0:T(8,128)(2,1)S(1)} %shard_map.86), channel_id=1, source_target_pairs={{0,2},{1,3},{2,0},{3,1},{4,6},{5,7},{6,4},{7,5},{8,10},{9,11},{10,... | collective-permute-start | bytes 393224 | tf_op jit(solution)/shard_map/ppermute | solution.py:251
  25.7 12.0 %slice-start = ((s8[8388608]{0:T(1024)(128)(4,1)}), s8[4194304]{0:T(1024)(128)(4,1)S(1)}, s32[]{:S(2)}) async-start(s8[8388608]{0:T(1024)(128)(4,1)} %bitcast), calls=%async_computation | async-start | bytes 8388608
  25.8 4.7 %collective-permute-start.10 = (bf16[1088,512]{1,0:T(8,128)(2,1)S(1)}, bf16[1088,512]{1,0:T(8,128)(2,1)S(1)}, u32[]{:S(2)}, u32[]{:S(2)}) collective-permute-start(bf16[1088,512]{1,0:T(8,128)(2,1)S(1)} %shard_map.88.refs_2_), channel_id=1, source_target_pairs={{0,4},{4,0},{8,12},{12,8},{16,20},{20,16},{24,28},{28,24},{1,5},{5... | collective-permute-start | bytes 3342344 | tf_op jit(solution)/shard_map/ppermute | solution.py:251
  25.9 4.6 %collective-permute-start.11 = (bf16[512,512]{1,0:T(8,128)(2,1)S(1)}, bf16[512,512]{1,0:T(8,128)(2,1)S(1)}, u32[]{:S(2)}, u32[]{:S(2)}) collective-permute-start(bf16[512,512]{1,0:T(8,128)(2,1)S(1)} %shard_map.85.refs_4_), channel_id=1, source_target_pairs={{0,4},{4,0},{8,12},{12,8},{16,20},{20,16},{24,28},{28,24},{1,5},{5... | collective-permute-start | bytes 1572872 | tf_op jit(solution)/shard_map/ppermute | solution.py:251
  26.4 9.2 %collective-permute-start.4 = (bf16[512,512]{1,0:T(8,128)(2,1)S(1)}, bf16[512,512]{1,0:T(8,128)(2,1)S(1)}, u32[]{:S(2)}, u32[]{:S(2)}) collective-permute-start(bf16[512,512]{1,0:T(8,128)(2,1)S(1)} %shard_map.85.refs_4_), channel_id=1, source_target_pairs={{0,16},{4,12},{8,24},{12,4},{16,0},{20,28},{24,8},{28,20},{1,17},{... | collective-permute-start | bytes 1572872 | tf_op jit(solution)/shard_map/ppermute | solution.py:256
  28.2 6.9 %collective-permute-start.12 = (bf16[64,1024]{1,0:T(8,128)(2,1)S(1)}, bf16[64,1024]{1,0:T(8,128)(2,1)S(1)}, u32[]{:S(2)}, u32[]{:S(2)}) collective-permute-start(bf16[64,1024]{1,0:T(8,128)(2,1)S(1)} %shard_map.90), channel_id=1, source_target_pairs={{0,3},{1,2},{2,1},{3,0},{4,7},{5,6},{6,5},{7,4},{8,11},{9,10},{10,... | collective-permute-start | bytes 393224 | tf_op jit(solution)/shard_map/ppermute | solution.py:251
  30.4 7.2 %slice-start.1 = ((s8[8388608]{0:T(1024)(128)(4,1)}), s8[4194304]{0:T(1024)(128)(4,1)S(1)}, s32[]{:S(2)}) async-start(s8[8388608]{0:T(1024)(128)(4,1)} %bitcast), calls=%async_computation.1 | async-start | bytes 8388608
  35.7 2.0 %collective-permute-start.13 = (bf16[512,512]{1,0:T(8,128)(2,1)S(1)}, bf16[512,512]{1,0:T(8,128)(2,1)S(1)}, u32[]{:S(2)}, u32[]{:S(2)}) collective-permute-start(bf16[512,512]{1,0:T(8,128)(2,1)S(1)} %shard_map.91.refs_2_), channel_id=1, source_target_pairs={{0,4},{4,0},{8,12},{12,8},{16,20},{20,16},{24,28},{28,24},{1,5},{5... | collective-permute-start | bytes 1572872 | tf_op jit(solution)/shard_map/ppermute | solution.py:251
  40.6 26.2 %collective-permute-start.16 = (bf16[64,4096]{1,0:T(8,128)(2,1)S(1)}, bf16[64,4096]{1,0:T(8,128)(2,1)S(1)}, u32[]{:S(2)}, u32[]{:S(2)}) collective-permute-start(bf16[64,4096]{1,0:T(8,128)(2,1)S(1)} %shard_map.92.refs_6_.refs_7_), channel_id=1, source_target_pairs={{0,1},{1,3},{2,0},{3,2},{4,5},{5,7},{6,4},{7,6},{8,9},{9,11},{10,8... | collective-permute-start | bytes 1572872 | tf_op jit(solution)/shard_map/ppermute | solution.py:266
  47.0 31.0 %collective-permute-start.15 = (bf16[64,4096]{1,0:T(8,128)(2,1)S(1)}, bf16[64,4096]{1,0:T(8,128)(2,1)S(1)}, u32[]{:S(2)}, u32[]{:S(2)}) collective-permute-start(bf16[64,4096]{1,0:T(8,128)(2,1)S(1)} %shard_map.94.refs_6_.refs_7_.refs_0_), channel_id=1, source_target_pairs={{0,3},{3,0},{4,7},{7,4},{8,11},{11,8},{12,15},{15,12},{16,19},{19,... | collective-permute-start | bytes 1572872 | tf_op jit(solution)/shard_map/ppermute | solution.py:266
  57.5 20.5 %collective-permute-start.14 = (bf16[64,4096]{1,0:T(8,128)(2,1)S(1)}, bf16[64,4096]{1,0:T(8,128)(2,1)S(1)}, u32[]{:S(2)}, u32[]{:S(2)}) collective-permute-start(bf16[64,4096]{1,0:T(8,128)(2,1)S(1)} %shard_map.96.refs_6_.refs_7_), channel_id=1, source_target_pairs={{0,1},{1,0},{2,3},{3,2},{4,5},{5,4},{6,7},{7,6},{8,9},{9,8},{10,11... | collective-permute-start | bytes 1572872 | tf_op jit(solution)/shard_map/ppermute | solution.py:266
  66.9 11.1 %collective-permute-start.17 = (bf16[64,4096]{1,0:T(8,128)(2,1)S(1)}, bf16[64,4096]{1,0:T(8,128)(2,1)S(1)}, u32[]{:S(2)}, u32[]{:S(2)}) collective-permute-start(bf16[64,4096]{1,0:T(8,128)(2,1)S(1)} %shard_map.99), channel_id=1, source_target_pairs={{1,2},{2,1},{5,6},{6,5},{9,10},{10,9},{13,14},{14,13},{17,18},{18,... | collective-permute-start | bytes 1572872 | tf_op jit(solution)/shard_map/ppermute | solution.py:266

commit v6 on v5

--- a/solution.py
+++ b/solution.py
@@ -49,35 +49,52 @@
     return ref[:, pl.ds(pl.multiple_of(index * width, width), width)]
 
 
-def pack_kernel(pages, k_ref, v_ref, ck_ref, cv_ref, *outs):
-    *fresh, cache = outs
+def own_rows(rows, q_width, kv_width, block):
+    return [0, rows, rows + block, rows + block + rows * q_width // kv_width, 16 + rows + block + rows * q_width // kv_width]
+
+
+def pack_kernel(n_head, lengths, pages, k_ref, v_ref, q_ref, ck_ref, cv_ref, *outs):
+    fresh, query, (cache, own) = outs[:n_head - 1], outs[n_head - 1:-2], outs[-2:]
     head = lax.axis_index("head")
-    tokens, width = ck_ref.shape
-    for x, out in enumerate(fresh):
-        out[:, :width] = part_of(k_ref, head ^ x, len(fresh))
-        out[:, width:] = part_of(v_ref, head ^ x, len(fresh))
-    cache[:tokens, :width] = ck_ref[...]
-    cache[:tokens, width:] = cv_ref[...]
-    count = pages.shape[0]
-    page = iota((count, 2 * width), 0)
-    owner = jnp.zeros((count, 2 * width), jnp.int32)
+    rows, (tokens, width) = k_ref.shape[0], ck_ref.shape
+    kv_width, count = 2 * width, pages.shape[0]
+    q_width = q_ref.shape[1] // n_head
+    _, own_cache, own_query, own_ends, _ = own_rows(rows, q_width, kv_width, tokens + count)
+    page = iota((count, kv_width), 0)
+    owner = jnp.zeros((count, kv_width), jnp.int32)
     for p in range(count):
         owner = jnp.where(page == p, pages[p], owner)
-    cache[tokens:, :] = owner.astype(F32).astype(BF16)
-
-
-def stage_kernel(lengths, q_ref, fresh_ref, cache_ref, fresh, cache, ends, *query):
-    head = lax.axis_index("head")
-    for x, out in enumerate(query):
-        out[...] = part_of(q_ref, head ^ x, len(query))
-    fresh[...] = fresh_ref[...]
-    cache[...] = cache_ref[...]
-    row = iota(ends.shape, 0)
-    end, filled = 0, jnp.zeros(ends.shape, jnp.int32)
+    owner = owner.astype(F32).astype(BF16)
+    for out, start in ((cache, 0), (own, own_cache)):
+        out[start:start + tokens, :width] = ck_ref[...]
+        out[start:start + tokens, width:] = cv_ref[...]
+        out[start + tokens:start + tokens + count, :] = owner
+    for x, out in enumerate([own, *fresh]):
+        out[:rows, :width] = part_of(k_ref, head ^ x, n_head)
+        out[:rows, width:] = part_of(v_ref, head ^ x, n_head)
+    for x, out in enumerate(query, 1):
+        out[...] = part_of(q_ref, head ^ x, n_head)
+    mine = part_of(q_ref, head, n_head)
+    for i in range(q_width // kv_width):
+        own[own_query + i * rows:own_query + (i + 1) * rows, :] = mine[:, i * kv_width:(i + 1) * kv_width]
+    row, low = iota((16, kv_width), 0), iota((16, kv_width), 1) >= LANES
+    end, filled = 0, jnp.zeros((16, kv_width), jnp.int32)
     for r in range(lengths.shape[0]):
         end = end + lengths[r]
-        filled = jnp.where(row == r, end, filled)
-    ends[...] = filled
+        filled = jnp.where(row == r, jnp.where(low, end & 127, end >> 7), filled)
+    own[own_ends:, :] = filled.astype(F32).astype(BF16)
+
+
+def stage_kernel(own, fresh, cache, ends, query):
+    rows, q_width = query.shape
+    block, kv_width = cache.shape
+    _, own_cache, own_query, own_ends, _ = own_rows(rows, q_width, kv_width, block)
+    fresh[...] = own[:rows, :]
+    cache[...] = own[own_cache:own_query, :]
+    for i in range(q_width // kv_width):
+        query[:, i * kv_width:(i + 1) * kv_width] = own[own_query + i * rows:own_query + (i + 1) * rows, :]
+    digits = own[own_ends:, :].astype(F32).astype(jnp.int32)
+    ends[...] = (digits[:, :LANES] * 128 + digits[:, LANES:2 * LANES])[:ends.shape[0]]
 
 
 def stack_kernel(*refs):
@@ -136,7 +153,7 @@
     def fresh_mask(self, b, head):
         p0 = self.start_of(self.c, head)
         parts = []
-        for x in range(self.n_head):
+        for x in [0, *range(self.n_head - 1, 0, -1)]:
             position = self.start_of(self.c ^ self.step_of(b), self.h ^ x) + self.row
             other = (self.lane < len(self.ends)) & (self.request(position) != self.lane)
             later = (self.row_lane >= 0) & (position > p0 + self.row_lane)
@@ -296,20 +313,23 @@
     stacked = q_width // (groups * HD) * rows
     keys = n_ctx * tokens
 
-    *packed, sent = call(
-        pack_kernel, [shaped(rows, kv_width)] * n_head + [shaped(tokens + pages, kv_width)],
-        [page_request, fresh_keys, fresh_values, cache_keys, cache_values], room=58 * MIB,
+    own = shaped(own_rows(rows, q_width, kv_width, tokens + pages)[-1], kv_width)
+    *packed, sent, own = call(
+        functools.partial(pack_kernel, n_head),
+        [shaped(rows, kv_width)] * (n_head - 1) + [shaped(rows, q_width)] * (n_head - 1) + [shaped(tokens + pages, kv_width), own],
+        [prompt_lengths, page_request, fresh_keys, fresh_values, queries, cache_keys, cache_values], room=58 * MIB,
     )
     fresh, cache, ends, *query = call(
         stage_kernel,
         [shaped(rows, kv_width), shaped(tokens + pages, kv_width), shaped(prompt_lengths.shape[0], LANES, jnp.int32)]
-        + [shaped(rows, q_width)] * n_head,
-        [prompt_lengths, queries, packed[0], sent],
+        + [shaped(rows, q_width)],
+        [own],
     )
-
-    fresh = stack([fresh, *(swap(packed[x], "head", x) for x in range(1, n_head))])
+    query += packed[n_head - 1:]
+
+    fresh = stack([fresh, *(swap(packed[x - 1], "head", x) for x in range(n_head - 1, 0, -1))])
     for x in range(1, n_head):
-        query[x] = swap(stack([query[x]], fresh) if x > 1 else query[x], "head", x)
+        query[x] = swap(query[x], "head", x)
     square = n_ctx == 8 and n_head == 4
     if square:
         beside, across = leg(sent, True), leg(sent, False)

time: 79.5 us -> 78.6 us (0.989)
  local copies, waits for them, and re-layouts: 3.5 us -> 1.05 us
  waiting for transfers between devices: 23.3 us -> 25.1 us
    unnamed x12, local copies, waits for them, and re-layouts: 3.5 us -> 1.05 us
    ppermute x9, waiting for transfers between devices: 9.21 us -> 10.5 us  [swap(): lax.ppermute(value, axis, [(i, i ^ mask) for i in range(lax.axis_size(axi...]
    pallas_call x19 -> x17, Pallas kernels: 28.3 us -> 28.1 us  [call(): pl.pallas_call(body, out_shape=outs, in_specs=specs + [pl.BlockSpec(memor...]
  transfers between devices with their start and end apart: 18 -> 18, of which waited for: 8 -> 10; matrix products, arithmetic and copies ran while one was open for 0% -> 0% of each run, Pallas kernels for 28% -> 27%
where the time goes in v6:
time: 78.6 us; the launch traced here: 78.4 us
  Pallas kernels  28.1 us (36%)
  waiting for transfers between devices  25.1 us (32%)
  starting transfers between devices  23.9 us (30%)
  local copies, waits for them, and re-layouts  1.05 us (1%)
    pallas_call x17, Pallas kernels, call(): pl.pallas_call(body, out_shape=outs, in_specs=specs + [pl.BlockSpec(memor...  28.1 us
    ppermute x4, waiting for transfers between devices, send(): return lax.ppermute(value, 'head', pairs)  13.6 us
    ppermute x9, starting transfers between devices, swap(): lax.ppermute(value, axis, [(i, i ^ mask) for i in range(lax.axis_size(axi...  10.6 us
    ppermute x9, waiting for transfers between devices, swap(): lax.ppermute(value, axis, [(i, i ^ mask) for i in range(lax.axis_size(axi...  10.5 us
    ppermute x5, starting transfers between devices, leg(): lax.ppermute(block, 'ctx', [(i, i ^ (odd if i % 2 else even)) for i in ra...  7.99 us
    ppermute x4, starting transfers between devices, send(): return lax.ppermute(value, 'head', pairs)  5.36 us
  transfers between devices with their start and end apart: 18, of which 10 were waited for; matrix products, arithmetic and copies ran while one was open for 0% of the time, Pallas kernels for 27%

profile of v6, /device:TPU:0, one launch (start us, length us, event | category | flops | bytes accessed | tf_op | source)
XLA Modules:
  0.0 78.4 jit_solution(1612143555063018884)
XLA Ops:
  0.0 2.4 %shard_map.82 = (bf16[64,512]{1,0:T(8,128)(2,1)}, bf16[64,512]{1,0:T(8,128)(2,1)}, bf16[64,512]{1,0:T(8,128)(2,1)}, bf16[64,1024]{1,0:T(8,128)(2,1)}, bf16[64,10...) custom-call(s32[2]{0:T(128)} %refs_0_.1, s32[16]{0:T(128)} %refs_1_.1, ...), custom_call_target="tpu_custom_call" | custom-call | tf_op jit(solution)/shard_map/pallas_call | solution.py:36
  2.4 2.9 %collective-permute-start.6 = (bf16[272,512]{1,0:T(8,128)(2,1)}, bf16[272,512]{1,0:T(8,128)(2,1)S(1)}, u32[]{:S(2)}, u32[]{:S(2)}) collective-permute-start(bf16[272,512]{1,0:T(8,128)(2,1)} %get-tuple-element.34), channel_id=1, source_target_pairs={{0,8},{4,20},{8,0},{12,28},{16,24},{20,4},{24,16},{28,12},{1,9},{5... | collective-permute-start | bytes 835592 | tf_op jit(solution)/shard_map/ppermute | solution.py:273
  5.3 3.6 %collective-permute-start = (bf16[64,512]{1,0:T(8,128)(2,1)}, bf16[64,512]{1,0:T(8,128)(2,1)S(1)}, u32[]{:S(2)}, u32[]{:S(2)}) collective-permute-start(bf16[64,512]{1,0:T(8,128)(2,1)} %get-tuple-element.29), channel_id=1, source_target_pairs={{0,3},{1,2},{2,1},{3,0},{4,7},{5,6},{6,5},{7,4},{8,11},{9,10},{10,... | collective-permute-start | bytes 196616 | tf_op jit(solution)/shard_map/ppermute | solution.py:268
  8.9 0.0 collective-permute-start.1
  8.9 0.8 collective-permute-start.2
  9.7 1.5 %collective-permute-start.7 = (bf16[272,512]{1,0:T(8,128)(2,1)}, bf16[272,512]{1,0:T(8,128)(2,1)S(1)}, u32[]{:S(2)}, u32[]{:S(2)}) collective-permute-start(bf16[272,512]{1,0:T(8,128)(2,1)} %get-tuple-element.34), channel_id=1, source_target_pairs={{0,16},{4,12},{8,24},{12,4},{16,0},{20,28},{24,8},{28,20},{1,17},{... | collective-permute-start | bytes 835592 | tf_op jit(solution)/shard_map/ppermute | solution.py:273
  11.2 0.0 copy-start
  11.3 1.0 %copy-done = bf16[480,512]{1,0:T(8,128)(2,1)S(1)} copy-done((bf16[480,512]{1,0:T(8,128)(2,1)S(1)}, bf16[480,512]{1,0:T(8,128)(2,1)}, u32[]{:S(2)}) %copy-start) | copy-done | bytes 491544
  12.3 0.0 copy-start.3
  12.3 0.0 copy-start.2
  12.3 0.1 collective-permute-done.refs_1_
  12.4 2.2 %collective-permute-done.1.refs_2_ = bf16[64,512]{1,0:T(8,128)(2,1)S(1)} collective-permute-done((bf16[64,512]{1,0:T(8,128)(2,1)}, bf16[64,512]{1,0:T(8,128)(2,1)S(1)}, u32[]{:S(2)}, u32[]{:S(2)}) %collective-permute-start.1) | collective-permute-done | bytes 65568 | tf_op jit(solution)/shard_map/ppermute | solution.py:268
  14.6 0.1 collective-permute-done.2.refs_3_
  14.6 0.0 collective-permute-done.6.refs_0_.refs_1_
  14.6 0.0 copy-start.1
  14.7 1.3 %collective-permute-start.8 = (bf16[272,512]{1,0:T(8,128)(2,1)S(1)}, bf16[272,512]{1,0:T(8,128)(2,1)S(1)}, u32[]{:S(2)}, u32[]{:S(2)}) collective-permute-start(bf16[272,512]{1,0:T(8,128)(2,1)S(1)} %shard_map.86), channel_id=1, source_target_pairs={{0,16},{4,12},{8,24},{12,4},{16,0},{20,28},{24,8},{28,20},{1,17},{... | collective-permute-start | bytes 835592 | tf_op jit(solution)/shard_map/ppermute | solution.py:273
  16.0 0.8 collective-permute-start.3
  16.7 0.0 copy-done.3
  16.8 1.8 %collective-permute-start.5 = (bf16[64,1024]{1,0:T(8,128)(2,1)S(1)}, bf16[64,1024]{1,0:T(8,128)(2,1)S(1)}, u32[]{:S(2)}, u32[]{:S(2)}) collective-permute-start(bf16[64,1024]{1,0:T(8,128)(2,1)S(1)} %copy-done.3), channel_id=1, source_target_pairs={{0,2},{1,3},{2,0},{3,1},{4,6},{5,7},{6,4},{7,5},{8,10},{9,11},{10,... | collective-permute-start | bytes 393224 | tf_op jit(solution)/shard_map/ppermute | solution.py:268
  18.5 0.0 copy-done.2
  18.5 1.3 %collective-permute-start.9 = (bf16[64,1024]{1,0:T(8,128)(2,1)S(1)}, bf16[64,1024]{1,0:T(8,128)(2,1)S(1)}, u32[]{:S(2)}, u32[]{:S(2)}) collective-permute-start(bf16[64,1024]{1,0:T(8,128)(2,1)S(1)} %copy-done.2), channel_id=1, source_target_pairs={{0,1},{1,0},{2,3},{3,2},{4,5},{5,4},{6,7},{7,6},{8,9},{9,8},{10,11... | collective-permute-start | bytes 393224 | tf_op jit(solution)/shard_map/ppermute | solution.py:268
  19.9 4.9 %collective-permute-done.5.refs_6_.refs_1_ = bf16[64,1024]{1,0:T(8,128)(2,1)S(1)} collective-permute-done((bf16[64,1024]{1,0:T(8,128)(2,1)S(1)}, bf16[64,1024]{1,0:T(8,128)(2,1)S(1)}, u32[]{:S(2)}, u32[]{:S(2)}) %collective-permute-start.5) | collective-permute-done | bytes 131104 | tf_op jit(solution)/shard_map/ppermute | solution.py:268
  24.8 0.1 collective-permute-done.9.refs_5_.refs_1_
  24.9 0.0 collective-permute-done.7.refs_2_
  24.9 0.0 collective-permute-done.3.refs_1_.refs_4_
  24.9 0.0 collective-permute-done.8.refs_3_
  24.9 0.0 slice-start
  24.9 0.1 shard_map.87.refs_2_
  25.0 0.1 collective-permute-start.10
  25.1 0.6 collective-permute-start.11
  25.7 1.5 %collective-permute-start.4 = (bf16[512,512]{1,0:T(8,128)(2,1)S(1)}, bf16[512,512]{1,0:T(8,128)(2,1)S(1)}, u32[]{:S(2)}, u32[]{:S(2)}) collective-permute-start(bf16[512,512]{1,0:T(8,128)(2,1)S(1)} %shard_map.85.refs_4_), channel_id=1, source_target_pairs={{0,16},{4,12},{8,24},{12,4},{16,0},{20,28},{24,8},{28,20},{1,17},{... | collective-permute-start | bytes 1572872 | tf_op jit(solution)/shard_map/ppermute | solution.py:273
  27.1 0.0 copy-done.1
  27.1 2.4 %collective-permute-start.12 = (bf16[64,1024]{1,0:T(8,128)(2,1)S(1)}, bf16[64,1024]{1,0:T(8,128)(2,1)S(1)}, u32[]{:S(2)}, u32[]{:S(2)}) collective-permute-start(bf16[64,1024]{1,0:T(8,128)(2,1)S(1)} %copy-done.1), channel_id=1, source_target_pairs={{0,3},{1,2},{2,1},{3,0},{4,7},{5,6},{6,5},{7,4},{8,11},{9,10},{10,... | collective-permute-start | bytes 393224 | tf_op jit(solution)/shard_map/ppermute | solution.py:268
  29.5 0.0 collective-permute-done.11.refs_5_
  29.5 0.0 collective-permute-done.10.refs_3_
  29.5 0.0 slice-start.1
  29.6 3.1 %shard_map.88 = (f32[2,256,256]{2,1,0:T(8,128)S(1)}, f32[2,256,128]{2,1,0:T(8,128)S(1)}) custom-call(s32[2,128]{1,0:T(2,128)S(1)} %get-tuple-element.26.refs_0_, bf16[64,1024]{1,0:T(8,128)(2,1)S(1)} %collective-permute-done.5.refs_6_.refs_1_, bf16[1088,512]{1,0:T(8,128)(2,1)S(1)} %shard_map.87.refs_2_, ...), custom_call_target="tpu_custom_call" | custom-call | flops 3221225472 | bytes 3145728 | tf_op jit(solution)/shard_map/pallas_call | solution.py:36
  32.6 1.3 %collective-permute-done.12.refs_2_.refs_1_ = bf16[64,1024]{1,0:T(8,128)(2,1)S(1)} collective-permute-done((bf16[64,1024]{1,0:T(8,128)(2,1)S(1)}, bf16[64,1024]{1,0:T(8,128)(2,1)S(1)}, u32[]{:S(2)}, u32[]{:S(2)}) %collective-permute-start.12) | collective-permute-done | bytes 131104 | tf_op jit(solution)/shard_map/ppermute | solution.py:268
  34.0 0.9 %collective-permute-done.4.refs_0_ = bf16[512,512]{1,0:T(8,128)(2,1)S(1)} collective-permute-done((bf16[512,512]{1,0:T(8,128)(2,1)S(1)}, bf16[512,512]{1,0:T(8,128)(2,1)S(1)}, u32[]{:S(2)}, u32[]{:S(2)}) %collective-permute-start.4) | collective-permute-done | bytes 524320 | tf_op jit(solution)/shard_map/ppermute | solution.py:273
  34.9 0.1 collective-permute-start.13
  35.0 1.9 %collective-permute-done.13.refs_3_ = bf16[512,512]{1,0:T(8,128)(2,1)S(1)} collective-permute-done((bf16[512,512]{1,0:T(8,128)(2,1)S(1)}, bf16[512,512]{1,0:T(8,128)(2,1)S(1)}, u32[]{:S(2)}, u32[]{:S(2)}) %collective-permute-start.13) | collective-permute-done | bytes 524320 | tf_op jit(solution)/shard_map/ppermute | solution.py:268
  36.9 0.0 slice-done
  36.9 0.0 slice-done.1
  36.9 3.0 %shard_map.90.refs_6_.refs_7_ = bf16[64,4096]{1,0:T(8,128)(2,1)S(1)} custom-call(s32[2,128]{1,0:T(2,128)S(1)} %get-tuple-element.26.refs_0_, bf16[64,1024]{1,0:T(8,128)(2,1)S(1)} %collective-permute-done.5.refs_6_.refs_1_, bf16[512,512]{1,0:T(8,128)(2,1)S(1)} %shard_map.89.refs_2_, bf16[512,512]{1,0:T(8,128)(2,1)S(1)} %collective-permute-done.13.refs_3_, ...), custom_call_target="tpu_custom_call" | custom-call | flops 3221225472 | bytes 1048576 | tf_op jit(solution)/shard_map/pallas_call | solution.py:36
  39.8 0.6 collective-permute-start.16
  40.4 3.1 %shard_map.91 = (f32[2,256,256]{2,1,0:T(8,128)S(1)}, f32[2,256,128]{2,1,0:T(8,128)S(1)}) custom-call(s32[2,128]{1,0:T(2,128)S(1)} %get-tuple-element.26.refs_0_, bf16[64,1024]{1,0:T(8,128)(2,1)S(1)} %collective-permute-done.12.refs_2_.refs_1_, bf16[1088,512]{1,0:T(8,128)(2,1)S(1)} %shard_map.87.refs_2_, ...), custom_call_target="tpu_custom_call" | custom-call | flops 3221225472 | bytes 3145728 | tf_op jit(solution)/shard_map/pallas_call | solution.py:36
  43.5 3.0 %shard_map.92.refs_6_.refs_7_.refs_0_ = bf16[64,4096]{1,0:T(8,128)(2,1)S(1)} custom-call(s32[2,128]{1,0:T(2,128)S(1)} %get-tuple-element.26.refs_0_, bf16[64,1024]{1,0:T(8,128)(2,1)S(1)} %collective-permute-done.12.refs_2_.refs_1_, bf16[512,512]{1,0:T(8,128)(2,1)S(1)} %shard_map.89.refs_2_, bf16[512,512]{1,0:T(8,128)(2,1)S(1)} %collective-permute-done.13.refs_3_, ...), custom_call_target="tpu_custom_call" | custom-call | flops 3221225472 | bytes 1048576 | tf_op jit(solution)/shard_map/pallas_call | solution.py:36
  46.5 4.0 %collective-permute-start.15 = (bf16[64,4096]{1,0:T(8,128)(2,1)S(1)}, bf16[64,4096]{1,0:T(8,128)(2,1)S(1)}, u32[]{:S(2)}, u32[]{:S(2)}) collective-permute-start(bf16[64,4096]{1,0:T(8,128)(2,1)S(1)} %shard_map.92.refs_6_.refs_7_.refs_0_), channel_id=1, source_target_pairs={{0,3},{3,0},{4,7},{7,4},{8,11},{11,8},{12,15},{15,12},{16,19},{19,... | collective-permute-start | bytes 1572872 | tf_op jit(solution)/shard_map/ppermute | solution.py:283
  50.5 3.1 %shard_map.93 = (f32[2,256,256]{2,1,0:T(8,128)S(1)}, f32[2,256,128]{2,1,0:T(8,128)S(1)}) custom-call(s32[2,128]{1,0:T(2,128)S(1)} %get-tuple-element.26.refs_0_, bf16[64,1024]{1,0:T(8,128)(2,1)S(1)} %collective-permute-done.9.refs_5_.refs_1_, bf16[1088,512]{1,0:T(8,128)(2,1)S(1)} %shard_map.87.refs_2_, ...), custom_call_target="tpu_custom_call" | custom-call | flops 3221225472 | bytes 3145728 | tf_op jit(solution)/shard_map/pallas_call | solution.py:36
  53.6 3.0 %shard_map.94.refs_6_.refs_7_ = bf16[64,4096]{1,0:T(8,128)(2,1)S(1)} custom-call(s32[2,128]{1,0:T(2,128)S(1)} %get-tuple-element.26.refs_0_, bf16[64,1024]{1,0:T(8,128)(2,1)S(1)} %collective-permute-done.9.refs_5_.refs_1_, bf16[512,512]{1,0:T(8,128)(2,1)S(1)} %shard_map.89.refs_2_, bf16[512,512]{1,0:T(8,128)(2,1)S(1)} %collective-permute-done.13.refs_3_, ...), custom_call_target="tpu_custom_call" | custom-call | flops 3221225472 | bytes 1048576 | tf_op jit(solution)/shard_map/pallas_call | solution.py:36
  56.6 0.1 collective-permute-start.14
  56.7 9.6 %collective-permute-done.16.refs_1_.refs_4_ = bf16[64,4096]{1,0:T(8,128)(2,1)S(1)} collective-permute-done((bf16[64,4096]{1,0:T(8,128)(2,1)S(1)}, bf16[64,4096]{1,0:T(8,128)(2,1)S(1)}, u32[]{:S(2)}, u32[]{:S(2)}) %collective-permute-start.16) | collective-permute-done | bytes 524320 | tf_op jit(solution)/shard_map/ppermute | solution.py:283
  66.3 0.1 shard_map.97
  66.4 0.7 collective-permute-start.17
  67.1 3.1 %shard_map.95 = (f32[2,256,256]{2,1,0:T(8,128)S(1)}, f32[2,256,128]{2,1,0:T(8,128)S(1)}) custom-call(s32[2,128]{1,0:T(2,128)S(1)} %get-tuple-element.26.refs_0_, bf16[64,1024]{1,0:T(8,128)(2,1)S(1)} %get-tuple-element.27.refs_1_, bf16[1088,512]{1,0:T(8,128)(2,1)S(1)} %shard_map.87.refs_2_, bf16[1088,512]{1,0:T(8,128)(2,1)S(1)} %collective-permute-done.10.refs_3_, ...), custom_call_target="tpu_custom_call" | custom-call | flops 3221225472 | bytes 3145728 | tf_op jit(solution)/shard_map/pallas_call | solution.py:36
  70.2 3.0 %shard_map.96.refs_0_ = bf16[64,4096]{1,0:T(8,128)(2,1)S(1)} custom-call(s32[2,128]{1,0:T(2,128)S(1)} %get-tuple-element.26.refs_0_, bf16[64,1024]{1,0:T(8,128)(2,1)S(1)} %get-tuple-element.27.refs_1_, bf16[512,512]{1,0:T(8,128)(2,1)S(1)} %shard_map.89.refs_2_, bf16[512,512]{1,0:T(8,128)(2,1)S(1)} %collective-permute-done.13.refs_3_, ...), custom_call_target="tpu_custom_call" | custom-call | flops 3221225472 | bytes 1048576 | tf_op jit(solution)/shard_map/pallas_call | solution.py:36
  73.2 4.1 %collective-permute-done.14.refs_1_ = bf16[64,4096]{1,0:T(8,128)(2,1)S(1)} collective-permute-done((bf16[64,4096]{1,0:T(8,128)(2,1)S(1)}, bf16[64,4096]{1,0:T(8,128)(2,1)S(1)}, u32[]{:S(2)}, u32[]{:S(2)}) %collective-permute-start.14) | collective-permute-done | bytes 524320 | tf_op jit(solution)/shard_map/ppermute | solution.py:283
  77.2 0.0 collective-permute-done.15.refs_2_
  77.2 0.0 collective-permute-done.17.refs_3_
  77.2 1.1 %shard_map.98 = bf16[64,4096]{1,0:T(8,128)(2,1)} custom-call(bf16[64,4096]{1,0:T(8,128)(2,1)S(1)} %shard_map.96.refs_0_, bf16[64,4096]{1,0:T(8,128)(2,1)S(1)} %collective-permute-done.14.refs_1_, bf16[64,4096]{1,0:T(8,128)(2,1)S(1)} %collective-permute-done.15.refs_2_, bf16[64,4096]{1,0:T(8,128)(2,1)S(1)} %collective-permute-done.17.refs_3_, ...), custom_call_target="tpu_custom_call" | custom-call | tf_op jit(solution)/shard_map/pallas_call | solution.py:36
  (6 shorter events, 0.1 us)
Async XLA Ops:
  2.4 12.2 %collective-permute-start.6 = (bf16[272,512]{1,0:T(8,128)(2,1)}, bf16[272,512]{1,0:T(8,128)(2,1)S(1)}, u32[]{:S(2)}, u32[]{:S(2)}) collective-permute-start(bf16[272,512]{1,0:T(8,128)(2,1)} %get-tuple-element.34), channel_id=1, source_target_pairs={{0,8},{4,20},{8,0},{12,28},{16,24},{20,4},{24,16},{28,12},{1,9},{5... | collective-permute-start | bytes 835592 | tf_op jit(solution)/shard_map/ppermute | solution.py:273
  5.3 7.1 %collective-permute-start = (bf16[64,512]{1,0:T(8,128)(2,1)}, bf16[64,512]{1,0:T(8,128)(2,1)S(1)}, u32[]{:S(2)}, u32[]{:S(2)}) collective-permute-start(bf16[64,512]{1,0:T(8,128)(2,1)} %get-tuple-element.29), channel_id=1, source_target_pairs={{0,3},{1,2},{2,1},{3,0},{4,7},{5,6},{6,5},{7,4},{8,11},{9,10},{10,... | collective-permute-start | bytes 196616 | tf_op jit(solution)/shard_map/ppermute | solution.py:268
  8.9 5.6 %collective-permute-start.1 = (bf16[64,512]{1,0:T(8,128)(2,1)}, bf16[64,512]{1,0:T(8,128)(2,1)S(1)}, u32[]{:S(2)}, u32[]{:S(2)}) collective-permute-start(bf16[64,512]{1,0:T(8,128)(2,1)} %get-tuple-element.30), channel_id=1, source_target_pairs={{0,2},{1,3},{2,0},{3,1},{4,6},{5,7},{6,4},{7,5},{8,10},{9,11},{10,... | collective-permute-start | bytes 196616 | tf_op jit(solution)/shard_map/ppermute | solution.py:268
  8.9 5.7 %collective-permute-start.2 = (bf16[64,512]{1,0:T(8,128)(2,1)}, bf16[64,512]{1,0:T(8,128)(2,1)S(1)}, u32[]{:S(2)}, u32[]{:S(2)}) collective-permute-start(bf16[64,512]{1,0:T(8,128)(2,1)} %get-tuple-element.31), channel_id=1, source_target_pairs={{0,1},{1,0},{2,3},{3,2},{4,5},{5,4},{6,7},{7,6},{8,9},{9,8},{10,11... | collective-permute-start | bytes 196616 | tf_op jit(solution)/shard_map/ppermute | solution.py:268
  9.7 15.1 %collective-permute-start.7 = (bf16[272,512]{1,0:T(8,128)(2,1)}, bf16[272,512]{1,0:T(8,128)(2,1)S(1)}, u32[]{:S(2)}, u32[]{:S(2)}) collective-permute-start(bf16[272,512]{1,0:T(8,128)(2,1)} %get-tuple-element.34), channel_id=1, source_target_pairs={{0,16},{4,12},{8,24},{12,4},{16,0},{20,28},{24,8},{28,20},{1,17},{... | collective-permute-start | bytes 835592 | tf_op jit(solution)/shard_map/ppermute | solution.py:273
  11.2 1.0 %copy-start = (bf16[480,512]{1,0:T(8,128)(2,1)S(1)}, bf16[480,512]{1,0:T(8,128)(2,1)}, u32[]{:S(2)}) copy-start(bf16[480,512]{1,0:T(8,128)(2,1)} %get-tuple-element.25.refs_0_) | copy-start | bytes 1474564
  12.3 4.5 %copy-start.3 = (bf16[64,1024]{1,0:T(8,128)(2,1)S(1)}, bf16[64,1024]{1,0:T(8,128)(2,1)}, u32[]{:S(2)}) copy-start(bf16[64,1024]{1,0:T(8,128)(2,1)} %get-tuple-element.32) | copy-start | bytes 393220
  12.3 6.3 %copy-start.2 = (bf16[64,1024]{1,0:T(8,128)(2,1)S(1)}, bf16[64,1024]{1,0:T(8,128)(2,1)}, u32[]{:S(2)}) copy-start(bf16[64,1024]{1,0:T(8,128)(2,1)} %get-tuple-element.35) | copy-start | bytes 393220
  14.6 12.5 %copy-start.1 = (bf16[64,1024]{1,0:T(8,128)(2,1)S(1)}, bf16[64,1024]{1,0:T(8,128)(2,1)}, u32[]{:S(2)}) copy-start(bf16[64,1024]{1,0:T(8,128)(2,1)} %get-tuple-element.37) | copy-start | bytes 393220
  14.7 10.2 %collective-permute-start.8 = (bf16[272,512]{1,0:T(8,128)(2,1)S(1)}, bf16[272,512]{1,0:T(8,128)(2,1)S(1)}, u32[]{:S(2)}, u32[]{:S(2)}) collective-permute-start(bf16[272,512]{1,0:T(8,128)(2,1)S(1)} %shard_map.86), channel_id=1, source_target_pairs={{0,16},{4,12},{8,24},{12,4},{16,0},{20,28},{24,8},{28,20},{1,17},{... | collective-permute-start | bytes 835592 | tf_op jit(solution)/shard_map/ppermute | solution.py:273
  16.0 8.9 %collective-permute-start.3 = (bf16[256,512]{1,0:T(8,128)(2,1)S(1)}, bf16[256,512]{1,0:T(8,128)(2,1)S(1)}, u32[]{:S(2)}, u32[]{:S(2)}) collective-permute-start(bf16[256,512]{1,0:T(8,128)(2,1)S(1)} %shard_map.84.refs_0_.refs_1_), channel_id=1, source_target_pairs={{0,8},{4,20},{8,0},{12,28},{16,24},{20,4},{24,16},{28,12},{1,9},{5... | collective-permute-start | bytes 786440 | tf_op jit(solution)/shard_map/ppermute | solution.py:273
  16.8 8.0 %collective-permute-start.5 = (bf16[64,1024]{1,0:T(8,128)(2,1)S(1)}, bf16[64,1024]{1,0:T(8,128)(2,1)S(1)}, u32[]{:S(2)}, u32[]{:S(2)}) collective-permute-start(bf16[64,1024]{1,0:T(8,128)(2,1)S(1)} %copy-done.3), channel_id=1, source_target_pairs={{0,2},{1,3},{2,0},{3,1},{4,6},{5,7},{6,4},{7,5},{8,10},{9,11},{10,... | collective-permute-start | bytes 393224 | tf_op jit(solution)/shard_map/ppermute | solution.py:268
  18.5 6.3 %collective-permute-start.9 = (bf16[64,1024]{1,0:T(8,128)(2,1)S(1)}, bf16[64,1024]{1,0:T(8,128)(2,1)S(1)}, u32[]{:S(2)}, u32[]{:S(2)}) collective-permute-start(bf16[64,1024]{1,0:T(8,128)(2,1)S(1)} %copy-done.2), channel_id=1, source_target_pairs={{0,1},{1,0},{2,3},{3,2},{4,5},{5,4},{6,7},{7,6},{8,9},{9,8},{10,11... | collective-permute-start | bytes 393224 | tf_op jit(solution)/shard_map/ppermute | solution.py:268
  24.9 12.0 %slice-start = ((s8[8388608]{0:T(1024)(128)(4,1)}), s8[4194304]{0:T(1024)(128)(4,1)S(1)}, s32[]{:S(2)}) async-start(s8[8388608]{0:T(1024)(128)(4,1)} %bitcast), calls=%async_computation | async-start | bytes 8388608
  25.0 4.6 %collective-permute-start.10 = (bf16[1088,512]{1,0:T(8,128)(2,1)S(1)}, bf16[1088,512]{1,0:T(8,128)(2,1)S(1)}, u32[]{:S(2)}, u32[]{:S(2)}) collective-permute-start(bf16[1088,512]{1,0:T(8,128)(2,1)S(1)} %shard_map.87.refs_2_), channel_id=1, source_target_pairs={{0,4},{4,0},{8,12},{12,8},{16,20},{20,16},{24,28},{28,24},{1,5},{5... | collective-permute-start | bytes 3342344 | tf_op jit(solution)/shard_map/ppermute | solution.py:268
  25.1 4.4 %collective-permute-start.11 = (bf16[512,512]{1,0:T(8,128)(2,1)S(1)}, bf16[512,512]{1,0:T(8,128)(2,1)S(1)}, u32[]{:S(2)}, u32[]{:S(2)}) collective-permute-start(bf16[512,512]{1,0:T(8,128)(2,1)S(1)} %shard_map.85.refs_4_), channel_id=1, source_target_pairs={{0,4},{4,0},{8,12},{12,8},{16,20},{20,16},{24,28},{28,24},{1,5},{5... | collective-permute-start | bytes 1572872 | tf_op jit(solution)/shard_map/ppermute | solution.py:268
  25.7 9.2 %collective-permute-start.4 = (bf16[512,512]{1,0:T(8,128)(2,1)S(1)}, bf16[512,512]{1,0:T(8,128)(2,1)S(1)}, u32[]{:S(2)}, u32[]{:S(2)}) collective-permute-start(bf16[512,512]{1,0:T(8,128)(2,1)S(1)} %shard_map.85.refs_4_), channel_id=1, source_target_pairs={{0,16},{4,12},{8,24},{12,4},{16,0},{20,28},{24,8},{28,20},{1,17},{... | collective-permute-start | bytes 1572872 | tf_op jit(solution)/shard_map/ppermute | solution.py:273
  27.1 6.8 %collective-permute-start.12 = (bf16[64,1024]{1,0:T(8,128)(2,1)S(1)}, bf16[64,1024]{1,0:T(8,128)(2,1)S(1)}, u32[]{:S(2)}, u32[]{:S(2)}) collective-permute-start(bf16[64,1024]{1,0:T(8,128)(2,1)S(1)} %copy-done.1), channel_id=1, source_target_pairs={{0,3},{1,2},{2,1},{3,0},{4,7},{5,6},{6,5},{7,4},{8,11},{9,10},{10,... | collective-permute-start | bytes 393224 | tf_op jit(solution)/shard_map/ppermute | solution.py:268
  29.5 7.3 %slice-start.1 = ((s8[8388608]{0:T(1024)(128)(4,1)}), s8[4194304]{0:T(1024)(128)(4,1)S(1)}, s32[]{:S(2)}) async-start(s8[8388608]{0:T(1024)(128)(4,1)} %bitcast), calls=%async_computation.1 | async-start | bytes 8388608
  34.9 2.0 %collective-permute-start.13 = (bf16[512,512]{1,0:T(8,128)(2,1)S(1)}, bf16[512,512]{1,0:T(8,128)(2,1)S(1)}, u32[]{:S(2)}, u32[]{:S(2)}) collective-permute-start(bf16[512,512]{1,0:T(8,128)(2,1)S(1)} %shard_map.89.refs_2_), channel_id=1, source_target_pairs={{0,4},{4,0},{8,12},{12,8},{16,20},{20,16},{24,28},{28,24},{1,5},{5... | collective-permute-start | bytes 1572872 | tf_op jit(solution)/shard_map/ppermute | solution.py:268
  39.8 26.4 %collective-permute-start.16 = (bf16[64,4096]{1,0:T(8,128)(2,1)S(1)}, bf16[64,4096]{1,0:T(8,128)(2,1)S(1)}, u32[]{:S(2)}, u32[]{:S(2)}) collective-permute-start(bf16[64,4096]{1,0:T(8,128)(2,1)S(1)} %shard_map.90.refs_6_.refs_7_), channel_id=1, source_target_pairs={{0,1},{1,3},{2,0},{3,2},{4,5},{5,7},{6,4},{7,6},{8,9},{9,11},{10,8... | collective-permute-start | bytes 1572872 | tf_op jit(solution)/shard_map/ppermute | solution.py:283
  46.5 30.7 %collective-permute-start.15 = (bf16[64,4096]{1,0:T(8,128)(2,1)S(1)}, bf16[64,4096]{1,0:T(8,128)(2,1)S(1)}, u32[]{:S(2)}, u32[]{:S(2)}) collective-permute-start(bf16[64,4096]{1,0:T(8,128)(2,1)S(1)} %shard_map.92.refs_6_.refs_7_.refs_0_), channel_id=1, source_target_pairs={{0,3},{3,0},{4,7},{7,4},{8,11},{11,8},{12,15},{15,12},{16,19},{19,... | collective-permute-start | bytes 1572872 | tf_op jit(solution)/shard_map/ppermute | solution.py:283
  56.6 20.6 %collective-permute-start.14 = (bf16[64,4096]{1,0:T(8,128)(2,1)S(1)}, bf16[64,4096]{1,0:T(8,128)(2,1)S(1)}, u32[]{:S(2)}, u32[]{:S(2)}) collective-permute-start(bf16[64,4096]{1,0:T(8,128)(2,1)S(1)} %shard_map.94.refs_6_.refs_7_), channel_id=1, source_target_pairs={{0,1},{1,0},{2,3},{3,2},{4,5},{5,4},{6,7},{7,6},{8,9},{9,8},{10,11... | collective-permute-start | bytes 1572872 | tf_op jit(solution)/shard_map/ppermute | solution.py:283
  66.4 10.9 %collective-permute-start.17 = (bf16[64,4096]{1,0:T(8,128)(2,1)S(1)}, bf16[64,4096]{1,0:T(8,128)(2,1)S(1)}, u32[]{:S(2)}, u32[]{:S(2)}) collective-permute-start(bf16[64,4096]{1,0:T(8,128)(2,1)S(1)} %shard_map.97), channel_id=1, source_target_pairs={{1,2},{2,1},{5,6},{6,5},{9,10},{10,9},{13,14},{14,13},{17,18},{18,... | collective-permute-start | bytes 1572872 | tf_op jit(solution)/shard_map/ppermute | solution.py:283

commit v7 on v6

--- a/solution.py
+++ b/solution.py
@@ -193,35 +193,37 @@
     return [ref.at[pl.ds(i, tokens)] for ref in refs for i in range(0, ref.shape[0], tokens)]
 
 
-def first_kernel(xs, cached, count, n_ctx, n_head, q_width, ends, *refs):
+def first_kernel(xs, cached, count, skip, n_ctx, n_head, q_width, ends, *refs):
     query, refs = refs[:len(xs)], refs[len(xs):]
     outs, (scores, masks) = refs[count:-2], refs[-2:]
     tokens = masks.shape[1]
     cache = views(refs[:cached], tokens + tokens // PAGE)
     fresh = views(refs[cached:count], tokens)
-    at = Layout(ends, query[0].shape[0], q_width, cache[0].shape[1], n_ctx, n_head)
-    for b in range(n_ctx):
+    at = Layout(ends, query[0].shape[0], q_width, refs[0].shape[1], n_ctx, n_head)
+    blocks = cache + fresh
+    for b in range(len(cache)):
         masks[b] = at.cache_mask(cache[b][tokens:, :LANES])
     for i, x in enumerate(xs):
         summed, tops = outs[2 * i:2 * i + 2]
         for b in range(len(fresh)):
-            masks[n_ctx + b] = at.fresh_mask(b, at.h ^ x)
+            masks[len(cache) + b] = at.fresh_mask(skip + b, at.h ^ x)
         q_rows = at.query_rows(query[i], x)
         for g in range(at.groups):
             summed[g], tops[g] = attend(
-                q_rows[g], cache + fresh, [masks.at[b] for b in range(n_ctx + len(fresh))], scores.at[g], tokens, g, at.groups
+                q_rows[g], blocks, [masks.at[b] for b in range(len(blocks))], scores.at[g], tokens, g, at.groups
             )
 
 
-def last_kernel(xs, count, n_ctx, n_head, q_width, ends, *refs):
+def last_kernel(xs, count, states, n_ctx, n_head, q_width, ends, *refs):
     query, refs = refs[:len(xs)], refs[len(xs):]
-    fresh, state, refs = refs[:count], refs[count:count + 2 * len(xs)], refs[count + 2 * len(xs):]
+    split = count + 2 * states * len(xs)
+    fresh, state, refs = refs[:count], refs[count:split], refs[split:]
     weight, outs, (scores, masks, mixed) = refs[0], refs[1:-3], refs[-3:]
     rows, tokens = query[0].shape[0], masks.shape[1]
     fresh = views(fresh, tokens)
     at = Layout(ends, rows, q_width, fresh[0].shape[1], n_ctx, n_head)
     for i, x in enumerate(xs):
-        summed, tops = state[2 * i:2 * i + 2]
+        earlier = state[2 * states * i:2 * states * (i + 1)]
         for b in range(len(fresh)):
             masks[b] = at.fresh_mask(n_ctx - len(fresh) + b, at.h ^ x)
         q_rows = at.query_rows(query[i], x)
@@ -229,10 +231,13 @@
             sum_b, top_b = attend(
                 q_rows[g], fresh, [masks.at[b] for b in range(len(fresh))], scores.at[g], tokens, g, at.groups
             )
-            top = jnp.maximum(tops[g], top_b)
-            factor_a, factor_b = jnp.exp2(tops[g] - top), jnp.exp2(top_b - top)
-            value = summed[g, :, :HD] * factor_a + sum_b[:, :HD] * factor_b
-            total = summed[g, :, HD:] * factor_a + sum_b[:, HD:] * factor_b
+            top = top_b
+            for tops in earlier[1::2]:
+                top = jnp.maximum(top, tops[g])
+            joined = sum_b * jnp.concatenate([jnp.exp2(top_b - top)] * 2, axis=1)
+            for summed, tops in zip(earlier[::2], earlier[1::2]):
+                joined += summed[g] * jnp.concatenate([jnp.exp2(tops[g] - top)] * 2, axis=1)
+            value, total = joined[:, :HD], joined[:, HD:]
             attended = (value / total).astype(BF16)
             for j in range(at.repeat):
                 n = g * at.repeat + j
@@ -353,7 +358,7 @@
     def first(xs, *after):
         n = n_ctx + n_ctx // 2
         found = call(
-            functools.partial(first_kernel, xs, len(cache), len(cache) + len(early), n_ctx, n_head, q_width),
+            functools.partial(first_kernel, xs, len(cache), len(cache) + len(early), 0, n_ctx, n_head, q_width),
             [jax.ShapeDtypeStruct((groups, stacked, lanes), F32) for _ in xs for lanes in (2 * HD, LANES)],
             [ends, *(query[x] for x in xs), *cache, *early], after=after, **attend_keys(n),
             cost=pl.CostEstimate(
@@ -365,12 +370,14 @@
         state.update((x, found[2 * i:2 * i + 2]) for i, x in enumerate(xs))
 
     def part(xs, *after):
-        n = n_ctx - n_ctx // 2
+        states = len(state[xs[0]]) // 2
+        blocks = late[states - 1:]
+        n = sum(block.shape[0] for block in blocks) // tokens
         options = attend_keys(n)
         options["scratch"].append(pltpu.VMEM((len(xs) * rows, q_width), BF16))
         return call(
-            functools.partial(last_kernel, xs, len(late), n_ctx, n_head, q_width), [shaped(rows, columns)] * len(xs),
-            [ends, *(query[x] for x in xs), *late, *(a for x in xs for a in state[x]), output_weight],
+            functools.partial(last_kernel, xs, len(blocks), states, n_ctx, n_head, q_width), [shaped(rows, columns)] * len(xs),
+            [ends, *(query[x] for x in xs), *blocks, *(a for x in xs for a in state[x]), output_weight],
             after=after, **options,
             cost=pl.CostEstimate(
                 flops=len(xs) * (16 * rows * q_width * n * tokens + 8 * rows * q_width * columns),
@@ -383,6 +390,12 @@
         first((2,))
         late = [stack(late, state[2][1], query[3])]
         late.append(swap(late[0], "ctx", 1))
+        n = late[0].shape[0] // tokens
+        state[2] = state[2] + call(
+            functools.partial(first_kernel, (2,), 0, 1, n_ctx - 2 * n, n_ctx, n_head, q_width),
+            [jax.ShapeDtypeStruct((groups, stacked, lanes), F32) for lanes in (2 * HD, LANES)],
+            [ends, query[2], late[0]], **attend_keys(n),
+        )
 
     def chunks(xs, *after):
         todo = tuple(x for x in xs if x not in state)

time: 78.6 us -> 78 us (level)
    pallas_call x17 -> x18, Pallas kernels: 28.1 us -> 28 us  [call(): pl.pallas_call(body, out_shape=outs, in_specs=specs + [pl.BlockSpec(memor...]
  transfers between devices with their start and end apart: 18 -> 18, of which waited for: 10 -> 10; matrix products, arithmetic and copies ran while one was open for 0% -> 0% of each run, Pallas kernels for 27% -> 28%
where the time goes in v7:
time: 78 us; the launch traced here: 77.8 us
  Pallas kernels  28 us (36%)
  waiting for transfers between devices  24.6 us (32%)
  starting transfers between devices  23.9 us (31%)
  local copies, waits for them, and re-layouts  1.05 us (1%)
    pallas_call x18, Pallas kernels, call(): pl.pallas_call(body, out_shape=outs, in_specs=specs + [pl.BlockSpec(memor...  28 us
    ppermute x4, waiting for transfers between devices, send(): return lax.ppermute(value, 'head', pairs)  13.9 us
    ppermute x9, starting transfers between devices, swap(): lax.ppermute(value, axis, [(i, i ^ mask) for i in range(lax.axis_size(axi...  10.6 us
    ppermute x9, waiting for transfers between devices, swap(): lax.ppermute(value, axis, [(i, i ^ mask) for i in range(lax.axis_size(axi...  9.77 us
    ppermute x5, starting transfers between devices, leg(): lax.ppermute(block, 'ctx', [(i, i ^ (odd if i % 2 else even)) for i in ra...  7.99 us
    ppermute x4, starting transfers between devices, send(): return lax.ppermute(value, 'head', pairs)  5.36 us
  transfers between devices with their start and end apart: 18, of which 10 were waited for; matrix products, arithmetic and copies ran while one was open for 0% of the time, Pallas kernels for 28%

profile of v7, /device:TPU:0, one launch (start us, length us, event | category | flops | bytes accessed | tf_op | source)
XLA Modules:
  0.0 77.8 jit_solution(11771190465669824276)
XLA Ops:
  0.0 2.4 %shard_map.82 = (bf16[64,512]{1,0:T(8,128)(2,1)}, bf16[64,512]{1,0:T(8,128)(2,1)}, bf16[64,512]{1,0:T(8,128)(2,1)}, bf16[64,1024]{1,0:T(8,128)(2,1)}, bf16[64,10...) custom-call(s32[2]{0:T(128)} %refs_0_.1, s32[16]{0:T(128)} %refs_1_.1, ...), custom_call_target="tpu_custom_call" | custom-call | tf_op jit(solution)/shard_map/pallas_call | solution.py:36
  2.4 2.9 %collective-permute-start.6 = (bf16[272,512]{1,0:T(8,128)(2,1)}, bf16[272,512]{1,0:T(8,128)(2,1)S(1)}, u32[]{:S(2)}, u32[]{:S(2)}) collective-permute-start(bf16[272,512]{1,0:T(8,128)(2,1)} %get-tuple-element.36), channel_id=1, source_target_pairs={{0,8},{4,20},{8,0},{12,28},{16,24},{20,4},{24,16},{28,12},{1,9},{5... | collective-permute-start | bytes 835592 | tf_op jit(solution)/shard_map/ppermute | solution.py:278
  5.3 3.6 %collective-permute-start = (bf16[64,512]{1,0:T(8,128)(2,1)}, bf16[64,512]{1,0:T(8,128)(2,1)S(1)}, u32[]{:S(2)}, u32[]{:S(2)}) collective-permute-start(bf16[64,512]{1,0:T(8,128)(2,1)} %get-tuple-element.31), channel_id=1, source_target_pairs={{0,3},{1,2},{2,1},{3,0},{4,7},{5,6},{6,5},{7,4},{8,11},{9,10},{10,... | collective-permute-start | bytes 196616 | tf_op jit(solution)/shard_map/ppermute | solution.py:273
  8.9 0.0 collective-permute-start.1
  8.9 0.8 %collective-permute-start.2 = (bf16[64,512]{1,0:T(8,128)(2,1)}, bf16[64,512]{1,0:T(8,128)(2,1)S(1)}, u32[]{:S(2)}, u32[]{:S(2)}) collective-permute-start(bf16[64,512]{1,0:T(8,128)(2,1)} %get-tuple-element.33), channel_id=1, source_target_pairs={{0,1},{1,0},{2,3},{3,2},{4,5},{5,4},{6,7},{7,6},{8,9},{9,8},{10,11... | collective-permute-start | bytes 196616 | tf_op jit(solution)/shard_map/ppermute | solution.py:273
  9.7 1.5 %collective-permute-start.7 = (bf16[272,512]{1,0:T(8,128)(2,1)}, bf16[272,512]{1,0:T(8,128)(2,1)S(1)}, u32[]{:S(2)}, u32[]{:S(2)}) collective-permute-start(bf16[272,512]{1,0:T(8,128)(2,1)} %get-tuple-element.36), channel_id=1, source_target_pairs={{0,16},{4,12},{8,24},{12,4},{16,0},{20,28},{24,8},{28,20},{1,17},{... | collective-permute-start | bytes 835592 | tf_op jit(solution)/shard_map/ppermute | solution.py:278
  11.2 0.0 copy-start
  11.3 1.0 %copy-done = bf16[480,512]{1,0:T(8,128)(2,1)S(1)} copy-done((bf16[480,512]{1,0:T(8,128)(2,1)S(1)}, bf16[480,512]{1,0:T(8,128)(2,1)}, u32[]{:S(2)}) %copy-start) | copy-done | bytes 491544
  12.3 0.0 copy-start.3
  12.3 0.0 copy-start.2
  12.3 0.1 collective-permute-done.refs_1_
  12.4 2.2 %collective-permute-done.1.refs_2_ = bf16[64,512]{1,0:T(8,128)(2,1)S(1)} collective-permute-done((bf16[64,512]{1,0:T(8,128)(2,1)}, bf16[64,512]{1,0:T(8,128)(2,1)S(1)}, u32[]{:S(2)}, u32[]{:S(2)}) %collective-permute-start.1) | collective-permute-done | bytes 65568 | tf_op jit(solution)/shard_map/ppermute | solution.py:273
  14.6 0.1 collective-permute-done.2.refs_3_
  14.6 0.0 collective-permute-done.6.refs_0_.refs_1_
  14.6 0.0 copy-start.1
  14.7 1.3 %collective-permute-start.8 = (bf16[272,512]{1,0:T(8,128)(2,1)S(1)}, bf16[272,512]{1,0:T(8,128)(2,1)S(1)}, u32[]{:S(2)}, u32[]{:S(2)}) collective-permute-start(bf16[272,512]{1,0:T(8,128)(2,1)S(1)} %shard_map.86), channel_id=1, source_target_pairs={{0,16},{4,12},{8,24},{12,4},{16,0},{20,28},{24,8},{28,20},{1,17},{... | collective-permute-start | bytes 835592 | tf_op jit(solution)/shard_map/ppermute | solution.py:278
  16.0 0.8 collective-permute-start.3
  16.7 0.0 copy-done.3
  16.8 1.8 %collective-permute-start.5 = (bf16[64,1024]{1,0:T(8,128)(2,1)S(1)}, bf16[64,1024]{1,0:T(8,128)(2,1)S(1)}, u32[]{:S(2)}, u32[]{:S(2)}) collective-permute-start(bf16[64,1024]{1,0:T(8,128)(2,1)S(1)} %copy-done.3), channel_id=1, source_target_pairs={{0,2},{1,3},{2,0},{3,1},{4,6},{5,7},{6,4},{7,5},{8,10},{9,11},{10,... | collective-permute-start | bytes 393224 | tf_op jit(solution)/shard_map/ppermute | solution.py:273
  18.5 0.0 copy-done.2
  18.5 1.3 %collective-permute-start.9 = (bf16[64,1024]{1,0:T(8,128)(2,1)S(1)}, bf16[64,1024]{1,0:T(8,128)(2,1)S(1)}, u32[]{:S(2)}, u32[]{:S(2)}) collective-permute-start(bf16[64,1024]{1,0:T(8,128)(2,1)S(1)} %copy-done.2), channel_id=1, source_target_pairs={{0,1},{1,0},{2,3},{3,2},{4,5},{5,4},{6,7},{7,6},{8,9},{9,8},{10,11... | collective-permute-start | bytes 393224 | tf_op jit(solution)/shard_map/ppermute | solution.py:273
  19.9 4.9 %collective-permute-done.5.refs_6_.refs_1_ = bf16[64,1024]{1,0:T(8,128)(2,1)S(1)} collective-permute-done((bf16[64,1024]{1,0:T(8,128)(2,1)S(1)}, bf16[64,1024]{1,0:T(8,128)(2,1)S(1)}, u32[]{:S(2)}, u32[]{:S(2)}) %collective-permute-start.5) | collective-permute-done | bytes 131104 | tf_op jit(solution)/shard_map/ppermute | solution.py:273
  24.8 0.1 collective-permute-done.9.refs_5_.refs_1_
  24.9 0.0 collective-permute-done.7.refs_2_
  24.9 0.0 collective-permute-done.3.refs_1_.refs_4_
  24.9 0.0 collective-permute-done.8.refs_3_
  24.9 0.0 slice-start
  24.9 0.1 shard_map.87.refs_2_
  25.0 0.1 collective-permute-start.10
  25.1 0.6 collective-permute-start.11
  25.7 1.5 %collective-permute-start.4 = (bf16[512,512]{1,0:T(8,128)(2,1)S(1)}, bf16[512,512]{1,0:T(8,128)(2,1)S(1)}, u32[]{:S(2)}, u32[]{:S(2)}) collective-permute-start(bf16[512,512]{1,0:T(8,128)(2,1)S(1)} %shard_map.85.refs_4_), channel_id=1, source_target_pairs={{0,16},{4,12},{8,24},{12,4},{16,0},{20,28},{24,8},{28,20},{1,17},{... | collective-permute-start | bytes 1572872 | tf_op jit(solution)/shard_map/ppermute | solution.py:278
  27.1 0.0 copy-done.1
  27.1 2.4 %collective-permute-start.12 = (bf16[64,1024]{1,0:T(8,128)(2,1)S(1)}, bf16[64,1024]{1,0:T(8,128)(2,1)S(1)}, u32[]{:S(2)}, u32[]{:S(2)}) collective-permute-start(bf16[64,1024]{1,0:T(8,128)(2,1)S(1)} %copy-done.1), channel_id=1, source_target_pairs={{0,3},{1,2},{2,1},{3,0},{4,7},{5,6},{6,5},{7,4},{8,11},{9,10},{10,... | collective-permute-start | bytes 393224 | tf_op jit(solution)/shard_map/ppermute | solution.py:273
  29.5 0.0 collective-permute-done.11.refs_5_
  29.5 0.0 collective-permute-done.10.refs_3_
  29.5 0.0 slice-start.1
  29.6 3.0 %shard_map.88 = (f32[2,256,256]{2,1,0:T(8,128)S(1)}, f32[2,256,128]{2,1,0:T(8,128)S(1)}) custom-call(s32[2,128]{1,0:T(2,128)S(1)} %get-tuple-element.28.refs_0_, bf16[64,1024]{1,0:T(8,128)(2,1)S(1)} %collective-permute-done.5.refs_6_.refs_1_, bf16[1088,512]{1,0:T(8,128)(2,1)S(1)} %shard_map.87.refs_2_, ...), custom_call_target="tpu_custom_call" | custom-call | flops 3221225472 | bytes 3145728 | tf_op jit(solution)/shard_map/pallas_call | solution.py:36
  32.6 1.4 %collective-permute-done.12.refs_2_.refs_1_ = bf16[64,1024]{1,0:T(8,128)(2,1)S(1)} collective-permute-done((bf16[64,1024]{1,0:T(8,128)(2,1)S(1)}, bf16[64,1024]{1,0:T(8,128)(2,1)S(1)}, u32[]{:S(2)}, u32[]{:S(2)}) %collective-permute-start.12) | collective-permute-done | bytes 131104 | tf_op jit(solution)/shard_map/ppermute | solution.py:273
  34.0 0.9 %collective-permute-done.4.refs_0_ = bf16[512,512]{1,0:T(8,128)(2,1)S(1)} collective-permute-done((bf16[512,512]{1,0:T(8,128)(2,1)S(1)}, bf16[512,512]{1,0:T(8,128)(2,1)S(1)}, u32[]{:S(2)}, u32[]{:S(2)}) %collective-permute-start.4) | collective-permute-done | bytes 524320 | tf_op jit(solution)/shard_map/ppermute | solution.py:278
  34.9 0.1 collective-permute-start.13
  35.0 0.8 %shard_map.90 = (f32[2,256,256]{2,1,0:T(8,128)S(1)}, f32[2,256,128]{2,1,0:T(8,128)S(1)}) custom-call(s32[2,128]{1,0:T(2,128)S(1)} %get-tuple-element.28.refs_0_, bf16[64,1024]{1,0:T(8,128)(2,1)S(1)} %collective-permute-done.5.refs_6_.refs_1_, bf16[512,512]{1,0:T(8,128)(2,1)S(1)} %shard_map.89.refs_2_), custom_call_target="tpu_custom_call" | custom-call | tf_op jit(solution)/shard_map/pallas_call | solution.py:36
  35.8 1.1 %collective-permute-done.13.refs_2_.refs_3_ = bf16[512,512]{1,0:T(8,128)(2,1)S(1)} collective-permute-done((bf16[512,512]{1,0:T(8,128)(2,1)S(1)}, bf16[512,512]{1,0:T(8,128)(2,1)S(1)}, u32[]{:S(2)}, u32[]{:S(2)}) %collective-permute-start.13) | collective-permute-done | bytes 524320 | tf_op jit(solution)/shard_map/ppermute | solution.py:273
  36.9 0.0 slice-done
  36.9 0.0 slice-done.1
  36.9 2.4 %shard_map.91.refs_6_.refs_7_ = bf16[64,4096]{1,0:T(8,128)(2,1)S(1)} custom-call(s32[2,128]{1,0:T(2,128)S(1)} %get-tuple-element.28.refs_0_, bf16[64,1024]{1,0:T(8,128)(2,1)S(1)} %collective-permute-done.5.refs_6_.refs_1_, bf16[512,512]{1,0:T(8,128)(2,1)S(1)} %collective-permute-done.13.refs_2_.refs_3_, f32[2,256,256]{2,1,0:T(8,128)S(1)} %get-tuple-element.40.refs_3_, ...), custom_call_target="tpu_custom_call" | custom-call | flops 2684354560 | bytes 524288 | tf_op jit(solution)/shard_map/pallas_call | solution.py:36
  39.2 0.6 collective-permute-start.16
  39.8 3.0 %shard_map.92 = (f32[2,256,256]{2,1,0:T(8,128)S(1)}, f32[2,256,128]{2,1,0:T(8,128)S(1)}) custom-call(s32[2,128]{1,0:T(2,128)S(1)} %get-tuple-element.28.refs_0_, bf16[64,1024]{1,0:T(8,128)(2,1)S(1)} %collective-permute-done.12.refs_2_.refs_1_, bf16[1088,512]{1,0:T(8,128)(2,1)S(1)} %shard_map.87.refs_2_, ...), custom_call_target="tpu_custom_call" | custom-call | flops 3221225472 | bytes 3145728 | tf_op jit(solution)/shard_map/pallas_call | solution.py:36
  42.8 3.0 %shard_map.93.refs_6_.refs_7_.refs_0_ = bf16[64,4096]{1,0:T(8,128)(2,1)S(1)} custom-call(s32[2,128]{1,0:T(2,128)S(1)} %get-tuple-element.28.refs_0_, bf16[64,1024]{1,0:T(8,128)(2,1)S(1)} %collective-permute-done.12.refs_2_.refs_1_, bf16[512,512]{1,0:T(8,128)(2,1)S(1)} %shard_map.89.refs_2_, bf16[512,512]{1,0:T(8,128)(2,1)S(1)} %collective-permute-done.13.refs_2_.refs_3_, ...), custom_call_target="tpu_custom_call" | custom-call | flops 3221225472 | bytes 1048576 | tf_op jit(solution)/shard_map/pallas_call | solution.py:36
  45.8 4.0 %collective-permute-start.15 = (bf16[64,4096]{1,0:T(8,128)(2,1)S(1)}, bf16[64,4096]{1,0:T(8,128)(2,1)S(1)}, u32[]{:S(2)}, u32[]{:S(2)}) collective-permute-start(bf16[64,4096]{1,0:T(8,128)(2,1)S(1)} %shard_map.93.refs_6_.refs_7_.refs_0_), channel_id=1, source_target_pairs={{0,3},{3,0},{4,7},{7,4},{8,11},{11,8},{12,15},{15,12},{16,19},{19,... | collective-permute-start | bytes 1572872 | tf_op jit(solution)/shard_map/ppermute | solution.py:288
  49.8 3.0 %shard_map.94 = (f32[2,256,256]{2,1,0:T(8,128)S(1)}, f32[2,256,128]{2,1,0:T(8,128)S(1)}) custom-call(s32[2,128]{1,0:T(2,128)S(1)} %get-tuple-element.28.refs_0_, bf16[64,1024]{1,0:T(8,128)(2,1)S(1)} %collective-permute-done.9.refs_5_.refs_1_, bf16[1088,512]{1,0:T(8,128)(2,1)S(1)} %shard_map.87.refs_2_, ...), custom_call_target="tpu_custom_call" | custom-call | flops 3221225472 | bytes 3145728 | tf_op jit(solution)/shard_map/pallas_call | solution.py:36
  52.8 3.0 %shard_map.95.refs_6_.refs_7_ = bf16[64,4096]{1,0:T(8,128)(2,1)S(1)} custom-call(s32[2,128]{1,0:T(2,128)S(1)} %get-tuple-element.28.refs_0_, bf16[64,1024]{1,0:T(8,128)(2,1)S(1)} %collective-permute-done.9.refs_5_.refs_1_, bf16[512,512]{1,0:T(8,128)(2,1)S(1)} %shard_map.89.refs_2_, bf16[512,512]{1,0:T(8,128)(2,1)S(1)} %collective-permute-done.13.refs_2_.refs_3_, ...), custom_call_target="tpu_custom_call" | custom-call | flops 3221225472 | bytes 1048576 | tf_op jit(solution)/shard_map/pallas_call | solution.py:36
  55.8 0.1 collective-permute-start.14
  55.9 9.7 %collective-permute-done.16.refs_1_.refs_4_ = bf16[64,4096]{1,0:T(8,128)(2,1)S(1)} collective-permute-done((bf16[64,4096]{1,0:T(8,128)(2,1)S(1)}, bf16[64,4096]{1,0:T(8,128)(2,1)S(1)}, u32[]{:S(2)}, u32[]{:S(2)}) %collective-permute-start.16) | collective-permute-done | bytes 524320 | tf_op jit(solution)/shard_map/ppermute | solution.py:288
  65.6 0.1 shard_map.98
  65.8 0.7 collective-permute-start.17
  66.5 3.0 %shard_map.96 = (f32[2,256,256]{2,1,0:T(8,128)S(1)}, f32[2,256,128]{2,1,0:T(8,128)S(1)}) custom-call(s32[2,128]{1,0:T(2,128)S(1)} %get-tuple-element.28.refs_0_, bf16[64,1024]{1,0:T(8,128)(2,1)S(1)} %get-tuple-element.29.refs_1_, bf16[1088,512]{1,0:T(8,128)(2,1)S(1)} %shard_map.87.refs_2_, bf16[1088,512]{1,0:T(8,128)(2,1)S(1)} %collective-permute-done.10.refs_3_, ...), custom_call_target="tpu_custom_call" | custom-call | flops 3221225472 | bytes 3145728 | tf_op jit(solution)/shard_map/pallas_call | solution.py:36
  69.5 3.0 %shard_map.97.refs_0_ = bf16[64,4096]{1,0:T(8,128)(2,1)S(1)} custom-call(s32[2,128]{1,0:T(2,128)S(1)} %get-tuple-element.28.refs_0_, bf16[64,1024]{1,0:T(8,128)(2,1)S(1)} %get-tuple-element.29.refs_1_, bf16[512,512]{1,0:T(8,128)(2,1)S(1)} %shard_map.89.refs_2_, bf16[512,512]{1,0:T(8,128)(2,1)S(1)} %collective-permute-done.13.refs_2_.refs_3_, ...), custom_call_target="tpu_custom_call" | custom-call | flops 3221225472 | bytes 1048576 | tf_op jit(solution)/shard_map/pallas_call | solution.py:36
  72.5 4.1 %collective-permute-done.14.refs_1_ = bf16[64,4096]{1,0:T(8,128)(2,1)S(1)} collective-permute-done((bf16[64,4096]{1,0:T(8,128)(2,1)S(1)}, bf16[64,4096]{1,0:T(8,128)(2,1)S(1)}, u32[]{:S(2)}, u32[]{:S(2)}) %collective-permute-start.14) | collective-permute-done | bytes 524320 | tf_op jit(solution)/shard_map/ppermute | solution.py:288
  76.6 0.0 collective-permute-done.15.refs_2_
  76.6 0.0 collective-permute-done.17.refs_3_
  76.6 1.1 %shard_map.99 = bf16[64,4096]{1,0:T(8,128)(2,1)} custom-call(bf16[64,4096]{1,0:T(8,128)(2,1)S(1)} %shard_map.97.refs_0_, bf16[64,4096]{1,0:T(8,128)(2,1)S(1)} %collective-permute-done.14.refs_1_, bf16[64,4096]{1,0:T(8,128)(2,1)S(1)} %collective-permute-done.15.refs_2_, bf16[64,4096]{1,0:T(8,128)(2,1)S(1)} %collective-permute-done.17.refs_3_, ...), custom_call_target="tpu_custom_call" | custom-call | tf_op jit(solution)/shard_map/pallas_call | solution.py:36
  (6 shorter events, 0.1 us)
Async XLA Ops:
  2.4 12.2 %collective-permute-start.6 = (bf16[272,512]{1,0:T(8,128)(2,1)}, bf16[272,512]{1,0:T(8,128)(2,1)S(1)}, u32[]{:S(2)}, u32[]{:S(2)}) collective-permute-start(bf16[272,512]{1,0:T(8,128)(2,1)} %get-tuple-element.36), channel_id=1, source_target_pairs={{0,8},{4,20},{8,0},{12,28},{16,24},{20,4},{24,16},{28,12},{1,9},{5... | collective-permute-start | bytes 835592 | tf_op jit(solution)/shard_map/ppermute | solution.py:278
  5.3 7.1 %collective-permute-start = (bf16[64,512]{1,0:T(8,128)(2,1)}, bf16[64,512]{1,0:T(8,128)(2,1)S(1)}, u32[]{:S(2)}, u32[]{:S(2)}) collective-permute-start(bf16[64,512]{1,0:T(8,128)(2,1)} %get-tuple-element.31), channel_id=1, source_target_pairs={{0,3},{1,2},{2,1},{3,0},{4,7},{5,6},{6,5},{7,4},{8,11},{9,10},{10,... | collective-permute-start | bytes 196616 | tf_op jit(solution)/shard_map/ppermute | solution.py:273
  8.9 5.6 %collective-permute-start.1 = (bf16[64,512]{1,0:T(8,128)(2,1)}, bf16[64,512]{1,0:T(8,128)(2,1)S(1)}, u32[]{:S(2)}, u32[]{:S(2)}) collective-permute-start(bf16[64,512]{1,0:T(8,128)(2,1)} %get-tuple-element.32), channel_id=1, source_target_pairs={{0,2},{1,3},{2,0},{3,1},{4,6},{5,7},{6,4},{7,5},{8,10},{9,11},{10,... | collective-permute-start | bytes 196616 | tf_op jit(solution)/shard_map/ppermute | solution.py:273
  8.9 5.7 %collective-permute-start.2 = (bf16[64,512]{1,0:T(8,128)(2,1)}, bf16[64,512]{1,0:T(8,128)(2,1)S(1)}, u32[]{:S(2)}, u32[]{:S(2)}) collective-permute-start(bf16[64,512]{1,0:T(8,128)(2,1)} %get-tuple-element.33), channel_id=1, source_target_pairs={{0,1},{1,0},{2,3},{3,2},{4,5},{5,4},{6,7},{7,6},{8,9},{9,8},{10,11... | collective-permute-start | bytes 196616 | tf_op jit(solution)/shard_map/ppermute | solution.py:273
  9.7 15.1 %collective-permute-start.7 = (bf16[272,512]{1,0:T(8,128)(2,1)}, bf16[272,512]{1,0:T(8,128)(2,1)S(1)}, u32[]{:S(2)}, u32[]{:S(2)}) collective-permute-start(bf16[272,512]{1,0:T(8,128)(2,1)} %get-tuple-element.36), channel_id=1, source_target_pairs={{0,16},{4,12},{8,24},{12,4},{16,0},{20,28},{24,8},{28,20},{1,17},{... | collective-permute-start | bytes 835592 | tf_op jit(solution)/shard_map/ppermute | solution.py:278
  11.2 1.0 %copy-start = (bf16[480,512]{1,0:T(8,128)(2,1)S(1)}, bf16[480,512]{1,0:T(8,128)(2,1)}, u32[]{:S(2)}) copy-start(bf16[480,512]{1,0:T(8,128)(2,1)} %get-tuple-element.27.refs_0_) | copy-start | bytes 1474564
  12.3 4.5 %copy-start.3 = (bf16[64,1024]{1,0:T(8,128)(2,1)S(1)}, bf16[64,1024]{1,0:T(8,128)(2,1)}, u32[]{:S(2)}) copy-start(bf16[64,1024]{1,0:T(8,128)(2,1)} %get-tuple-element.34) | copy-start | bytes 393220
  12.3 6.3 %copy-start.2 = (bf16[64,1024]{1,0:T(8,128)(2,1)S(1)}, bf16[64,1024]{1,0:T(8,128)(2,1)}, u32[]{:S(2)}) copy-start(bf16[64,1024]{1,0:T(8,128)(2,1)} %get-tuple-element.37) | copy-start | bytes 393220
  14.6 12.5 %copy-start.1 = (bf16[64,1024]{1,0:T(8,128)(2,1)S(1)}, bf16[64,1024]{1,0:T(8,128)(2,1)}, u32[]{:S(2)}) copy-start(bf16[64,1024]{1,0:T(8,128)(2,1)} %get-tuple-element.39) | copy-start | bytes 393220
  14.7 10.2 %collective-permute-start.8 = (bf16[272,512]{1,0:T(8,128)(2,1)S(1)}, bf16[272,512]{1,0:T(8,128)(2,1)S(1)}, u32[]{:S(2)}, u32[]{:S(2)}) collective-permute-start(bf16[272,512]{1,0:T(8,128)(2,1)S(1)} %shard_map.86), channel_id=1, source_target_pairs={{0,16},{4,12},{8,24},{12,4},{16,0},{20,28},{24,8},{28,20},{1,17},{... | collective-permute-start | bytes 835592 | tf_op jit(solution)/shard_map/ppermute | solution.py:278
  16.0 8.9 %collective-permute-start.3 = (bf16[256,512]{1,0:T(8,128)(2,1)S(1)}, bf16[256,512]{1,0:T(8,128)(2,1)S(1)}, u32[]{:S(2)}, u32[]{:S(2)}) collective-permute-start(bf16[256,512]{1,0:T(8,128)(2,1)S(1)} %shard_map.84.refs_0_.refs_1_), channel_id=1, source_target_pairs={{0,8},{4,20},{8,0},{12,28},{16,24},{20,4},{24,16},{28,12},{1,9},{5... | collective-permute-start | bytes 786440 | tf_op jit(solution)/shard_map/ppermute | solution.py:278
  16.8 8.0 %collective-permute-start.5 = (bf16[64,1024]{1,0:T(8,128)(2,1)S(1)}, bf16[64,1024]{1,0:T(8,128)(2,1)S(1)}, u32[]{:S(2)}, u32[]{:S(2)}) collective-permute-start(bf16[64,1024]{1,0:T(8,128)(2,1)S(1)} %copy-done.3), channel_id=1, source_target_pairs={{0,2},{1,3},{2,0},{3,1},{4,6},{5,7},{6,4},{7,5},{8,10},{9,11},{10,... | collective-permute-start | bytes 393224 | tf_op jit(solution)/shard_map/ppermute | solution.py:273
  18.5 6.3 %collective-permute-start.9 = (bf16[64,1024]{1,0:T(8,128)(2,1)S(1)}, bf16[64,1024]{1,0:T(8,128)(2,1)S(1)}, u32[]{:S(2)}, u32[]{:S(2)}) collective-permute-start(bf16[64,1024]{1,0:T(8,128)(2,1)S(1)} %copy-done.2), channel_id=1, source_target_pairs={{0,1},{1,0},{2,3},{3,2},{4,5},{5,4},{6,7},{7,6},{8,9},{9,8},{10,11... | collective-permute-start | bytes 393224 | tf_op jit(solution)/shard_map/ppermute | solution.py:273
  24.9 12.0 %slice-start = ((s8[8388608]{0:T(1024)(128)(4,1)}), s8[4194304]{0:T(1024)(128)(4,1)S(1)}, s32[]{:S(2)}) async-start(s8[8388608]{0:T(1024)(128)(4,1)} %bitcast), calls=%async_computation | async-start | bytes 8388608
  25.0 4.6 %collective-permute-start.10 = (bf16[1088,512]{1,0:T(8,128)(2,1)S(1)}, bf16[1088,512]{1,0:T(8,128)(2,1)S(1)}, u32[]{:S(2)}, u32[]{:S(2)}) collective-permute-start(bf16[1088,512]{1,0:T(8,128)(2,1)S(1)} %shard_map.87.refs_2_), channel_id=1, source_target_pairs={{0,4},{4,0},{8,12},{12,8},{16,20},{20,16},{24,28},{28,24},{1,5},{5... | collective-permute-start | bytes 3342344 | tf_op jit(solution)/shard_map/ppermute | solution.py:273
  25.1 4.4 %collective-permute-start.11 = (bf16[512,512]{1,0:T(8,128)(2,1)S(1)}, bf16[512,512]{1,0:T(8,128)(2,1)S(1)}, u32[]{:S(2)}, u32[]{:S(2)}) collective-permute-start(bf16[512,512]{1,0:T(8,128)(2,1)S(1)} %shard_map.85.refs_4_), channel_id=1, source_target_pairs={{0,4},{4,0},{8,12},{12,8},{16,20},{20,16},{24,28},{28,24},{1,5},{5... | collective-permute-start | bytes 1572872 | tf_op jit(solution)/shard_map/ppermute | solution.py:273
  25.7 9.2 %collective-permute-start.4 = (bf16[512,512]{1,0:T(8,128)(2,1)S(1)}, bf16[512,512]{1,0:T(8,128)(2,1)S(1)}, u32[]{:S(2)}, u32[]{:S(2)}) collective-permute-start(bf16[512,512]{1,0:T(8,128)(2,1)S(1)} %shard_map.85.refs_4_), channel_id=1, source_target_pairs={{0,16},{4,12},{8,24},{12,4},{16,0},{20,28},{24,8},{28,20},{1,17},{... | collective-permute-start | bytes 1572872 | tf_op jit(solution)/shard_map/ppermute | solution.py:278
  27.1 6.8 %collective-permute-start.12 = (bf16[64,1024]{1,0:T(8,128)(2,1)S(1)}, bf16[64,1024]{1,0:T(8,128)(2,1)S(1)}, u32[]{:S(2)}, u32[]{:S(2)}) collective-permute-start(bf16[64,1024]{1,0:T(8,128)(2,1)S(1)} %copy-done.1), channel_id=1, source_target_pairs={{0,3},{1,2},{2,1},{3,0},{4,7},{5,6},{6,5},{7,4},{8,11},{9,10},{10,... | collective-permute-start | bytes 393224 | tf_op jit(solution)/shard_map/ppermute | solution.py:273
  29.5 7.3 %slice-start.1 = ((s8[8388608]{0:T(1024)(128)(4,1)}), s8[4194304]{0:T(1024)(128)(4,1)S(1)}, s32[]{:S(2)}) async-start(s8[8388608]{0:T(1024)(128)(4,1)} %bitcast), calls=%async_computation.1 | async-start | bytes 8388608
  34.9 2.0 %collective-permute-start.13 = (bf16[512,512]{1,0:T(8,128)(2,1)S(1)}, bf16[512,512]{1,0:T(8,128)(2,1)S(1)}, u32[]{:S(2)}, u32[]{:S(2)}) collective-permute-start(bf16[512,512]{1,0:T(8,128)(2,1)S(1)} %shard_map.89.refs_2_), channel_id=1, source_target_pairs={{0,4},{4,0},{8,12},{12,8},{16,20},{20,16},{24,28},{28,24},{1,5},{5... | collective-permute-start | bytes 1572872 | tf_op jit(solution)/shard_map/ppermute | solution.py:273
  39.2 26.4 %collective-permute-start.16 = (bf16[64,4096]{1,0:T(8,128)(2,1)S(1)}, bf16[64,4096]{1,0:T(8,128)(2,1)S(1)}, u32[]{:S(2)}, u32[]{:S(2)}) collective-permute-start(bf16[64,4096]{1,0:T(8,128)(2,1)S(1)} %shard_map.91.refs_6_.refs_7_), channel_id=1, source_target_pairs={{0,1},{1,3},{2,0},{3,2},{4,5},{5,7},{6,4},{7,6},{8,9},{9,11},{10,8... | collective-permute-start | bytes 1572872 | tf_op jit(solution)/shard_map/ppermute | solution.py:288
  45.8 30.9 %collective-permute-start.15 = (bf16[64,4096]{1,0:T(8,128)(2,1)S(1)}, bf16[64,4096]{1,0:T(8,128)(2,1)S(1)}, u32[]{:S(2)}, u32[]{:S(2)}) collective-permute-start(bf16[64,4096]{1,0:T(8,128)(2,1)S(1)} %shard_map.93.refs_6_.refs_7_.refs_0_), channel_id=1, source_target_pairs={{0,3},{3,0},{4,7},{7,4},{8,11},{11,8},{12,15},{15,12},{16,19},{19,... | collective-permute-start | bytes 1572872 | tf_op jit(solution)/shard_map/ppermute | solution.py:288
  55.8 20.8 %collective-permute-start.14 = (bf16[64,4096]{1,0:T(8,128)(2,1)S(1)}, bf16[64,4096]{1,0:T(8,128)(2,1)S(1)}, u32[]{:S(2)}, u32[]{:S(2)}) collective-permute-start(bf16[64,4096]{1,0:T(8,128)(2,1)S(1)} %shard_map.95.refs_6_.refs_7_), channel_id=1, source_target_pairs={{0,1},{1,0},{2,3},{3,2},{4,5},{5,4},{6,7},{7,6},{8,9},{9,8},{10,11... | collective-permute-start | bytes 1572872 | tf_op jit(solution)/shard_map/ppermute | solution.py:288
  65.8 10.9 %collective-permute-start.17 = (bf16[64,4096]{1,0:T(8,128)(2,1)S(1)}, bf16[64,4096]{1,0:T(8,128)(2,1)S(1)}, u32[]{:S(2)}, u32[]{:S(2)}) collective-permute-start(bf16[64,4096]{1,0:T(8,128)(2,1)S(1)} %shard_map.98), channel_id=1, source_target_pairs={{1,2},{2,1},{5,6},{6,5},{9,10},{10,9},{13,14},{14,13},{17,18},{18,... | collective-permute-start | bytes 1572872 | tf_op jit(solution)/shard_map/ppermute | solution.py:288

commit v8 on v7

--- a/solution.py
+++ b/solution.py
@@ -284,6 +284,38 @@
     return [b for pair in blocks for b in (pair, swap(pair, "ctx", 1))]
 
 
+def finish_kernel(count, *refs):
+    out, total, sems = refs[-3:]
+    head = lax.axis_index("head")
+    last = refs[count]
+    step = out.shape[1] // 4
+    copies = []
+    for n in range(4):
+        columns = pl.ds(n * step, step)
+        part = refs[0][:, columns].astype(F32)
+        for ref in refs[1:count]:
+            part += ref[:, columns].astype(F32)
+        at_end = (head == 0) | (head == lax.axis_size("head") - 1)
+        part += jnp.where(at_end, last[:, columns].astype(F32), 0.0)
+        total[:, columns] = part.astype(BF16)
+        copies.append(pltpu.make_async_copy(total.at[:, columns], out.at[:, columns], sems.at[n]))
+        copies[-1].start()
+    for copy in copies:
+        copy.wait()
+
+
+def finish(parts, at_ends):
+    shape = parts[0].shape
+    return pl.pallas_call(
+        functools.partial(finish_kernel, len(parts)),
+        out_shape=shaped(*shape),
+        in_specs=[pl.BlockSpec(memory_space=pltpu.VMEM)] * (len(parts) + 1),
+        out_specs=pl.BlockSpec(memory_space=pl.ANY),
+        scratch_shapes=[pltpu.VMEM(shape, BF16), pltpu.SemaphoreType.DMA((4,))],
+        compiler_params=pltpu.CompilerParams(vmem_limit_bytes=6 * MIB),
+    )(*parts, at_ends)
+
+
 def send(value, pairs):
     return lax.ppermute(value, "head", pairs)
 
@@ -297,7 +329,7 @@
     own, = part((0,), near)
     near = send(near, [(0, 1), (1, 0), (2, 3), (3, 2)])
     middle = send(add([far, first]), [(1, 2), (2, 1)])
-    return add([own, near, ends, middle], [first])
+    return finish([own, near, ends, middle], first)
 
 
 def scatter_direct(part, n_head):

time: 78 us -> 78 us (level)
    pallas_call x18 -> x17, Pallas kernels: 28 us -> 26.9 us  [call(): pl.pallas_call(body, out_shape=outs, in_specs=specs + [pl.BlockSpec(memor...]
    pallas_call x0 -> x1, Pallas kernels: none -> 1.05 us  [finish(): pl.pallas_call(functools.partial(finish_kernel, len(parts)), out_shape=sh...]
where the time goes in v8:
time: 78 us; the launch traced here: 77.8 us
  Pallas kernels  27.9 us (36%)
  waiting for transfers between devices  24.6 us (32%)
  starting transfers between devices  23.9 us (31%)
  local copies, waits for them, and re-layouts  1.05 us (1%)
    pallas_call x17, Pallas kernels, call(): pl.pallas_call(body, out_shape=outs, in_specs=specs + [pl.BlockSpec(memor...  26.9 us
    ppermute x4, waiting for transfers between devices, send(): return lax.ppermute(value, 'head', pairs)  13.9 us
    ppermute x9, starting transfers between devices, swap(): lax.ppermute(value, axis, [(i, i ^ mask) for i in range(lax.axis_size(axi...  10.6 us
    ppermute x9, waiting for transfers between devices, swap(): lax.ppermute(value, axis, [(i, i ^ mask) for i in range(lax.axis_size(axi...  9.77 us
    ppermute x5, starting transfers between devices, leg(): lax.ppermute(block, 'ctx', [(i, i ^ (odd if i % 2 else even)) for i in ra...  7.99 us
    ppermute x4, starting transfers between devices, send(): return lax.ppermute(value, 'head', pairs)  5.36 us
  transfers between devices with their start and end apart: 18, of which 10 were waited for; matrix products, arithmetic and copies ran while one was open for 0% of the time, Pallas kernels for 28%

profile of v8, /device:TPU:0, one launch (start us, length us, event | category | flops | bytes accessed | tf_op | source)
XLA Modules:
  0.0 77.8 jit_solution(9898778296374128713)
XLA Ops:
  0.0 2.4 %shard_map.82 = (bf16[64,512]{1,0:T(8,128)(2,1)}, bf16[64,512]{1,0:T(8,128)(2,1)}, bf16[64,512]{1,0:T(8,128)(2,1)}, bf16[64,1024]{1,0:T(8,128)(2,1)}, bf16[64,10...) custom-call(s32[2]{0:T(128)} %refs_0_.1, s32[16]{0:T(128)} %refs_1_.1, ...), custom_call_target="tpu_custom_call" | custom-call | tf_op jit(solution)/shard_map/pallas_call | solution.py:36
  2.4 2.9 %collective-permute-start.6 = (bf16[272,512]{1,0:T(8,128)(2,1)}, bf16[272,512]{1,0:T(8,128)(2,1)S(1)}, u32[]{:S(2)}, u32[]{:S(2)}) collective-permute-start(bf16[272,512]{1,0:T(8,128)(2,1)} %get-tuple-element.36), channel_id=1, source_target_pairs={{0,8},{4,20},{8,0},{12,28},{16,24},{20,4},{24,16},{28,12},{1,9},{5... | collective-permute-start | bytes 835592 | tf_op jit(solution)/shard_map/ppermute | solution.py:278
  5.3 3.6 %collective-permute-start = (bf16[64,512]{1,0:T(8,128)(2,1)}, bf16[64,512]{1,0:T(8,128)(2,1)S(1)}, u32[]{:S(2)}, u32[]{:S(2)}) collective-permute-start(bf16[64,512]{1,0:T(8,128)(2,1)} %get-tuple-element.31), channel_id=1, source_target_pairs={{0,3},{1,2},{2,1},{3,0},{4,7},{5,6},{6,5},{7,4},{8,11},{9,10},{10,... | collective-permute-start | bytes 196616 | tf_op jit(solution)/shard_map/ppermute | solution.py:273
  8.9 0.0 collective-permute-start.1
  8.9 0.8 %collective-permute-start.2 = (bf16[64,512]{1,0:T(8,128)(2,1)}, bf16[64,512]{1,0:T(8,128)(2,1)S(1)}, u32[]{:S(2)}, u32[]{:S(2)}) collective-permute-start(bf16[64,512]{1,0:T(8,128)(2,1)} %get-tuple-element.33), channel_id=1, source_target_pairs={{0,1},{1,0},{2,3},{3,2},{4,5},{5,4},{6,7},{7,6},{8,9},{9,8},{10,11... | collective-permute-start | bytes 196616 | tf_op jit(solution)/shard_map/ppermute | solution.py:273
  9.7 1.5 %collective-permute-start.7 = (bf16[272,512]{1,0:T(8,128)(2,1)}, bf16[272,512]{1,0:T(8,128)(2,1)S(1)}, u32[]{:S(2)}, u32[]{:S(2)}) collective-permute-start(bf16[272,512]{1,0:T(8,128)(2,1)} %get-tuple-element.36), channel_id=1, source_target_pairs={{0,16},{4,12},{8,24},{12,4},{16,0},{20,28},{24,8},{28,20},{1,17},{... | collective-permute-start | bytes 835592 | tf_op jit(solution)/shard_map/ppermute | solution.py:278
  11.2 0.0 copy-start
  11.3 1.0 %copy-done = bf16[480,512]{1,0:T(8,128)(2,1)S(1)} copy-done((bf16[480,512]{1,0:T(8,128)(2,1)S(1)}, bf16[480,512]{1,0:T(8,128)(2,1)}, u32[]{:S(2)}) %copy-start) | copy-done | bytes 491544
  12.3 0.0 copy-start.3
  12.3 0.0 copy-start.2
  12.3 0.1 collective-permute-done.refs_1_
  12.4 2.2 %collective-permute-done.1.refs_2_ = bf16[64,512]{1,0:T(8,128)(2,1)S(1)} collective-permute-done((bf16[64,512]{1,0:T(8,128)(2,1)}, bf16[64,512]{1,0:T(8,128)(2,1)S(1)}, u32[]{:S(2)}, u32[]{:S(2)}) %collective-permute-start.1) | collective-permute-done | bytes 65568 | tf_op jit(solution)/shard_map/ppermute | solution.py:273
  14.6 0.1 collective-permute-done.2.refs_3_
  14.6 0.0 collective-permute-done.6.refs_0_.refs_1_
  14.6 0.0 copy-start.1
  14.7 1.3 %collective-permute-start.8 = (bf16[272,512]{1,0:T(8,128)(2,1)S(1)}, bf16[272,512]{1,0:T(8,128)(2,1)S(1)}, u32[]{:S(2)}, u32[]{:S(2)}) collective-permute-start(bf16[272,512]{1,0:T(8,128)(2,1)S(1)} %shard_map.86), channel_id=1, source_target_pairs={{0,16},{4,12},{8,24},{12,4},{16,0},{20,28},{24,8},{28,20},{1,17},{... | collective-permute-start | bytes 835592 | tf_op jit(solution)/shard_map/ppermute | solution.py:278
  16.0 0.8 collective-permute-start.3
  16.7 0.0 copy-done.3
  16.8 1.8 %collective-permute-start.5 = (bf16[64,1024]{1,0:T(8,128)(2,1)S(1)}, bf16[64,1024]{1,0:T(8,128)(2,1)S(1)}, u32[]{:S(2)}, u32[]{:S(2)}) collective-permute-start(bf16[64,1024]{1,0:T(8,128)(2,1)S(1)} %copy-done.3), channel_id=1, source_target_pairs={{0,2},{1,3},{2,0},{3,1},{4,6},{5,7},{6,4},{7,5},{8,10},{9,11},{10,... | collective-permute-start | bytes 393224 | tf_op jit(solution)/shard_map/ppermute | solution.py:273
  18.5 0.0 copy-done.2
  18.5 1.3 %collective-permute-start.9 = (bf16[64,1024]{1,0:T(8,128)(2,1)S(1)}, bf16[64,1024]{1,0:T(8,128)(2,1)S(1)}, u32[]{:S(2)}, u32[]{:S(2)}) collective-permute-start(bf16[64,1024]{1,0:T(8,128)(2,1)S(1)} %copy-done.2), channel_id=1, source_target_pairs={{0,1},{1,0},{2,3},{3,2},{4,5},{5,4},{6,7},{7,6},{8,9},{9,8},{10,11... | collective-permute-start | bytes 393224 | tf_op jit(solution)/shard_map/ppermute | solution.py:273
  19.9 4.9 %collective-permute-done.5.refs_6_.refs_1_ = bf16[64,1024]{1,0:T(8,128)(2,1)S(1)} collective-permute-done((bf16[64,1024]{1,0:T(8,128)(2,1)S(1)}, bf16[64,1024]{1,0:T(8,128)(2,1)S(1)}, u32[]{:S(2)}, u32[]{:S(2)}) %collective-permute-start.5) | collective-permute-done | bytes 131104 | tf_op jit(solution)/shard_map/ppermute | solution.py:273
  24.8 0.1 collective-permute-done.9.refs_5_.refs_1_
  24.9 0.0 collective-permute-done.7.refs_2_
  24.9 0.0 collective-permute-done.3.refs_1_.refs_4_
  24.9 0.0 collective-permute-done.8.refs_3_
  24.9 0.0 slice-start
  24.9 0.1 shard_map.87.refs_2_
  25.0 0.1 collective-permute-start.10
  25.1 0.6 collective-permute-start.11
  25.7 1.5 %collective-permute-start.4 = (bf16[512,512]{1,0:T(8,128)(2,1)S(1)}, bf16[512,512]{1,0:T(8,128)(2,1)S(1)}, u32[]{:S(2)}, u32[]{:S(2)}) collective-permute-start(bf16[512,512]{1,0:T(8,128)(2,1)S(1)} %shard_map.85.refs_4_), channel_id=1, source_target_pairs={{0,16},{4,12},{8,24},{12,4},{16,0},{20,28},{24,8},{28,20},{1,17},{... | collective-permute-start | bytes 1572872 | tf_op jit(solution)/shard_map/ppermute | solution.py:278
  27.1 0.0 copy-done.1
  27.1 2.4 %collective-permute-start.12 = (bf16[64,1024]{1,0:T(8,128)(2,1)S(1)}, bf16[64,1024]{1,0:T(8,128)(2,1)S(1)}, u32[]{:S(2)}, u32[]{:S(2)}) collective-permute-start(bf16[64,1024]{1,0:T(8,128)(2,1)S(1)} %copy-done.1), channel_id=1, source_target_pairs={{0,3},{1,2},{2,1},{3,0},{4,7},{5,6},{6,5},{7,4},{8,11},{9,10},{10,... | collective-permute-start | bytes 393224 | tf_op jit(solution)/shard_map/ppermute | solution.py:273
  29.5 0.0 collective-permute-done.11.refs_5_
  29.5 0.0 collective-permute-done.10.refs_3_
  29.5 0.0 slice-start.1
  29.6 3.0 %shard_map.88 = (f32[2,256,256]{2,1,0:T(8,128)S(1)}, f32[2,256,128]{2,1,0:T(8,128)S(1)}) custom-call(s32[2,128]{1,0:T(2,128)S(1)} %get-tuple-element.28.refs_0_, bf16[64,1024]{1,0:T(8,128)(2,1)S(1)} %collective-permute-done.5.refs_6_.refs_1_, bf16[1088,512]{1,0:T(8,128)(2,1)S(1)} %shard_map.87.refs_2_, ...), custom_call_target="tpu_custom_call" | custom-call | flops 3221225472 | bytes 3145728 | tf_op jit(solution)/shard_map/pallas_call | solution.py:36
  32.6 1.4 %collective-permute-done.12.refs_2_.refs_1_ = bf16[64,1024]{1,0:T(8,128)(2,1)S(1)} collective-permute-done((bf16[64,1024]{1,0:T(8,128)(2,1)S(1)}, bf16[64,1024]{1,0:T(8,128)(2,1)S(1)}, u32[]{:S(2)}, u32[]{:S(2)}) %collective-permute-start.12) | collective-permute-done | bytes 131104 | tf_op jit(solution)/shard_map/ppermute | solution.py:273
  34.0 0.9 %collective-permute-done.4.refs_0_ = bf16[512,512]{1,0:T(8,128)(2,1)S(1)} collective-permute-done((bf16[512,512]{1,0:T(8,128)(2,1)S(1)}, bf16[512,512]{1,0:T(8,128)(2,1)S(1)}, u32[]{:S(2)}, u32[]{:S(2)}) %collective-permute-start.4) | collective-permute-done | bytes 524320 | tf_op jit(solution)/shard_map/ppermute | solution.py:278
  34.9 0.1 collective-permute-start.13
  35.0 0.8 %shard_map.90 = (f32[2,256,256]{2,1,0:T(8,128)S(1)}, f32[2,256,128]{2,1,0:T(8,128)S(1)}) custom-call(s32[2,128]{1,0:T(2,128)S(1)} %get-tuple-element.28.refs_0_, bf16[64,1024]{1,0:T(8,128)(2,1)S(1)} %collective-permute-done.5.refs_6_.refs_1_, bf16[512,512]{1,0:T(8,128)(2,1)S(1)} %shard_map.89.refs_2_), custom_call_target="tpu_custom_call" | custom-call | tf_op jit(solution)/shard_map/pallas_call | solution.py:36
  35.8 1.1 %collective-permute-done.13.refs_2_.refs_3_ = bf16[512,512]{1,0:T(8,128)(2,1)S(1)} collective-permute-done((bf16[512,512]{1,0:T(8,128)(2,1)S(1)}, bf16[512,512]{1,0:T(8,128)(2,1)S(1)}, u32[]{:S(2)}, u32[]{:S(2)}) %collective-permute-start.13) | collective-permute-done | bytes 524320 | tf_op jit(solution)/shard_map/ppermute | solution.py:273
  36.9 0.0 slice-done
  36.9 0.0 slice-done.1
  36.9 2.4 %shard_map.91.refs_6_.refs_7_ = bf16[64,4096]{1,0:T(8,128)(2,1)S(1)} custom-call(s32[2,128]{1,0:T(2,128)S(1)} %get-tuple-element.28.refs_0_, bf16[64,1024]{1,0:T(8,128)(2,1)S(1)} %collective-permute-done.5.refs_6_.refs_1_, bf16[512,512]{1,0:T(8,128)(2,1)S(1)} %collective-permute-done.13.refs_2_.refs_3_, f32[2,256,256]{2,1,0:T(8,128)S(1)} %get-tuple-element.40.refs_3_, ...), custom_call_target="tpu_custom_call" | custom-call | flops 2684354560 | bytes 524288 | tf_op jit(solution)/shard_map/pallas_call | solution.py:36
  39.2 0.6 collective-permute-start.16
  39.8 3.0 %shard_map.92 = (f32[2,256,256]{2,1,0:T(8,128)S(1)}, f32[2,256,128]{2,1,0:T(8,128)S(1)}) custom-call(s32[2,128]{1,0:T(2,128)S(1)} %get-tuple-element.28.refs_0_, bf16[64,1024]{1,0:T(8,128)(2,1)S(1)} %collective-permute-done.12.refs_2_.refs_1_, bf16[1088,512]{1,0:T(8,128)(2,1)S(1)} %shard_map.87.refs_2_, ...), custom_call_target="tpu_custom_call" | custom-call | flops 3221225472 | bytes 3145728 | tf_op jit(solution)/shard_map/pallas_call | solution.py:36
  42.8 3.0 %shard_map.93.refs_6_.refs_7_.refs_0_ = bf16[64,4096]{1,0:T(8,128)(2,1)S(1)} custom-call(s32[2,128]{1,0:T(2,128)S(1)} %get-tuple-element.28.refs_0_, bf16[64,1024]{1,0:T(8,128)(2,1)S(1)} %collective-permute-done.12.refs_2_.refs_1_, bf16[512,512]{1,0:T(8,128)(2,1)S(1)} %shard_map.89.refs_2_, bf16[512,512]{1,0:T(8,128)(2,1)S(1)} %collective-permute-done.13.refs_2_.refs_3_, ...), custom_call_target="tpu_custom_call" | custom-call | flops 3221225472 | bytes 1048576 | tf_op jit(solution)/shard_map/pallas_call | solution.py:36
  45.8 4.0 %collective-permute-start.15 = (bf16[64,4096]{1,0:T(8,128)(2,1)S(1)}, bf16[64,4096]{1,0:T(8,128)(2,1)S(1)}, u32[]{:S(2)}, u32[]{:S(2)}) collective-permute-start(bf16[64,4096]{1,0:T(8,128)(2,1)S(1)} %shard_map.93.refs_6_.refs_7_.refs_0_), channel_id=1, source_target_pairs={{0,3},{3,0},{4,7},{7,4},{8,11},{11,8},{12,15},{15,12},{16,19},{19,... | collective-permute-start | bytes 1572872 | tf_op jit(solution)/shard_map/ppermute | solution.py:320
  49.8 3.0 %shard_map.94 = (f32[2,256,256]{2,1,0:T(8,128)S(1)}, f32[2,256,128]{2,1,0:T(8,128)S(1)}) custom-call(s32[2,128]{1,0:T(2,128)S(1)} %get-tuple-element.28.refs_0_, bf16[64,1024]{1,0:T(8,128)(2,1)S(1)} %collective-permute-done.9.refs_5_.refs_1_, bf16[1088,512]{1,0:T(8,128)(2,1)S(1)} %shard_map.87.refs_2_, ...), custom_call_target="tpu_custom_call" | custom-call | flops 3221225472 | bytes 3145728 | tf_op jit(solution)/shard_map/pallas_call | solution.py:36
  52.8 3.0 %shard_map.95.refs_6_.refs_7_ = bf16[64,4096]{1,0:T(8,128)(2,1)S(1)} custom-call(s32[2,128]{1,0:T(2,128)S(1)} %get-tuple-element.28.refs_0_, bf16[64,1024]{1,0:T(8,128)(2,1)S(1)} %collective-permute-done.9.refs_5_.refs_1_, bf16[512,512]{1,0:T(8,128)(2,1)S(1)} %shard_map.89.refs_2_, bf16[512,512]{1,0:T(8,128)(2,1)S(1)} %collective-permute-done.13.refs_2_.refs_3_, ...), custom_call_target="tpu_custom_call" | custom-call | flops 3221225472 | bytes 1048576 | tf_op jit(solution)/shard_map/pallas_call | solution.py:36
  55.8 0.1 collective-permute-start.14
  55.9 9.7 %collective-permute-done.16.refs_1_.refs_4_ = bf16[64,4096]{1,0:T(8,128)(2,1)S(1)} collective-permute-done((bf16[64,4096]{1,0:T(8,128)(2,1)S(1)}, bf16[64,4096]{1,0:T(8,128)(2,1)S(1)}, u32[]{:S(2)}, u32[]{:S(2)}) %collective-permute-start.16) | collective-permute-done | bytes 524320 | tf_op jit(solution)/shard_map/ppermute | solution.py:320
  65.6 0.1 shard_map.98
  65.8 0.7 collective-permute-start.17
  66.5 3.0 %shard_map.96 = (f32[2,256,256]{2,1,0:T(8,128)S(1)}, f32[2,256,128]{2,1,0:T(8,128)S(1)}) custom-call(s32[2,128]{1,0:T(2,128)S(1)} %get-tuple-element.28.refs_0_, bf16[64,1024]{1,0:T(8,128)(2,1)S(1)} %get-tuple-element.29.refs_1_, bf16[1088,512]{1,0:T(8,128)(2,1)S(1)} %shard_map.87.refs_2_, bf16[1088,512]{1,0:T(8,128)(2,1)S(1)} %collective-permute-done.10.refs_3_, ...), custom_call_target="tpu_custom_call" | custom-call | flops 3221225472 | bytes 3145728 | tf_op jit(solution)/shard_map/pallas_call | solution.py:36
  69.5 3.0 %shard_map.97.refs_0_ = bf16[64,4096]{1,0:T(8,128)(2,1)S(1)} custom-call(s32[2,128]{1,0:T(2,128)S(1)} %get-tuple-element.28.refs_0_, bf16[64,1024]{1,0:T(8,128)(2,1)S(1)} %get-tuple-element.29.refs_1_, bf16[512,512]{1,0:T(8,128)(2,1)S(1)} %shard_map.89.refs_2_, bf16[512,512]{1,0:T(8,128)(2,1)S(1)} %collective-permute-done.13.refs_2_.refs_3_, ...), custom_call_target="tpu_custom_call" | custom-call | flops 3221225472 | bytes 1048576 | tf_op jit(solution)/shard_map/pallas_call | solution.py:36
  72.5 4.1 %collective-permute-done.14.refs_1_ = bf16[64,4096]{1,0:T(8,128)(2,1)S(1)} collective-permute-done((bf16[64,4096]{1,0:T(8,128)(2,1)S(1)}, bf16[64,4096]{1,0:T(8,128)(2,1)S(1)}, u32[]{:S(2)}, u32[]{:S(2)}) %collective-permute-start.14) | collective-permute-done | bytes 524320 | tf_op jit(solution)/shard_map/ppermute | solution.py:320
  76.6 0.0 collective-permute-done.15.refs_2_
  76.6 0.0 collective-permute-done.17.refs_3_
  76.6 1.1 %shard_map.99 = bf16[64,4096]{1,0:T(8,128)(2,1)} custom-call(bf16[64,4096]{1,0:T(8,128)(2,1)S(1)} %shard_map.97.refs_0_, bf16[64,4096]{1,0:T(8,128)(2,1)S(1)} %collective-permute-done.14.refs_1_, bf16[64,4096]{1,0:T(8,128)(2,1)S(1)} %collective-permute-done.15.refs_2_, bf16[64,4096]{1,0:T(8,128)(2,1)S(1)} %collective-permute-done.17.refs_3_, ...), custom_call_target="tpu_custom_call" | custom-call | tf_op jit(solution)/shard_map/pallas_call | solution.py:309
  (6 shorter events, 0.1 us)
Async XLA Ops:
  2.4 12.2 %collective-permute-start.6 = (bf16[272,512]{1,0:T(8,128)(2,1)}, bf16[272,512]{1,0:T(8,128)(2,1)S(1)}, u32[]{:S(2)}, u32[]{:S(2)}) collective-permute-start(bf16[272,512]{1,0:T(8,128)(2,1)} %get-tuple-element.36), channel_id=1, source_target_pairs={{0,8},{4,20},{8,0},{12,28},{16,24},{20,4},{24,16},{28,12},{1,9},{5... | collective-permute-start | bytes 835592 | tf_op jit(solution)/shard_map/ppermute | solution.py:278
  5.3 7.1 %collective-permute-start = (bf16[64,512]{1,0:T(8,128)(2,1)}, bf16[64,512]{1,0:T(8,128)(2,1)S(1)}, u32[]{:S(2)}, u32[]{:S(2)}) collective-permute-start(bf16[64,512]{1,0:T(8,128)(2,1)} %get-tuple-element.31), channel_id=1, source_target_pairs={{0,3},{1,2},{2,1},{3,0},{4,7},{5,6},{6,5},{7,4},{8,11},{9,10},{10,... | collective-permute-start | bytes 196616 | tf_op jit(solution)/shard_map/ppermute | solution.py:273
  8.9 5.6 %collective-permute-start.1 = (bf16[64,512]{1,0:T(8,128)(2,1)}, bf16[64,512]{1,0:T(8,128)(2,1)S(1)}, u32[]{:S(2)}, u32[]{:S(2)}) collective-permute-start(bf16[64,512]{1,0:T(8,128)(2,1)} %get-tuple-element.32), channel_id=1, source_target_pairs={{0,2},{1,3},{2,0},{3,1},{4,6},{5,7},{6,4},{7,5},{8,10},{9,11},{10,... | collective-permute-start | bytes 196616 | tf_op jit(solution)/shard_map/ppermute | solution.py:273
  8.9 5.7 %collective-permute-start.2 = (bf16[64,512]{1,0:T(8,128)(2,1)}, bf16[64,512]{1,0:T(8,128)(2,1)S(1)}, u32[]{:S(2)}, u32[]{:S(2)}) collective-permute-start(bf16[64,512]{1,0:T(8,128)(2,1)} %get-tuple-element.33), channel_id=1, source_target_pairs={{0,1},{1,0},{2,3},{3,2},{4,5},{5,4},{6,7},{7,6},{8,9},{9,8},{10,11... | collective-permute-start | bytes 196616 | tf_op jit(solution)/shard_map/ppermute | solution.py:273
  9.7 15.1 %collective-permute-start.7 = (bf16[272,512]{1,0:T(8,128)(2,1)}, bf16[272,512]{1,0:T(8,128)(2,1)S(1)}, u32[]{:S(2)}, u32[]{:S(2)}) collective-permute-start(bf16[272,512]{1,0:T(8,128)(2,1)} %get-tuple-element.36), channel_id=1, source_target_pairs={{0,16},{4,12},{8,24},{12,4},{16,0},{20,28},{24,8},{28,20},{1,17},{... | collective-permute-start | bytes 835592 | tf_op jit(solution)/shard_map/ppermute | solution.py:278
  11.2 1.0 %copy-start = (bf16[480,512]{1,0:T(8,128)(2,1)S(1)}, bf16[480,512]{1,0:T(8,128)(2,1)}, u32[]{:S(2)}) copy-start(bf16[480,512]{1,0:T(8,128)(2,1)} %get-tuple-element.27.refs_0_) | copy-start | bytes 1474564
  12.3 4.5 %copy-start.3 = (bf16[64,1024]{1,0:T(8,128)(2,1)S(1)}, bf16[64,1024]{1,0:T(8,128)(2,1)}, u32[]{:S(2)}) copy-start(bf16[64,1024]{1,0:T(8,128)(2,1)} %get-tuple-element.34) | copy-start | bytes 393220
  12.3 6.3 %copy-start.2 = (bf16[64,1024]{1,0:T(8,128)(2,1)S(1)}, bf16[64,1024]{1,0:T(8,128)(2,1)}, u32[]{:S(2)}) copy-start(bf16[64,1024]{1,0:T(8,128)(2,1)} %get-tuple-element.37) | copy-start | bytes 393220
  14.6 12.5 %copy-start.1 = (bf16[64,1024]{1,0:T(8,128)(2,1)S(1)}, bf16[64,1024]{1,0:T(8,128)(2,1)}, u32[]{:S(2)}) copy-start(bf16[64,1024]{1,0:T(8,128)(2,1)} %get-tuple-element.39) | copy-start | bytes 393220
  14.7 10.2 %collective-permute-start.8 = (bf16[272,512]{1,0:T(8,128)(2,1)S(1)}, bf16[272,512]{1,0:T(8,128)(2,1)S(1)}, u32[]{:S(2)}, u32[]{:S(2)}) collective-permute-start(bf16[272,512]{1,0:T(8,128)(2,1)S(1)} %shard_map.86), channel_id=1, source_target_pairs={{0,16},{4,12},{8,24},{12,4},{16,0},{20,28},{24,8},{28,20},{1,17},{... | collective-permute-start | bytes 835592 | tf_op jit(solution)/shard_map/ppermute | solution.py:278
  16.0 8.9 %collective-permute-start.3 = (bf16[256,512]{1,0:T(8,128)(2,1)S(1)}, bf16[256,512]{1,0:T(8,128)(2,1)S(1)}, u32[]{:S(2)}, u32[]{:S(2)}) collective-permute-start(bf16[256,512]{1,0:T(8,128)(2,1)S(1)} %shard_map.84.refs_0_.refs_1_), channel_id=1, source_target_pairs={{0,8},{4,20},{8,0},{12,28},{16,24},{20,4},{24,16},{28,12},{1,9},{5... | collective-permute-start | bytes 786440 | tf_op jit(solution)/shard_map/ppermute | solution.py:278
  16.8 8.0 %collective-permute-start.5 = (bf16[64,1024]{1,0:T(8,128)(2,1)S(1)}, bf16[64,1024]{1,0:T(8,128)(2,1)S(1)}, u32[]{:S(2)}, u32[]{:S(2)}) collective-permute-start(bf16[64,1024]{1,0:T(8,128)(2,1)S(1)} %copy-done.3), channel_id=1, source_target_pairs={{0,2},{1,3},{2,0},{3,1},{4,6},{5,7},{6,4},{7,5},{8,10},{9,11},{10,... | collective-permute-start | bytes 393224 | tf_op jit(solution)/shard_map/ppermute | solution.py:273
  18.5 6.3 %collective-permute-start.9 = (bf16[64,1024]{1,0:T(8,128)(2,1)S(1)}, bf16[64,1024]{1,0:T(8,128)(2,1)S(1)}, u32[]{:S(2)}, u32[]{:S(2)}) collective-permute-start(bf16[64,1024]{1,0:T(8,128)(2,1)S(1)} %copy-done.2), channel_id=1, source_target_pairs={{0,1},{1,0},{2,3},{3,2},{4,5},{5,4},{6,7},{7,6},{8,9},{9,8},{10,11... | collective-permute-start | bytes 393224 | tf_op jit(solution)/shard_map/ppermute | solution.py:273
  24.9 12.0 %slice-start = ((s8[8388608]{0:T(1024)(128)(4,1)}), s8[4194304]{0:T(1024)(128)(4,1)S(1)}, s32[]{:S(2)}) async-start(s8[8388608]{0:T(1024)(128)(4,1)} %bitcast), calls=%async_computation | async-start | bytes 8388608
  25.0 4.6 %collective-permute-start.10 = (bf16[1088,512]{1,0:T(8,128)(2,1)S(1)}, bf16[1088,512]{1,0:T(8,128)(2,1)S(1)}, u32[]{:S(2)}, u32[]{:S(2)}) collective-permute-start(bf16[1088,512]{1,0:T(8,128)(2,1)S(1)} %shard_map.87.refs_2_), channel_id=1, source_target_pairs={{0,4},{4,0},{8,12},{12,8},{16,20},{20,16},{24,28},{28,24},{1,5},{5... | collective-permute-start | bytes 3342344 | tf_op jit(solution)/shard_map/ppermute | solution.py:273
  25.1 4.4 %collective-permute-start.11 = (bf16[512,512]{1,0:T(8,128)(2,1)S(1)}, bf16[512,512]{1,0:T(8,128)(2,1)S(1)}, u32[]{:S(2)}, u32[]{:S(2)}) collective-permute-start(bf16[512,512]{1,0:T(8,128)(2,1)S(1)} %shard_map.85.refs_4_), channel_id=1, source_target_pairs={{0,4},{4,0},{8,12},{12,8},{16,20},{20,16},{24,28},{28,24},{1,5},{5... | collective-permute-start | bytes 1572872 | tf_op jit(solution)/shard_map/ppermute | solution.py:273
  25.7 9.2 %collective-permute-start.4 = (bf16[512,512]{1,0:T(8,128)(2,1)S(1)}, bf16[512,512]{1,0:T(8,128)(2,1)S(1)}, u32[]{:S(2)}, u32[]{:S(2)}) collective-permute-start(bf16[512,512]{1,0:T(8,128)(2,1)S(1)} %shard_map.85.refs_4_), channel_id=1, source_target_pairs={{0,16},{4,12},{8,24},{12,4},{16,0},{20,28},{24,8},{28,20},{1,17},{... | collective-permute-start | bytes 1572872 | tf_op jit(solution)/shard_map/ppermute | solution.py:278
  27.1 6.8 %collective-permute-start.12 = (bf16[64,1024]{1,0:T(8,128)(2,1)S(1)}, bf16[64,1024]{1,0:T(8,128)(2,1)S(1)}, u32[]{:S(2)}, u32[]{:S(2)}) collective-permute-start(bf16[64,1024]{1,0:T(8,128)(2,1)S(1)} %copy-done.1), channel_id=1, source_target_pairs={{0,3},{1,2},{2,1},{3,0},{4,7},{5,6},{6,5},{7,4},{8,11},{9,10},{10,... | collective-permute-start | bytes 393224 | tf_op jit(solution)/shard_map/ppermute | solution.py:273
  29.5 7.3 %slice-start.1 = ((s8[8388608]{0:T(1024)(128)(4,1)}), s8[4194304]{0:T(1024)(128)(4,1)S(1)}, s32[]{:S(2)}) async-start(s8[8388608]{0:T(1024)(128)(4,1)} %bitcast), calls=%async_computation.1 | async-start | bytes 8388608
  34.9 2.0 %collective-permute-start.13 = (bf16[512,512]{1,0:T(8,128)(2,1)S(1)}, bf16[512,512]{1,0:T(8,128)(2,1)S(1)}, u32[]{:S(2)}, u32[]{:S(2)}) collective-permute-start(bf16[512,512]{1,0:T(8,128)(2,1)S(1)} %shard_map.89.refs_2_), channel_id=1, source_target_pairs={{0,4},{4,0},{8,12},{12,8},{16,20},{20,16},{24,28},{28,24},{1,5},{5... | collective-permute-start | bytes 1572872 | tf_op jit(solution)/shard_map/ppermute | solution.py:273
  39.2 26.4 %collective-permute-start.16 = (bf16[64,4096]{1,0:T(8,128)(2,1)S(1)}, bf16[64,4096]{1,0:T(8,128)(2,1)S(1)}, u32[]{:S(2)}, u32[]{:S(2)}) collective-permute-start(bf16[64,4096]{1,0:T(8,128)(2,1)S(1)} %shard_map.91.refs_6_.refs_7_), channel_id=1, source_target_pairs={{0,1},{1,3},{2,0},{3,2},{4,5},{5,7},{6,4},{7,6},{8,9},{9,11},{10,8... | collective-permute-start | bytes 1572872 | tf_op jit(solution)/shard_map/ppermute | solution.py:320
  45.8 30.9 %collective-permute-start.15 = (bf16[64,4096]{1,0:T(8,128)(2,1)S(1)}, bf16[64,4096]{1,0:T(8,128)(2,1)S(1)}, u32[]{:S(2)}, u32[]{:S(2)}) collective-permute-start(bf16[64,4096]{1,0:T(8,128)(2,1)S(1)} %shard_map.93.refs_6_.refs_7_.refs_0_), channel_id=1, source_target_pairs={{0,3},{3,0},{4,7},{7,4},{8,11},{11,8},{12,15},{15,12},{16,19},{19,... | collective-permute-start | bytes 1572872 | tf_op jit(solution)/shard_map/ppermute | solution.py:320
  55.8 20.8 %collective-permute-start.14 = (bf16[64,4096]{1,0:T(8,128)(2,1)S(1)}, bf16[64,4096]{1,0:T(8,128)(2,1)S(1)}, u32[]{:S(2)}, u32[]{:S(2)}) collective-permute-start(bf16[64,4096]{1,0:T(8,128)(2,1)S(1)} %shard_map.95.refs_6_.refs_7_), channel_id=1, source_target_pairs={{0,1},{1,0},{2,3},{3,2},{4,5},{5,4},{6,7},{7,6},{8,9},{9,8},{10,11... | collective-permute-start | bytes 1572872 | tf_op jit(solution)/shard_map/ppermute | solution.py:320
  65.8 10.9 %collective-permute-start.17 = (bf16[64,4096]{1,0:T(8,128)(2,1)S(1)}, bf16[64,4096]{1,0:T(8,128)(2,1)S(1)}, u32[]{:S(2)}, u32[]{:S(2)}) collective-permute-start(bf16[64,4096]{1,0:T(8,128)(2,1)S(1)} %shard_map.98), channel_id=1, source_target_pairs={{1,2},{2,1},{5,6},{6,5},{9,10},{10,9},{13,14},{14,13},{17,18},{18,... | collective-permute-start | bytes 1572872 | tf_op jit(solution)/shard_map/ppermute | solution.py:320
